TPU v7x, 128 devices: a whole 4x4x4 slice. The times are simulated.
128 devices in a mesh: ctx: 16 (over z, x), head: 4 (over y_lo, core), dp: 2 (over y_hi).
Axes of the slice: x: 4, y: 4 (y_hi: 2, y_lo: 2; y = y_hi * 2 + y_lo), z: 4, core: 2. Of those that a mesh axis runs over, the one named last changes fastest.
Arguments:
- queries: bfloat16 [2, 4096, 1536], P('dp', 'ctx', 'head'), may hold values from -12 to 12
- keys: bfloat16 [2, 4096, 1536], P('dp', 'ctx', 'head'), may hold values from -6 to 6
- values: bfloat16 [2, 4096, 1536], P('dp', 'ctx', 'head'), may hold values from -6 to 6
- grad_out: bfloat16 [2, 4096, 1536], P('dp', 'ctx', 'head'), may hold values from -6 to 6
- kv_list: int32 [64, 32], P('ctx'), may hold values from 0 to 63, as said below
- cover_lists: int32 [64, 2], P('ctx'), may hold values from 0 to 15, all different within a row
- cond_tokens: bfloat16 [2, 1024, 3072], P('dp', 'ctx'), may hold values from -6 to 6
- cond_weight: bfloat16 [3072, 1536], P(None, 'head'), may hold values from -0.109375 to 0.109375
Outputs:
- grad_query: bfloat16 [2, 4096, 1536], P('dp', 'ctx', 'head')
- grad_key: bfloat16 [2, 4096, 1536], P('dp', 'ctx', 'head')
- grad_value: bfloat16 [2, 4096, 1536], P('dp', 'ctx', 'head')
- grad_cond_weight: float32 [3072, 1536], P(('ctx', 'dp'), 'head')
Inputs may be any that keep to these rules, and one draw needn't show every extreme that they name: `kv_list`: entries j * 2 to j * 2 + 1 of a row are 2 different blocks among blocks j * 4 to j * 4 + 3. `cover_lists`: the 2 entries of a row are different.
All inputs are finite; a program needn't handle non-finite values.
Results may differ from a plain program's by a relative error of at most 0.025.
Values may be sent and summed in bfloat16 or wider, within the bound.
No kernel may reach another device: no remote copies, remote signals or barrier semaphores. Data moves between devices by JAX's collectives and lax.ppermute only.
A program may use at most 128 MiB of HBM per device.

v0:
```python
import math

import jax
import jax.numpy as jnp
from jax import lax
from jax.sharding import PartitionSpec as P

HD = 128
BLK = 64
PER = 2


def shifted(shard, axis, by):
    count = lax.axis_size(axis)
    return lax.ppermute(shard, axis, [(i, (i + by) % count) for i in range(count)])


def local_choice(kv_list, source, blocks_here):
    chosen = lax.dynamic_slice_in_dim(kv_list, source * PER, PER, 1)
    return chosen - source * blocks_here


def picked_blocks(kv_shard, chosen, heads_here):
    stacked_width = kv_shard.shape[-1]
    blocks = kv_shard.reshape(kv_shard.shape[0] // BLK, BLK, stacked_width)
    picked = jnp.take(blocks, chosen.reshape(-1), axis=0)
    picked = picked.reshape(chosen.shape[0], chosen.shape[1] * BLK, 2, heads_here, HD)
    return (picked[:, :, 0], picked[:, :, 1])


def score_pair(query_eff, grad_here, key_pick, value_pick, score_scale):
    scores = (
        jnp.einsum("qbhd,qkhd->qhbk", query_eff, key_pick, preferred_element_type=jnp.float32)
        * score_scale
    )
    grad_prob = jnp.einsum(
        "qbhd,qkhd->qhbk", grad_here, value_pick, preferred_element_type=jnp.float32
    )
    return (scores, grad_prob)


def softmax_update(soft_stats, scores, grad_prob):
    row_top, row_total, weighted = soft_stats
    new_top = jnp.maximum(row_top, jnp.max(scores, axis=-1))
    factor = jnp.exp(row_top - new_top)
    probs_part = jnp.exp(scores - new_top[..., None])
    row_total = row_total * factor + jnp.sum(probs_part, axis=-1)
    weighted = weighted * factor + jnp.sum(probs_part * grad_prob, axis=-1)
    return (new_top, row_total, weighted)


def finish_stats(soft_stats):
    row_top, row_total, weighted = soft_stats
    return (row_top + jnp.log(row_total), weighted / row_total)


def shard_grads(
    query_eff,
    grad_here,
    key_pick,
    value_pick,
    chosen,
    blocks_here,
    log_total,
    row_delta,
    score_scale,
):
    scores, grad_prob = score_pair(query_eff, grad_here, key_pick, value_pick, score_scale)
    probs_full = jnp.exp(scores - log_total[..., None])
    value_part = jnp.einsum(
        "qhbk,qbhd->qkhd",
        probs_full.astype(jnp.bfloat16),
        grad_here,
        preferred_element_type=jnp.float32,
    )
    grad_score = (probs_full * (grad_prob - row_delta[..., None]) * score_scale).astype(
        jnp.bfloat16
    )
    query_part = jnp.einsum(
        "qhbk,qkhd->qbhd", grad_score, key_pick, preferred_element_type=jnp.float32
    )
    key_part = jnp.einsum(
        "qhbk,qbhd->qkhd", grad_score, query_eff, preferred_element_type=jnp.float32
    )
    stacked = jnp.stack([key_part, value_part], axis=2)
    pair_count = chosen.shape[0] * chosen.shape[1]
    stacked = stacked.reshape(pair_count, -1)
    onehot = (
        chosen.reshape(-1)[:, None] == jnp.arange(blocks_here, dtype=jnp.int32)[None, :]
    ).astype(jnp.float32)
    shard_term = jnp.einsum("pk,pf->kf", onehot, stacked, precision=lax.Precision.HIGHEST)
    return (query_part, shard_term.reshape(blocks_here * BLK, -1))


def body(queries, keys, values, grad_out, kv_list, cover_lists, cond_tokens, cond_weight):
    shards = lax.axis_size("ctx")
    position = lax.axis_index("ctx")
    row_count = queries.shape[1]
    feature_width = queries.shape[2]
    heads_here = feature_width // HD
    blocks_here = row_count // BLK
    score_scale = 1.0 / math.sqrt(HD)
    cond_proj = jnp.dot(cond_tokens[0], cond_weight, preferred_element_type=jnp.float32).astype(
        jnp.bfloat16
    )
    cond_all = lax.all_gather(cond_proj, "ctx", axis=0, tiled=True).reshape(
        shards, BLK, feature_width
    )
    owners = jnp.sum(
        (cover_lists[:, :, None] == jnp.arange(shards, dtype=jnp.int32)[None, None, :]).astype(
            jnp.float32
        ),
        axis=1,
    )
    lifted = jnp.einsum(
        "bo,orf->brf", owners.astype(jnp.bfloat16), cond_all, preferred_element_type=jnp.float32
    )
    query_eff = (
        queries[0].reshape(blocks_here, BLK, feature_width).astype(jnp.float32) + lifted
    ).astype(jnp.bfloat16)
    query_eff = query_eff.reshape(blocks_here, BLK, heads_here, HD)
    grad_here = grad_out[0].reshape(blocks_here, BLK, heads_here, HD)
    kv_home = jnp.concatenate([keys[0], values[0]], axis=1)
    stat_shape = (blocks_here, heads_here, BLK)
    start_stats = (
        jnp.full(stat_shape, -jnp.inf, jnp.float32),
        jnp.zeros(stat_shape, jnp.float32),
        jnp.zeros(stat_shape, jnp.float32),
    )
    query_start = jnp.zeros((blocks_here, BLK, heads_here, HD), jnp.float32)

    def forward_shard(soft_stats, kv_shard, source):
        chosen = local_choice(kv_list, source, blocks_here)
        key_pick, value_pick = picked_blocks(kv_shard, chosen, heads_here)
        scores, grad_prob = score_pair(query_eff, grad_here, key_pick, value_pick, score_scale)
        return softmax_update(soft_stats, scores, grad_prob)

    def backward_shard(kv_shard, source, log_total, row_delta):
        chosen = local_choice(kv_list, source, blocks_here)
        key_pick, value_pick = picked_blocks(kv_shard, chosen, heads_here)
        return shard_grads(
            query_eff,
            grad_here,
            key_pick,
            value_pick,
            chosen,
            blocks_here,
            log_total,
            row_delta,
            score_scale,
        )

    def advance(kv_shard):
        return shifted(kv_shard, "ctx", 1)

    def forward_step(cycle_step, loop_state):
        kv_shard, soft_stats = loop_state
        source = (position - cycle_step) % shards
        return (advance(kv_shard), forward_shard(soft_stats, kv_shard, source))

    kv_back, soft_stats = lax.fori_loop(0, shards, forward_step, (kv_home, start_stats))
    log_total, row_delta = finish_stats(soft_stats)

    def backward_step(cycle_step, loop_state):
        kv_shard, grad_acc, query_acc = loop_state
        source = (position - cycle_step) % shards
        query_part, shard_term = backward_shard(kv_shard, source, log_total, row_delta)
        grad_acc = shifted(grad_acc + shard_term, "ctx", 1)
        return (advance(kv_shard), grad_acc, query_acc + query_part)

    grad_start = jnp.zeros((row_count, 2 * feature_width), jnp.float32)
    kv_end, key_value_grad, query_total = lax.fori_loop(
        0, shards, backward_step, (kv_back, grad_start, query_start)
    )
    query_flat = query_total.reshape(blocks_here, BLK * feature_width)
    term_rows = jnp.einsum("bo,bf->of", owners, query_flat, precision=lax.Precision.HIGHEST)
    cond_grad = lax.psum_scatter(
        term_rows.reshape(BLK * lax.axis_size("ctx"), feature_width).astype(jnp.bfloat16),
        "ctx",
        scatter_dimension=0,
        tiled=True,
    )
    tokens_here = cond_tokens[0]
    grad_cond_weight = lax.psum_scatter(
        jnp.einsum("rc,rf->cf", tokens_here, cond_grad, preferred_element_type=jnp.float32).astype(
            jnp.bfloat16
        ),
        ("ctx", "dp"),
        scatter_dimension=0,
        tiled=True,
    ).astype(jnp.float32)
    grad_query = query_total.reshape(row_count, feature_width).astype(jnp.bfloat16)[None]
    grad_key = key_value_grad[:, :feature_width].astype(jnp.bfloat16)[None]
    grad_value = key_value_grad[:, feature_width:].astype(jnp.bfloat16)[None]
    return (grad_query, grad_key, grad_value, grad_cond_weight)


def solution(mesh):
    return jax.shard_map(
        body,
        mesh=mesh,
        in_specs=(
            P("dp", "ctx", "head"),
            P("dp", "ctx", "head"),
            P("dp", "ctx", "head"),
            P("dp", "ctx", "head"),
            P("ctx", None),
            P("ctx", None),
            P("dp", "ctx", None),
            P(None, "head"),
        ),
        out_specs=(
            P("dp", "ctx", "head"),
            P("dp", "ctx", "head"),
            P("dp", "ctx", "head"),
            P(("ctx", "dp"), "head"),
        ),
        check_vma=False,
    )
```

profile of v0, /device:TPU:0, one launch (start us, length us, event | category | flops | bytes accessed | tf_op | source)
XLA Modules:
  0.0 1312.9 jit_solution(2677597069660716534)
XLA Ops:
  11.4 25.9 %all_gather.3 = bf16[1024,384]{1,0:T(8,128)(2,1)S(1)} all-gather(bf16[64,384]{1,0:T(8,128)(2,1)S(1)} %convolution_convert_fusion.2), channel_id=1, replica_groups=mesh['ctx'=16,'head'=4,'dp'=2] {'ctx'}, dimensions={0}, use_global_device_ids=true | all-gather | bytes 835584 | tf_op jit(solution)/shard_map/all_gather | solution.py:106
  39.4 228.9 %while.42 = (s32[]{:T(128)}, bf16[256,768]{1,0:T(8,128)(2,1)}, f32[4,3,64]{2,1,0:T(4,128)S(1)}, f32[4,3,64]{2,1,0:T(4,128)S(1)}, f32[4,3,64]{2,1,0:T(4,128)S(1)}...) while((s32[]{:T(128)}, bf16[256,768]{1,0:T(8,128)(2,1)}, ...), condition=%wide.region_5.7_spmd.clone, body=%wide.region_1.6_spmd.clone.sunk | while | flops 51419492 | bytes 11856591 | solution.py:161
  45.1 2.5 reshape.170
  76.5 3.2 collective-permute-done
  90.5 4.3 collective-permute-done
  105.5 5.4 collective-permute-done
  121.6 6.6 collective-permute-done
  138.9 5.8 collective-permute-done
  155.5 5.0 collective-permute-done
  171.2 4.1 collective-permute-done
  186.0 3.1 collective-permute-done
  269.8 728.3 %while.43 = (s32[]{:T(128)}, bf16[256,768]{1,0:T(8,128)(2,1)}, f32[256,768]{1,0:T(8,128)}, f32[4,64,3,128]{3,1,2,0:T(8,128)}, s32[]{:T(128)}, /*index=5*/s32[4,3...) while((s32[]{:T(128)}, bf16[256,768]{1,0:T(8,128)(2,1)}, ...), condition=%wide.region_7.9_spmd.clone, body=%wide.region_6.8_spmd.clone.sunk | while | flops 146572416 | bytes 43081012 | solution.py:172
  274.0 2.5 reshape.173
  282.1 3.6 reshape.174
  292.9 18.8 %collective-permute-done.1 = bf16[256,768]{1,0:T(8,128)(2,1)} collective-permute-done((bf16[256,768]{1,0:T(8,128)(2,1)S(1)}, bf16[256,768]{1,0:T(8,128)(2,1)}, u32[]{:S(2)}, u32[]{:S(2)}) %collective-permute-start.1) | collective-permute-done | bytes 393248 | tf_op jit(solution)/shard_map/while/body/eval_jaxpr/ppermute | solution.py:15
  315.9 2.5 reshape.173
  324.0 3.6 reshape.174
  335.9 17.8 %collective-permute-done.1 = bf16[256,768]{1,0:T(8,128)(2,1)} collective-permute-done((bf16[256,768]{1,0:T(8,128)(2,1)S(1)}, bf16[256,768]{1,0:T(8,128)(2,1)}, u32[]{:S(2)}, u32[]{:S(2)}) %collective-permute-start.1) | collective-permute-done | bytes 393248 | tf_op jit(solution)/shard_map/while/body/eval_jaxpr/ppermute | solution.py:15
  357.9 2.5 reshape.173
  366.0 3.6 reshape.174
  377.8 17.8 %collective-permute-done.1 = bf16[256,768]{1,0:T(8,128)(2,1)} collective-permute-done((bf16[256,768]{1,0:T(8,128)(2,1)S(1)}, bf16[256,768]{1,0:T(8,128)(2,1)}, u32[]{:S(2)}, u32[]{:S(2)}) %collective-permute-start.1) | collective-permute-done | bytes 393248 | tf_op jit(solution)/shard_map/while/body/eval_jaxpr/ppermute | solution.py:15
  399.8 2.5 reshape.173
  407.9 3.6 reshape.174
  419.7 17.8 %collective-permute-done.1 = bf16[256,768]{1,0:T(8,128)(2,1)} collective-permute-done((bf16[256,768]{1,0:T(8,128)(2,1)S(1)}, bf16[256,768]{1,0:T(8,128)(2,1)}, u32[]{:S(2)}, u32[]{:S(2)}) %collective-permute-start.1) | collective-permute-done | bytes 393248 | tf_op jit(solution)/shard_map/while/body/eval_jaxpr/ppermute | solution.py:15
  441.7 2.5 reshape.173
  449.8 3.6 reshape.174
  461.7 17.8 %collective-permute-done.1 = bf16[256,768]{1,0:T(8,128)(2,1)} collective-permute-done((bf16[256,768]{1,0:T(8,128)(2,1)S(1)}, bf16[256,768]{1,0:T(8,128)(2,1)}, u32[]{:S(2)}, u32[]{:S(2)}) %collective-permute-start.1) | collective-permute-done | bytes 393248 | tf_op jit(solution)/shard_map/while/body/eval_jaxpr/ppermute | solution.py:15
  483.6 2.5 reshape.173
  491.8 3.6 reshape.174
  503.6 18.7 %collective-permute-done.1 = bf16[256,768]{1,0:T(8,128)(2,1)} collective-permute-done((bf16[256,768]{1,0:T(8,128)(2,1)S(1)}, bf16[256,768]{1,0:T(8,128)(2,1)}, u32[]{:S(2)}, u32[]{:S(2)}) %collective-permute-start.1) | collective-permute-done | bytes 393248 | tf_op jit(solution)/shard_map/while/body/eval_jaxpr/ppermute | solution.py:15
  526.4 2.5 reshape.173
  534.6 3.6 reshape.174
  546.4 19.7 %collective-permute-done.1 = bf16[256,768]{1,0:T(8,128)(2,1)} collective-permute-done((bf16[256,768]{1,0:T(8,128)(2,1)S(1)}, bf16[256,768]{1,0:T(8,128)(2,1)}, u32[]{:S(2)}, u32[]{:S(2)}) %collective-permute-start.1) | collective-permute-done | bytes 393248 | tf_op jit(solution)/shard_map/while/body/eval_jaxpr/ppermute | solution.py:15
  570.3 2.5 reshape.173
  578.4 3.6 reshape.174
  590.2 20.8 %collective-permute-done.1 = bf16[256,768]{1,0:T(8,128)(2,1)} collective-permute-done((bf16[256,768]{1,0:T(8,128)(2,1)S(1)}, bf16[256,768]{1,0:T(8,128)(2,1)}, u32[]{:S(2)}, u32[]{:S(2)}) %collective-permute-start.1) | collective-permute-done | bytes 393248 | tf_op jit(solution)/shard_map/while/body/eval_jaxpr/ppermute | solution.py:15
  615.3 2.5 reshape.173
  623.4 3.6 reshape.174
  635.2 21.9 %collective-permute-done.1 = bf16[256,768]{1,0:T(8,128)(2,1)} collective-permute-done((bf16[256,768]{1,0:T(8,128)(2,1)S(1)}, bf16[256,768]{1,0:T(8,128)(2,1)}, u32[]{:S(2)}, u32[]{:S(2)}) %collective-permute-start.1) | collective-permute-done | bytes 393248 | tf_op jit(solution)/shard_map/while/body/eval_jaxpr/ppermute | solution.py:15
  661.3 2.5 reshape.173
  669.4 3.6 reshape.174
  681.3 23.0 %collective-permute-done.1 = bf16[256,768]{1,0:T(8,128)(2,1)} collective-permute-done((bf16[256,768]{1,0:T(8,128)(2,1)S(1)}, bf16[256,768]{1,0:T(8,128)(2,1)}, u32[]{:S(2)}, u32[]{:S(2)}) %collective-permute-start.1) | collective-permute-done | bytes 393248 | tf_op jit(solution)/shard_map/while/body/eval_jaxpr/ppermute | solution.py:15
  708.4 2.5 reshape.173
  716.6 3.6 reshape.174
  728.4 24.1 %collective-permute-done.1 = bf16[256,768]{1,0:T(8,128)(2,1)} collective-permute-done((bf16[256,768]{1,0:T(8,128)(2,1)S(1)}, bf16[256,768]{1,0:T(8,128)(2,1)}, u32[]{:S(2)}, u32[]{:S(2)}) %collective-permute-start.1) | collective-permute-done | bytes 393248 | tf_op jit(solution)/shard_map/while/body/eval_jaxpr/ppermute | solution.py:15
  756.7 2.5 reshape.173
  764.8 3.6 reshape.174
  776.6 25.2 %collective-permute-done.1 = bf16[256,768]{1,0:T(8,128)(2,1)} collective-permute-done((bf16[256,768]{1,0:T(8,128)(2,1)S(1)}, bf16[256,768]{1,0:T(8,128)(2,1)}, u32[]{:S(2)}, u32[]{:S(2)}) %collective-permute-start.1) | collective-permute-done | bytes 393248 | tf_op jit(solution)/shard_map/while/body/eval_jaxpr/ppermute | solution.py:15
  806.0 2.5 reshape.173
  814.1 3.6 reshape.174
  825.9 26.3 %collective-permute-done.1 = bf16[256,768]{1,0:T(8,128)(2,1)} collective-permute-done((bf16[256,768]{1,0:T(8,128)(2,1)S(1)}, bf16[256,768]{1,0:T(8,128)(2,1)}, u32[]{:S(2)}, u32[]{:S(2)}) %collective-permute-start.1) | collective-permute-done | bytes 393248 | tf_op jit(solution)/shard_map/while/body/eval_jaxpr/ppermute | solution.py:15
  856.3 2.5 reshape.173
  864.5 3.6 reshape.174
  876.3 27.3 %collective-permute-done.1 = bf16[256,768]{1,0:T(8,128)(2,1)} collective-permute-done((bf16[256,768]{1,0:T(8,128)(2,1)S(1)}, bf16[256,768]{1,0:T(8,128)(2,1)}, u32[]{:S(2)}, u32[]{:S(2)}) %collective-permute-start.1) | collective-permute-done | bytes 393248 | tf_op jit(solution)/shard_map/while/body/eval_jaxpr/ppermute | solution.py:15
  907.8 2.5 reshape.173
  916.0 3.6 reshape.174
  927.8 28.4 %collective-permute-done.1 = bf16[256,768]{1,0:T(8,128)(2,1)} collective-permute-done((bf16[256,768]{1,0:T(8,128)(2,1)S(1)}, bf16[256,768]{1,0:T(8,128)(2,1)}, u32[]{:S(2)}, u32[]{:S(2)}) %collective-permute-start.1) | collective-permute-done | bytes 393248 | tf_op jit(solution)/shard_map/while/body/eval_jaxpr/ppermute | solution.py:15
  960.4 2.5 reshape.173
  968.5 3.6 reshape.174
  980.3 17.8 %collective-permute-done.1 = bf16[256,768]{1,0:T(8,128)(2,1)} collective-permute-done((bf16[256,768]{1,0:T(8,128)(2,1)S(1)}, bf16[256,768]{1,0:T(8,128)(2,1)}, u32[]{:S(2)}, u32[]{:S(2)}) %collective-permute-start.1) | collective-permute-done | bytes 393248 | tf_op jit(solution)/shard_map/while/body/eval_jaxpr/ppermute | solution.py:15
  1003.2 69.3 %reduce-scatter.5.cloned.1.call-done = bf16[64,384]{1,0:T(8,128)(2,1)} async-done(((bf16[1024,384]{1,0:T(8,128)(2,1)}), bf16[64,384]{1,0:T(8,128)(2,1)}) %reduce-scatter.5.cloned.1.call-update) | async-done | bytes 49168 | tf_op jit(solution)/shard_map/reduce_scatter | solution.py:177
  1072.5 3.0 fusion.15
  1075.5 4.3 copy.79
  1083.8 220.5 %reduce-scatter.7.cloned.1.call-done = bf16[96,384]{1,0:T(8,128)(2,1)} async-done(((bf16[3072,384]{1,0:T(8,128)(2,1)}), bf16[96,384]{1,0:T(8,128)(2,1)}) %reduce-scatter.7.cloned.1.call-update) | async-done | bytes 73744
  (1059 shorter events, 490.5 us)
Async XLA Ops:
  7.2 1065.3 %reduce-scatter.5.cloned.1.call-start = ((), (), s32[]{:S(2)}) async-start(), calls=%async_computation.2 | async-start | bytes 835584 | tf_op jit(solution)/shard_map/reduce_scatter | solution.py:177
  8.2 30.0 %copy-start.18 = (f32[4,16]{1,0:T(4,128)}, f32[4,16]{1,0:T(4,128)S(1)}, u32[]{:S(2)}) copy-start(f32[4,16]{1,0:T(4,128)S(1)} %convert_reduce_fusion) | copy-start | bytes 772
  9.2 28.2 %copy-start.13 = (bf16[1,256,384]{2,1,0:T(8,128)(2,1)S(1)}, bf16[1,256,384]{2,1,0:T(8,128)(2,1)}, u32[]{:S(2)}) copy-start(bf16[1,256,384]{2,1,0:T(8,128)(2,1)} %param.16) | copy-start | bytes 589828
  9.2 28.1 %copy-start.14 = (bf16[1,256,384]{2,1,0:T(8,128)(2,1)S(1)}, bf16[1,256,384]{2,1,0:T(8,128)(2,1)}, u32[]{:S(2)}) copy-start(bf16[1,256,384]{2,1,0:T(8,128)(2,1)} %param.15) | copy-start | bytes 589828
  11.4 27.3 %copy-start.15 = (bf16[1,256,384]{2,1,0:T(8,128)(2,1)S(1)}, bf16[1,256,384]{2,1,0:T(8,128)(2,1)}, u32[]{:S(2)}) copy-start(bf16[1,256,384]{2,1,0:T(8,128)(2,1)} %param.14) | copy-start | bytes 589828
  11.4 28.0 %copy-start.12 = (s32[4,32]{1,0:T(4,128)S(1)}, s32[4,32]{1,0:T(4,128)}, u32[]{:S(2)}) copy-start(s32[4,32]{1,0:T(4,128)} %param.18) | copy-start | bytes 1540
  41.2 11.4 collective-permute-start
  54.4 11.4 collective-permute-start
  67.6 12.2 collective-permute-start
  81.5 13.2 %collective-permute-start = (bf16[256,768]{1,0:T(8,128)(2,1)}, bf16[256,768]{1,0:T(8,128)(2,1)}, u32[]{:S(2)}, u32[]{:S(2)}) collective-permute-start(bf16[256,768]{1,0:T(8,128)(2,1)} %copy.122), channel_id=1, source_target_pairs={{0,8},{8,16},{16,24},{24,32},{32,40},{40,48},{48,56},{56,64},{64,7... | collective-permute-start | bytes 1179656 | tf_op jit(solution)/shard_map/while/body/eval_jaxpr/ppermute | solution.py:15
  96.5 14.4 %collective-permute-start = (bf16[256,768]{1,0:T(8,128)(2,1)}, bf16[256,768]{1,0:T(8,128)(2,1)}, u32[]{:S(2)}, u32[]{:S(2)}) collective-permute-start(bf16[256,768]{1,0:T(8,128)(2,1)} %copy.122), channel_id=1, source_target_pairs={{0,8},{8,16},{16,24},{24,32},{32,40},{40,48},{48,56},{56,64},{64,7... | collective-permute-start | bytes 1179656 | tf_op jit(solution)/shard_map/while/body/eval_jaxpr/ppermute | solution.py:15
  112.7 15.5 %collective-permute-start = (bf16[256,768]{1,0:T(8,128)(2,1)}, bf16[256,768]{1,0:T(8,128)(2,1)}, u32[]{:S(2)}, u32[]{:S(2)}) collective-permute-start(bf16[256,768]{1,0:T(8,128)(2,1)} %copy.122), channel_id=1, source_target_pairs={{0,8},{8,16},{16,24},{24,32},{32,40},{40,48},{48,56},{56,64},{64,7... | collective-permute-start | bytes 1179656 | tf_op jit(solution)/shard_map/while/body/eval_jaxpr/ppermute | solution.py:15
  130.0 14.8 %collective-permute-start = (bf16[256,768]{1,0:T(8,128)(2,1)}, bf16[256,768]{1,0:T(8,128)(2,1)}, u32[]{:S(2)}, u32[]{:S(2)}) collective-permute-start(bf16[256,768]{1,0:T(8,128)(2,1)} %copy.122), channel_id=1, source_target_pairs={{0,8},{8,16},{16,24},{24,32},{32,40},{40,48},{48,56},{56,64},{64,7... | collective-permute-start | bytes 1179656 | tf_op jit(solution)/shard_map/while/body/eval_jaxpr/ppermute | solution.py:15
  146.5 13.9 %collective-permute-start = (bf16[256,768]{1,0:T(8,128)(2,1)}, bf16[256,768]{1,0:T(8,128)(2,1)}, u32[]{:S(2)}, u32[]{:S(2)}) collective-permute-start(bf16[256,768]{1,0:T(8,128)(2,1)} %copy.122), channel_id=1, source_target_pairs={{0,8},{8,16},{16,24},{24,32},{32,40},{40,48},{48,56},{56,64},{64,7... | collective-permute-start | bytes 1179656 | tf_op jit(solution)/shard_map/while/body/eval_jaxpr/ppermute | solution.py:15
  162.2 13.0 collective-permute-start
  177.0 12.1 collective-permute-start
  190.9 11.4 collective-permute-start
  204.1 11.4 collective-permute-start
  217.3 11.4 collective-permute-start
  230.5 11.4 collective-permute-start
  243.7 11.4 collective-permute-start
  256.8 11.4 collective-permute-start
  288.1 3.9 copy-start.2
  291.9 19.8 %collective-permute-start.2 = (f32[256,768]{1,0:T(8,128)}, f32[256,768]{1,0:T(8,128)}, u32[]{:S(2)}, u32[]{:S(2)}) collective-permute-start(f32[256,768]{1,0:T(8,128)} %add.190), channel_id=1, source_target_pairs={{0,8},{8,16},{16,24},{24,32},{32,40},{40,48},{48,56},{56,64},{64,7... | collective-permute-start | bytes 2359304 | tf_op jit(solution)/shard_map/while/body/eval_jaxpr/ppermute | solution.py:15
  291.9 19.8 %collective-permute-start.1 = (bf16[256,768]{1,0:T(8,128)(2,1)S(1)}, bf16[256,768]{1,0:T(8,128)(2,1)}, u32[]{:S(2)}, u32[]{:S(2)}) collective-permute-start(bf16[256,768]{1,0:T(8,128)(2,1)S(1)} %copy-done.2), channel_id=1, source_target_pairs={{0,8},{8,16},{16,24},{24,32},{32,40},{40,48},{48,56},{56,64},{64,7... | collective-permute-start | bytes 1179656 | tf_op jit(solution)/shard_map/while/body/eval_jaxpr/ppermute | solution.py:15
  330.0 3.9 copy-start.2
  333.8 19.8 %collective-permute-start.2 = (f32[256,768]{1,0:T(8,128)}, f32[256,768]{1,0:T(8,128)}, u32[]{:S(2)}, u32[]{:S(2)}) collective-permute-start(f32[256,768]{1,0:T(8,128)} %add.190), channel_id=1, source_target_pairs={{0,8},{8,16},{16,24},{24,32},{32,40},{40,48},{48,56},{56,64},{64,7... | collective-permute-start | bytes 2359304 | tf_op jit(solution)/shard_map/while/body/eval_jaxpr/ppermute | solution.py:15
  333.8 19.8 %collective-permute-start.1 = (bf16[256,768]{1,0:T(8,128)(2,1)S(1)}, bf16[256,768]{1,0:T(8,128)(2,1)}, u32[]{:S(2)}, u32[]{:S(2)}) collective-permute-start(bf16[256,768]{1,0:T(8,128)(2,1)S(1)} %copy-done.2), channel_id=1, source_target_pairs={{0,8},{8,16},{16,24},{24,32},{32,40},{40,48},{48,56},{56,64},{64,7... | collective-permute-start | bytes 1179656 | tf_op jit(solution)/shard_map/while/body/eval_jaxpr/ppermute | solution.py:15
  371.9 3.9 copy-start.2
  375.8 19.8 %collective-permute-start.2 = (f32[256,768]{1,0:T(8,128)}, f32[256,768]{1,0:T(8,128)}, u32[]{:S(2)}, u32[]{:S(2)}) collective-permute-start(f32[256,768]{1,0:T(8,128)} %add.190), channel_id=1, source_target_pairs={{0,8},{8,16},{16,24},{24,32},{32,40},{40,48},{48,56},{56,64},{64,7... | collective-permute-start | bytes 2359304 | tf_op jit(solution)/shard_map/while/body/eval_jaxpr/ppermute | solution.py:15
  375.8 19.8 %collective-permute-start.1 = (bf16[256,768]{1,0:T(8,128)(2,1)S(1)}, bf16[256,768]{1,0:T(8,128)(2,1)}, u32[]{:S(2)}, u32[]{:S(2)}) collective-permute-start(bf16[256,768]{1,0:T(8,128)(2,1)S(1)} %copy-done.2), channel_id=1, source_target_pairs={{0,8},{8,16},{16,24},{24,32},{32,40},{40,48},{48,56},{56,64},{64,7... | collective-permute-start | bytes 1179656 | tf_op jit(solution)/shard_map/while/body/eval_jaxpr/ppermute | solution.py:15
  413.8 3.9 copy-start.2
  417.7 19.8 %collective-permute-start.2 = (f32[256,768]{1,0:T(8,128)}, f32[256,768]{1,0:T(8,128)}, u32[]{:S(2)}, u32[]{:S(2)}) collective-permute-start(f32[256,768]{1,0:T(8,128)} %add.190), channel_id=1, source_target_pairs={{0,8},{8,16},{16,24},{24,32},{32,40},{40,48},{48,56},{56,64},{64,7... | collective-permute-start | bytes 2359304 | tf_op jit(solution)/shard_map/while/body/eval_jaxpr/ppermute | solution.py:15
  417.7 19.8 %collective-permute-start.1 = (bf16[256,768]{1,0:T(8,128)(2,1)S(1)}, bf16[256,768]{1,0:T(8,128)(2,1)}, u32[]{:S(2)}, u32[]{:S(2)}) collective-permute-start(bf16[256,768]{1,0:T(8,128)(2,1)S(1)} %copy-done.2), channel_id=1, source_target_pairs={{0,8},{8,16},{16,24},{24,32},{32,40},{40,48},{48,56},{56,64},{64,7... | collective-permute-start | bytes 1179656 | tf_op jit(solution)/shard_map/while/body/eval_jaxpr/ppermute | solution.py:15
  455.8 3.9 copy-start.2
  459.6 19.8 %collective-permute-start.2 = (f32[256,768]{1,0:T(8,128)}, f32[256,768]{1,0:T(8,128)}, u32[]{:S(2)}, u32[]{:S(2)}) collective-permute-start(f32[256,768]{1,0:T(8,128)} %add.190), channel_id=1, source_target_pairs={{0,8},{8,16},{16,24},{24,32},{32,40},{40,48},{48,56},{56,64},{64,7... | collective-permute-start | bytes 2359304 | tf_op jit(solution)/shard_map/while/body/eval_jaxpr/ppermute | solution.py:15
  459.6 19.8 %collective-permute-start.1 = (bf16[256,768]{1,0:T(8,128)(2,1)S(1)}, bf16[256,768]{1,0:T(8,128)(2,1)}, u32[]{:S(2)}, u32[]{:S(2)}) collective-permute-start(bf16[256,768]{1,0:T(8,128)(2,1)S(1)} %copy-done.2), channel_id=1, source_target_pairs={{0,8},{8,16},{16,24},{24,32},{32,40},{40,48},{48,56},{56,64},{64,7... | collective-permute-start | bytes 1179656 | tf_op jit(solution)/shard_map/while/body/eval_jaxpr/ppermute | solution.py:15
  497.7 3.9 copy-start.2
  501.6 20.7 %collective-permute-start.2 = (f32[256,768]{1,0:T(8,128)}, f32[256,768]{1,0:T(8,128)}, u32[]{:S(2)}, u32[]{:S(2)}) collective-permute-start(f32[256,768]{1,0:T(8,128)} %add.190), channel_id=1, source_target_pairs={{0,8},{8,16},{16,24},{24,32},{32,40},{40,48},{48,56},{56,64},{64,7... | collective-permute-start | bytes 2359304 | tf_op jit(solution)/shard_map/while/body/eval_jaxpr/ppermute | solution.py:15
  501.6 20.7 %collective-permute-start.1 = (bf16[256,768]{1,0:T(8,128)(2,1)S(1)}, bf16[256,768]{1,0:T(8,128)(2,1)}, u32[]{:S(2)}, u32[]{:S(2)}) collective-permute-start(bf16[256,768]{1,0:T(8,128)(2,1)S(1)} %copy-done.2), channel_id=1, source_target_pairs={{0,8},{8,16},{16,24},{24,32},{32,40},{40,48},{48,56},{56,64},{64,7... | collective-permute-start | bytes 1179656 | tf_op jit(solution)/shard_map/while/body/eval_jaxpr/ppermute | solution.py:15
  540.5 3.9 copy-start.2
  544.3 21.8 %collective-permute-start.2 = (f32[256,768]{1,0:T(8,128)}, f32[256,768]{1,0:T(8,128)}, u32[]{:S(2)}, u32[]{:S(2)}) collective-permute-start(f32[256,768]{1,0:T(8,128)} %add.190), channel_id=1, source_target_pairs={{0,8},{8,16},{16,24},{24,32},{32,40},{40,48},{48,56},{56,64},{64,7... | collective-permute-start | bytes 2359304 | tf_op jit(solution)/shard_map/while/body/eval_jaxpr/ppermute | solution.py:15
  544.3 21.8 %collective-permute-start.1 = (bf16[256,768]{1,0:T(8,128)(2,1)S(1)}, bf16[256,768]{1,0:T(8,128)(2,1)}, u32[]{:S(2)}, u32[]{:S(2)}) collective-permute-start(bf16[256,768]{1,0:T(8,128)(2,1)S(1)} %copy-done.2), channel_id=1, source_target_pairs={{0,8},{8,16},{16,24},{24,32},{32,40},{40,48},{48,56},{56,64},{64,7... | collective-permute-start | bytes 1179656 | tf_op jit(solution)/shard_map/while/body/eval_jaxpr/ppermute | solution.py:15
  588.2 22.9 %collective-permute-start.2 = (f32[256,768]{1,0:T(8,128)}, f32[256,768]{1,0:T(8,128)}, u32[]{:S(2)}, u32[]{:S(2)}) collective-permute-start(f32[256,768]{1,0:T(8,128)} %add.190), channel_id=1, source_target_pairs={{0,8},{8,16},{16,24},{24,32},{32,40},{40,48},{48,56},{56,64},{64,7... | collective-permute-start | bytes 2359304 | tf_op jit(solution)/shard_map/while/body/eval_jaxpr/ppermute | solution.py:15
  588.2 22.9 %collective-permute-start.1 = (bf16[256,768]{1,0:T(8,128)(2,1)S(1)}, bf16[256,768]{1,0:T(8,128)(2,1)}, u32[]{:S(2)}, u32[]{:S(2)}) collective-permute-start(bf16[256,768]{1,0:T(8,128)(2,1)S(1)} %copy-done.2), channel_id=1, source_target_pairs={{0,8},{8,16},{16,24},{24,32},{32,40},{40,48},{48,56},{56,64},{64,7... | collective-permute-start | bytes 1179656 | tf_op jit(solution)/shard_map/while/body/eval_jaxpr/ppermute | solution.py:15
  633.2 24.0 %collective-permute-start.2 = (f32[256,768]{1,0:T(8,128)}, f32[256,768]{1,0:T(8,128)}, u32[]{:S(2)}, u32[]{:S(2)}) collective-permute-start(f32[256,768]{1,0:T(8,128)} %add.190), channel_id=1, source_target_pairs={{0,8},{8,16},{16,24},{24,32},{32,40},{40,48},{48,56},{56,64},{64,7... | collective-permute-start | bytes 2359304 | tf_op jit(solution)/shard_map/while/body/eval_jaxpr/ppermute | solution.py:15
  633.2 23.9 %collective-permute-start.1 = (bf16[256,768]{1,0:T(8,128)(2,1)S(1)}, bf16[256,768]{1,0:T(8,128)(2,1)}, u32[]{:S(2)}, u32[]{:S(2)}) collective-permute-start(bf16[256,768]{1,0:T(8,128)(2,1)S(1)} %copy-done.2), channel_id=1, source_target_pairs={{0,8},{8,16},{16,24},{24,32},{32,40},{40,48},{48,56},{56,64},{64,7... | collective-permute-start | bytes 1179656 | tf_op jit(solution)/shard_map/while/body/eval_jaxpr/ppermute | solution.py:15
  675.4 3.9 copy-start.2
  679.2 25.0 %collective-permute-start.2 = (f32[256,768]{1,0:T(8,128)}, f32[256,768]{1,0:T(8,128)}, u32[]{:S(2)}, u32[]{:S(2)}) collective-permute-start(f32[256,768]{1,0:T(8,128)} %add.190), channel_id=1, source_target_pairs={{0,8},{8,16},{16,24},{24,32},{32,40},{40,48},{48,56},{56,64},{64,7... | collective-permute-start | bytes 2359304 | tf_op jit(solution)/shard_map/while/body/eval_jaxpr/ppermute | solution.py:15
  679.2 25.0 %collective-permute-start.1 = (bf16[256,768]{1,0:T(8,128)(2,1)S(1)}, bf16[256,768]{1,0:T(8,128)(2,1)}, u32[]{:S(2)}, u32[]{:S(2)}) collective-permute-start(bf16[256,768]{1,0:T(8,128)(2,1)S(1)} %copy-done.2), channel_id=1, source_target_pairs={{0,8},{8,16},{16,24},{24,32},{32,40},{40,48},{48,56},{56,64},{64,7... | collective-permute-start | bytes 1179656 | tf_op jit(solution)/shard_map/while/body/eval_jaxpr/ppermute | solution.py:15
  726.4 26.1 %collective-permute-start.2 = (f32[256,768]{1,0:T(8,128)}, f32[256,768]{1,0:T(8,128)}, u32[]{:S(2)}, u32[]{:S(2)}) collective-permute-start(f32[256,768]{1,0:T(8,128)} %add.190), channel_id=1, source_target_pairs={{0,8},{8,16},{16,24},{24,32},{32,40},{40,48},{48,56},{56,64},{64,7... | collective-permute-start | bytes 2359304 | tf_op jit(solution)/shard_map/while/body/eval_jaxpr/ppermute | solution.py:15
  726.4 26.1 %collective-permute-start.1 = (bf16[256,768]{1,0:T(8,128)(2,1)S(1)}, bf16[256,768]{1,0:T(8,128)(2,1)}, u32[]{:S(2)}, u32[]{:S(2)}) collective-permute-start(bf16[256,768]{1,0:T(8,128)(2,1)S(1)} %copy-done.2), channel_id=1, source_target_pairs={{0,8},{8,16},{16,24},{24,32},{32,40},{40,48},{48,56},{56,64},{64,7... | collective-permute-start | bytes 1179656 | tf_op jit(solution)/shard_map/while/body/eval_jaxpr/ppermute | solution.py:15
  774.6 27.2 %collective-permute-start.2 = (f32[256,768]{1,0:T(8,128)}, f32[256,768]{1,0:T(8,128)}, u32[]{:S(2)}, u32[]{:S(2)}) collective-permute-start(f32[256,768]{1,0:T(8,128)} %add.190), channel_id=1, source_target_pairs={{0,8},{8,16},{16,24},{24,32},{32,40},{40,48},{48,56},{56,64},{64,7... | collective-permute-start | bytes 2359304 | tf_op jit(solution)/shard_map/while/body/eval_jaxpr/ppermute | solution.py:15
  774.6 27.2 %collective-permute-start.1 = (bf16[256,768]{1,0:T(8,128)(2,1)S(1)}, bf16[256,768]{1,0:T(8,128)(2,1)}, u32[]{:S(2)}, u32[]{:S(2)}) collective-permute-start(bf16[256,768]{1,0:T(8,128)(2,1)S(1)} %copy-done.2), channel_id=1, source_target_pairs={{0,8},{8,16},{16,24},{24,32},{32,40},{40,48},{48,56},{56,64},{64,7... | collective-permute-start | bytes 1179656 | tf_op jit(solution)/shard_map/while/body/eval_jaxpr/ppermute | solution.py:15
  823.9 28.3 %collective-permute-start.2 = (f32[256,768]{1,0:T(8,128)}, f32[256,768]{1,0:T(8,128)}, u32[]{:S(2)}, u32[]{:S(2)}) collective-permute-start(f32[256,768]{1,0:T(8,128)} %add.190), channel_id=1, source_target_pairs={{0,8},{8,16},{16,24},{24,32},{32,40},{40,48},{48,56},{56,64},{64,7... | collective-permute-start | bytes 2359304 | tf_op jit(solution)/shard_map/while/body/eval_jaxpr/ppermute | solution.py:15
  823.9 28.3 %collective-permute-start.1 = (bf16[256,768]{1,0:T(8,128)(2,1)S(1)}, bf16[256,768]{1,0:T(8,128)(2,1)}, u32[]{:S(2)}, u32[]{:S(2)}) collective-permute-start(bf16[256,768]{1,0:T(8,128)(2,1)S(1)} %copy-done.2), channel_id=1, source_target_pairs={{0,8},{8,16},{16,24},{24,32},{32,40},{40,48},{48,56},{56,64},{64,7... | collective-permute-start | bytes 1179656 | tf_op jit(solution)/shard_map/while/body/eval_jaxpr/ppermute | solution.py:15
  874.3 29.4 %collective-permute-start.2 = (f32[256,768]{1,0:T(8,128)}, f32[256,768]{1,0:T(8,128)}, u32[]{:S(2)}, u32[]{:S(2)}) collective-permute-start(f32[256,768]{1,0:T(8,128)} %add.190), channel_id=1, source_target_pairs={{0,8},{8,16},{16,24},{24,32},{32,40},{40,48},{48,56},{56,64},{64,7... | collective-permute-start | bytes 2359304 | tf_op jit(solution)/shard_map/while/body/eval_jaxpr/ppermute | solution.py:15
  874.3 29.4 %collective-permute-start.1 = (bf16[256,768]{1,0:T(8,128)(2,1)S(1)}, bf16[256,768]{1,0:T(8,128)(2,1)}, u32[]{:S(2)}, u32[]{:S(2)}) collective-permute-start(bf16[256,768]{1,0:T(8,128)(2,1)S(1)} %copy-done.2), channel_id=1, source_target_pairs={{0,8},{8,16},{16,24},{24,32},{32,40},{40,48},{48,56},{56,64},{64,7... | collective-permute-start | bytes 1179656 | tf_op jit(solution)/shard_map/while/body/eval_jaxpr/ppermute | solution.py:15
  925.7 30.5 %collective-permute-start.2 = (f32[256,768]{1,0:T(8,128)}, f32[256,768]{1,0:T(8,128)}, u32[]{:S(2)}, u32[]{:S(2)}) collective-permute-start(f32[256,768]{1,0:T(8,128)} %add.190), channel_id=1, source_target_pairs={{0,8},{8,16},{16,24},{24,32},{32,40},{40,48},{48,56},{56,64},{64,7... | collective-permute-start | bytes 2359304 | tf_op jit(solution)/shard_map/while/body/eval_jaxpr/ppermute | solution.py:15
  925.7 30.5 %collective-permute-start.1 = (bf16[256,768]{1,0:T(8,128)(2,1)S(1)}, bf16[256,768]{1,0:T(8,128)(2,1)}, u32[]{:S(2)}, u32[]{:S(2)}) collective-permute-start(bf16[256,768]{1,0:T(8,128)(2,1)S(1)} %copy-done.2), channel_id=1, source_target_pairs={{0,8},{8,16},{16,24},{24,32},{32,40},{40,48},{48,56},{56,64},{64,7... | collective-permute-start | bytes 1179656 | tf_op jit(solution)/shard_map/while/body/eval_jaxpr/ppermute | solution.py:15
  978.3 19.8 %collective-permute-start.2 = (f32[256,768]{1,0:T(8,128)}, f32[256,768]{1,0:T(8,128)}, u32[]{:S(2)}, u32[]{:S(2)}) collective-permute-start(f32[256,768]{1,0:T(8,128)} %add.190), channel_id=1, source_target_pairs={{0,8},{8,16},{16,24},{24,32},{32,40},{40,48},{48,56},{56,64},{64,7... | collective-permute-start | bytes 2359304 | tf_op jit(solution)/shard_map/while/body/eval_jaxpr/ppermute | solution.py:15
  978.3 19.8 %collective-permute-start.1 = (bf16[256,768]{1,0:T(8,128)(2,1)S(1)}, bf16[256,768]{1,0:T(8,128)(2,1)}, u32[]{:S(2)}, u32[]{:S(2)}) collective-permute-start(bf16[256,768]{1,0:T(8,128)(2,1)S(1)} %copy-done.2), channel_id=1, source_target_pairs={{0,8},{8,16},{16,24},{24,32},{32,40},{40,48},{48,56},{56,64},{64,7... | collective-permute-start | bytes 1179656 | tf_op jit(solution)/shard_map/while/body/eval_jaxpr/ppermute | solution.py:15
  1001.9 70.6 %copy-start.11 = (bf16[1,64,3072]{2,1,0:T(8,128)(2,1)S(1)}, bf16[1,64,3072]{2,1,0:T(8,128)(2,1)}, u32[]{:S(2)}) copy-start(bf16[1,64,3072]{2,1,0:T(8,128)(2,1)} %param.20) | copy-start | bytes 1179652
  1003.1 301.2 %reduce-scatter.7.cloned.1.call-start = ((), (), s32[]{:S(2)}) async-start(), calls=%async_computation.3 | async-start | bytes 2433024
  (186 other events, 324.5 us)
Sparse Core Ops, SparseCore 0:
  1003.3 69.1 reduce-scatter.4
  1079.9 224.3 reduce-scatter.6
where the time goes:
time: 1320 us; the launch traced here: 1310 us
  waiting for transfers between devices  689 us (52%)
  local copies, waits for them, and re-layouts  344 us (26%)
  matrix products  130 us (10%)
  other arithmetic  105 us (8%)
  blocking collectives  25.9 us (2%)
  between operations  14.2 us (1%)
    ppermute x48, waiting for transfers between devices, shifted(): lax.ppermute(shard, axis, [(i, (i + by) % count) for i in range(count)])  399 us
    unnamed x3, waiting for transfers between devices  221 us
    reshape x32, local copies, waits for them, and re-layouts, picked_blocks(): picked.reshape(chosen.shape[0], chosen.shape[1] * BLK, 2, heads_here, HD)  80.8 us
    reduce_scatter x1, waiting for transfers between devices, body(): lax.psum_scatter(term_rows.reshape(BLK * lax.axis_size('ctx'), feature_wi...  69.3 us
    while x432, local copies, waits for them, and re-layouts  67.2 us
    reshape x16, local copies, waits for them, and re-layouts, shard_grads(): stacked = stacked.reshape(pair_count, -1)  57.5 us
    select_n x64, other arithmetic, picked_blocks(): picked = jnp.take(blocks, chosen.reshape(-1), axis=0)  43.4 us
    another operation x16, local copies, waits for them, and re-layouts, shard_grads(): stacked = jnp.stack([key_part, value_part], axis=2)  38.8 us
  transfers between devices with their start and end apart: 50, of which 34 were waited for; matrix products, arithmetic and copies ran while one was open for 13% of the time, Pallas kernels for 0%

commit v1 on v0

v1 whole, which is shorter than its diff:
```python
import math

import jax
import jax.numpy as jnp
import numpy as np
from jax import lax
from jax.experimental import pallas as pl
from jax.experimental.pallas import tpu as pltpu
from jax.sharding import PartitionSpec as P

HD = 128
BLK = 64
PER = 2
HEADS = 3
WIDTH = HEADS * HD
SIDE = 4
ROWS = 1024
SCALE = 1.0 / math.sqrt(HD)
LOG2E = 1.4426950408889634
SCALE2 = SCALE * LOG2E
OFFSETS = (0, -1, 1, 2)
SLOT_OF = {0: 0, 3: 1, 1: 2, 2: 3}
BF16 = jnp.bfloat16
F32 = jnp.float32
MIB = 1 << 20
CHUNK = 192
PADDED = 256


def roles(ctx, core):
    z, x = divmod(ctx, SIDE)
    return (x, z) if core == 0 else (z, x)


def ctx_of(u, v, core):
    return v * SIDE + u if core == 0 else u * SIDE + v


def info_table():
    table = np.zeros((2, SIDE * SIDE, 64), np.int32)
    for core in range(2):
        for ctx in range(SIDE * SIDE):
            u, v = roles(ctx, core)
            row = table[core, ctx]
            for slot, off in enumerate(OFFSETS):
                row[slot] = ctx_of(u, (v + off) % SIDE, core)
            for owner in range(SIDE * SIDE):
                uo, vo = roles(owner, core)
                place = SLOT_OF[(vo - v) % SIDE] * SIDE + SLOT_OF[(uo - u) % SIDE]
                row[4 + owner] = place
                row[20 + place] = owner
    return table


INFO = info_table()


def send(array, role, by):
    pairs = []
    for ctx in range(SIDE * SIDE):
        for head in range(4):
            core = head % 2
            u, v = roles(ctx, core)
            if role == "u":
                target = ctx_of((u + by) % SIDE, v, core)
            else:
                target = ctx_of(u, (v + by) % SIDE, core)
            pairs.append((ctx * 4 + head, target * 4 + head))
    return lax.ppermute(array, ("ctx", "head"), pairs)


def gathered(array, role):
    return [array] + [send(array, role, -off) for off in OFFSETS[1:]]


def scattered(parts, role):
    return [parts[0]] + [send(parts[slot], role, OFFSETS[slot]) for slot in range(1, SIDE)]


def summed(parts):
    total = parts[0].astype(F32)
    for part in parts[1:]:
        total = total + part.astype(F32)
    return total


def aligned(ref, off):
    parts = []
    for mine in OFFSETS:
        slot = SLOT_OF[(mine - off) % SIDE]
        parts.append(ref[:, slot * 256 : (slot + 1) * 256])
    return jnp.concatenate(parts, axis=1)


def nt(a, b):
    return lax.dot_general(a, b, (((1,), (1,)), ((), ())), preferred_element_type=F32)


def nn(a, b):
    return lax.dot_general(a, b, (((1,), (0,)), ((), ())), preferred_element_type=F32)


def tn(a, b):
    return lax.dot_general(a, b, (((0,), (0,)), ((), ())), preferred_element_type=F32)


def picks(info, lists, block):
    starts = []
    for slot in range(SIDE):
        shard = info[slot]
        for j in range(PER):
            local = lists[block, shard * PER + j] - shard * SIDE
            starts.append((slot, pl.multiple_of(local * BLK, BLK)))
    return starts


def taken(refs, starts, head):
    cols = slice(head * HD, (head + 1) * HD)
    return jnp.concatenate([refs[slot][pl.ds(at, BLK), cols] for slot, at in starts], axis=0)


def cover_places(info, lists, block):
    return [info[4 + lists[block, 32 + j]] for j in range(2)]


def score_kernel(info, lists, *refs):
    q, c, k = refs[0:4], refs[4:8], refs[8:12]
    qeff, stat, cbuf, cols = refs[12:]
    for slot in range(SIDE):
        cbuf[slot * 256 : (slot + 1) * 256, :] = c[slot][...]
        qeff[slot * 256 : (slot + 1) * 256, :] = q[slot][...]
    lane = lax.broadcasted_iota(jnp.int32, (BLK, HD), 1)

    def step(block, carry):
        rows = pl.ds(pl.multiple_of(block * BLK, BLK), BLK)
        places = cover_places(info, lists, block)
        lifted = [cbuf[pl.ds(pl.multiple_of(at * BLK, BLK), BLK), :].astype(F32) for at in places]
        query = (qeff[rows, :].astype(F32) + (lifted[0] + lifted[1])).astype(BF16)
        qeff[rows, :] = query
        starts = picks(info, lists, block)
        tile = jnp.zeros((BLK, HD), F32)
        for head in range(HEADS):
            scores = nt(query[:, head * HD : (head + 1) * HD], taken(k, starts, head))
            top = jnp.max(scores, axis=1, keepdims=True)
            total = jnp.sum(jnp.exp2((scores - top) * SCALE2), axis=1, keepdims=True)
            tile = jnp.where(lane == head, top, tile)
            tile = jnp.where(lane == HEADS + head, total, tile)
        cols[rows, :] = tile
        return carry

    lax.fori_loop(0, 16, step, 0)
    stat[...] = cols[...].T[0:8, :]


def value_kernel(info, lists, *refs):
    stats, qeff = refs[0:4], refs[4]
    k, grad, v = refs[5:9], refs[9:13], refs[13:17]
    dv, delta, lrow, grad_all = refs[17:21], refs[21], refs[22], refs[23]
    cols, dcols, wide, acc = refs[24:]
    stat = [stats[0][...]] + [aligned(stats[slot], OFFSETS[slot]) for slot in range(1, SIDE)]
    tops = [s[0:HEADS] for s in stat]
    top = jnp.maximum(jnp.maximum(tops[0], tops[1]), jnp.maximum(tops[2], tops[3]))
    total = jnp.zeros_like(top)
    for s, t in zip(stat, tops):
        total = total + s[HEADS : 2 * HEADS] * jnp.exp2((t - top) * SCALE2)
    log_total = top * SCALE2 + jnp.log(total) * LOG2E
    wide[...] = jnp.zeros_like(wide)
    wide[0:HEADS, :] = log_total
    lrow[...] = wide[0:8, :]
    cols[...] = wide[...].T
    acc[...] = jnp.zeros_like(acc)
    for slot in range(SIDE):
        grad_all[slot * 256 : (slot + 1) * 256, :] = grad[slot][...]
    lane = lax.broadcasted_iota(jnp.int32, (BLK, HD), 1)

    def step(block, carry):
        rows = pl.ds(pl.multiple_of(block * BLK, BLK), BLK)
        query, grad_here = qeff[rows, :], grad_all[rows, :]
        log_here = cols[rows, :]
        starts = picks(info, lists, block)
        tile = jnp.zeros((BLK, HD), F32)
        for head in range(HEADS):
            at = slice(head * HD, (head + 1) * HD)
            scores = nt(query[:, at], taken(k, starts, head))
            probs = jnp.exp2(scores * SCALE2 - log_here[:, head : head + 1])
            grad_prob = nt(grad_here[:, at], taken(v, starts, head))
            part = jnp.sum(probs * grad_prob, axis=1, keepdims=True)
            tile = jnp.where(lane == head, part, tile)
            value_part = tn(probs.astype(BF16), grad_here[:, at])
            for n, (slot, start) in enumerate(starts):
                acc[slot, pl.ds(start, BLK), at] += value_part[n * BLK : (n + 1) * BLK]
        dcols[rows, :] = tile
        return carry

    lax.fori_loop(0, 16, step, 0)
    delta[...] = dcols[...].T[0:8, :]
    for slot in range(SIDE):
        dv[slot][...] = acc[slot].astype(BF16)


def grad_kernel(info, lists, *refs):
    lrow, deltas, qeff, grad_all = refs[0], refs[1:5], refs[5], refs[6]
    k, v = refs[7:11], refs[11:15]
    dq, cg, dk = refs[15:19], refs[19:23], refs[23:27]
    cols, wide, qbuf, acc, cond = refs[27:]
    delta = deltas[0][...]
    for slot in range(1, SIDE):
        delta = delta + aligned(deltas[slot], OFFSETS[slot])
    wide[...] = jnp.zeros_like(wide)
    wide[0:8, :] = lrow[...]
    wide[8:16, :] = delta
    cols[...] = wide[...].T
    acc[...] = jnp.zeros_like(acc)
    cond[...] = jnp.zeros_like(cond)

    def step(block, carry):
        rows = pl.ds(pl.multiple_of(block * BLK, BLK), BLK)
        query, grad_here = qeff[rows, :], grad_all[rows, :]
        col = cols[rows, :]
        starts = picks(info, lists, block)
        parts = []
        for head in range(HEADS):
            at = slice(head * HD, (head + 1) * HD)
            keys = taken(k, starts, head)
            scores = nt(query[:, at], keys)
            probs = jnp.exp2(scores * SCALE2 - col[:, head : head + 1])
            grad_prob = nt(grad_here[:, at], taken(v, starts, head))
            grad_score = (probs * (grad_prob - col[:, 8 + head : 9 + head]) * SCALE).astype(BF16)
            parts.append(nn(grad_score, keys))
            key_part = tn(grad_score, query[:, at])
            for n, (slot, start) in enumerate(starts):
                acc[slot, pl.ds(start, BLK), at] += key_part[n * BLK : (n + 1) * BLK]
        query_part = jnp.concatenate(parts, axis=1)
        qbuf[rows, :] = query_part.astype(BF16)
        for place in cover_places(info, lists, block):
            turned = (place & 3) * 4 + (place >> 2)
            cond[pl.ds(pl.multiple_of(turned * BLK, BLK), BLK), :] += query_part
        return carry

    lax.fori_loop(0, 16, step, 0)
    for slot in range(SIDE):
        dq[slot][...] = qbuf[slot * 256 : (slot + 1) * 256, :]
        cg[slot][...] = cond[slot * 256 : (slot + 1) * 256, :].astype(BF16)
        dk[slot][...] = acc[slot].astype(BF16)


def token_kernel(info, tokens, *refs):
    out, padded = refs[0:4], refs[4]
    padded[...] = jnp.zeros_like(padded)
    for n in range(16):
        padded[:, n * PADDED : n * PADDED + CHUNK] = tokens[:, n * CHUNK : (n + 1) * CHUNK]
    for sv in range(SIDE):
        for su in range(SIDE):
            start = pl.multiple_of(info[20 + sv * SIDE + su] * PADDED, PADDED)
            out[sv][:, su * PADDED : (su + 1) * PADDED] = padded[:, pl.ds(start, PADDED)]


def weight_kernel(*refs):
    cond, tokens, out = refs[0:4], refs[4:8], refs[8:12]
    total = cond[0][...].astype(F32)
    for slot in range(1, SIDE):
        parts = []
        for mine in OFFSETS:
            at = SLOT_OF[(mine - OFFSETS[slot]) % SIDE]
            parts.append(cond[slot][at * BLK : (at + 1) * BLK, :])
        total = total + jnp.concatenate(parts, axis=0).astype(F32)
    half = total.astype(BF16)
    stacked = jnp.concatenate([t[...] for t in tokens], axis=0)
    for su in range(SIDE):
        part = tn(stacked[:, su * PADDED : (su + 1) * PADDED], half)
        out[su][...] = part[0:CHUNK, :].astype(BF16)


VMEM = pl.BlockSpec(memory_space=pltpu.VMEM)
SMEM = pl.BlockSpec(memory_space=pltpu.SMEM)


def call(kernel, name, scalars, arrays, outs, scratch, limit, flops=0, moved=0, exps=0):
    return pl.pallas_call(
        kernel,
        name=name,
        out_shape=[jax.ShapeDtypeStruct(shape, dtype) for shape, dtype in outs],
        in_specs=[SMEM] * len(scalars) + [VMEM] * len(arrays),
        out_specs=[VMEM] * len(outs),
        scratch_shapes=[pltpu.VMEM(shape, dtype) for shape, dtype in scratch],
        compiler_params=pltpu.CompilerParams(vmem_limit_bytes=limit * MIB),
        cost_estimate=pl.CostEstimate(flops=flops, bytes_accessed=moved, transcendentals=exps),
    )(*scalars, *arrays)


PRODUCT = 2 * 201326592
EXPS = 1572864


def body(queries, keys, values, grad_out, kv_list, cover_lists, cond_tokens, cond_weight):
    ctx = lax.axis_index("ctx")
    core = lax.axis_index("head") % 2
    info = lax.dynamic_slice(jnp.asarray(INFO), (core, ctx, 0), (1, 1, 64)).reshape(64)
    shard = ((256, WIDTH), BF16)
    q = gathered(queries[0], "u")
    k = gathered(keys[0], "v")
    cond_proj = jnp.dot(cond_tokens[0], cond_weight, preferred_element_type=F32).astype(BF16)
    lists_here = jnp.concatenate([kv_list, cover_lists], axis=1).astype(BF16)
    lists_here = jnp.pad(lists_here, ((0, 12), (0, WIDTH - 34)))
    row = gathered(jnp.concatenate([cond_proj, lists_here], axis=0), "u")
    lists = jnp.concatenate([part[BLK : BLK + 4, :HD] for part in row]).astype(jnp.int32)
    cond_all = gathered(jnp.concatenate([part[:BLK] for part in row]), "v")
    grad = gathered(grad_out[0], "u")
    v = gathered(values[0], "v")
    qeff, stat = call(
        score_kernel,
        "scores",
        [info, lists],
        q + cond_all + k,
        [((ROWS, WIDTH), BF16), ((8, ROWS), F32)],
        [((ROWS, WIDTH), BF16), ((ROWS, HD), F32)],
        16,
        PRODUCT,
        4 * MIB,
        EXPS,
    )
    stats = gathered(stat, "u")
    out = call(
        value_kernel,
        "values",
        [info, lists],
        stats + [qeff] + k + grad + v,
        [shard] * 4 + [((8, ROWS), F32)] * 2 + [((ROWS, WIDTH), BF16)],
        [((ROWS, HD), F32)] * 2 + [((HD, ROWS), F32), ((SIDE, 256, WIDTH), F32)],
        24,
        3 * PRODUCT,
        6 * MIB,
        EXPS,
    )
    dv, delta, lrow, grad_all = out[0:4], out[4], out[5], out[6]
    deltas = gathered(delta, "u")
    dv = scattered(dv, "v")
    tokens = call(
        token_kernel,
        "tokens",
        [info],
        [cond_tokens[0]],
        [((BLK, 4 * PADDED), BF16)] * 4,
        [((BLK, 16 * PADDED), BF16)],
        8,
        0,
        MIB,
    )
    tokens = scattered(tokens, "v")
    tokens = [tokens[0], tokens[2], tokens[1], tokens[3]]
    out = call(
        grad_kernel,
        "grads",
        [info, lists],
        [lrow] + deltas + [qeff, grad_all] + k + v,
        [shard] * 12,
        [
            ((ROWS, HD), F32),
            ((HD, ROWS), F32),
            ((ROWS, WIDTH), BF16),
            ((SIDE, 256, WIDTH), F32),
            ((ROWS, WIDTH), F32),
        ],
        24,
        4 * PRODUCT,
        7 * MIB,
        EXPS,
    )
    cond_part = summed(scattered(out[4:8], "u")).astype(BF16)
    dq = scattered(out[0:4], "u")
    dk = scattered(out[8:12], "v")
    cond_parts = gathered(cond_part, "v")
    weight = call(
        weight_kernel,
        "weights",
        [],
        cond_parts + tokens,
        [((CHUNK, WIDTH), BF16)] * 4,
        [],
        8,
        2 * 100663296,
        MIB,
    )
    weight = summed(scattered(weight, "u"))
    dp = lax.axis_index("dp")
    mine = lax.dynamic_slice_in_dim(weight, dp * 96, 96, 0)
    other = lax.dynamic_slice_in_dim(weight, (1 - dp) * 96, 96, 0).astype(BF16)
    grad_cond_weight = mine + lax.ppermute(other, "dp", [(0, 1), (1, 0)]).astype(F32)
    grad_query = summed(dq).astype(BF16)[None]
    grad_key = summed(dk).astype(BF16)[None]
    grad_value = summed(dv).astype(BF16)[None]
    return (grad_query, grad_key, grad_value, grad_cond_weight)


def solution(mesh):
    return jax.shard_map(
        body,
        mesh=mesh,
        in_specs=(
            P("dp", "ctx", "head"),
            P("dp", "ctx", "head"),
            P("dp", "ctx", "head"),
            P("dp", "ctx", "head"),
            P("ctx", None),
            P("ctx", None),
            P("dp", "ctx", None),
            P(None, "head"),
        ),
        out_specs=(
            P("dp", "ctx", "head"),
            P("dp", "ctx", "head"),
            P("dp", "ctx", "head"),
            P(("ctx", "dp"), "head"),
        ),
        check_vma=False,
    )
```

time: 1320 us -> 176 us (0.13)
  waiting for transfers between devices: 689 us -> 43.7 us
  local copies, waits for them, and re-layouts: 344 us -> 13.4 us
  matrix products: 130 us -> 1.44 us
  other arithmetic: 105 us -> 5.94 us
  starting transfers between devices: 1.52 us -> 65.5 us
  Pallas kernels: 0 us -> 44.5 us
  blocking collectives: 25.9 us -> 0 us
  between operations: 14.2 us -> 0.97 us
    ppermute x48 -> x46, waiting for transfers between devices: 399 us -> 43.7 us  [the longest x45 41.8 us: send(): return lax.ppermute(array, ('ctx', 'head'), pairs)]
    unnamed x3 -> x0, waiting for transfers between devices: 221 us -> none
    reshape x81 -> x1, local copies, waits for them, and re-layouts: 163 us -> 0.69 us  [body(): lax.dynamic_slice(jnp.asarray(INFO), (core, ctx, 0), (1, 1, 64)).reshape(64)]
    dot_general x132 -> x1, matrix products: 130 us -> 1.44 us  [body(): jnp.dot(cond_tokens[0], cond_weight, preferred_element_type=F32)]
    reduce_scatter x1 -> x0, waiting for transfers between devices: 69.3 us -> none  [body(): lax.psum_scatter(term_rows.reshape(BLK * lax.axis_size('ctx'), feature_wi...]
    while x433 -> x0, local copies, waits for them, and re-layouts: 68.4 us -> none
    ppermute x48 -> x46, starting transfers between devices: 1.44 us -> 65.5 us  [the longest x45 62.2 us: send(): return lax.ppermute(array, ('ctx', 'head'), pairs)]
    pallas_call x0 -> x5, Pallas kernels: none -> 44.5 us  [call(): pl.pallas_call(kernel, name=name, out_shape=[jax.ShapeDtypeStruct(shape,...]
  transfers between devices with their start and end apart: 50 -> 46, of which waited for: 34 -> 14; matrix products, arithmetic and copies ran while one was open for 13% -> 4% of each run, Pallas kernels for 0% -> 7%
where the time goes in v1:
time: 176 us; the launch traced here: 175 us
  starting transfers between devices  65.5 us (37%)
  Pallas kernels  44.5 us (25%)
  waiting for transfers between devices  43.7 us (25%)
  local copies, waits for them, and re-layouts  13.4 us (8%)
  other arithmetic  5.94 us (3%)
    ppermute x45, starting transfers between devices, send(): return lax.ppermute(array, ('ctx', 'head'), pairs)  62.2 us
    pallas_call x5, Pallas kernels, call(): pl.pallas_call(kernel, name=name, out_shape=[jax.ShapeDtypeStruct(shape,...  44.5 us
    ppermute x45, waiting for transfers between devices, send(): return lax.ppermute(array, ('ctx', 'head'), pairs)  41.8 us
    unnamed x66, local copies, waits for them, and re-layouts  10.5 us
  transfers between devices with their start and end apart: 46, of which 14 were waited for; matrix products, arithmetic and copies ran while one was open for 4% of the time, Pallas kernels for 7%

profile of v1, /device:TPU:0, one launch (start us, length us, event | category | flops | bytes accessed | tf_op | source)
XLA Modules:
  0.0 175.4 jit_solution(7578006979980731676)
XLA Ops:
  0.7 0.8 convert.7
  1.6 0.7 convert.6
  2.3 1.4 convolution_convert_fusion
  3.9 1.6 collective-permute-start
  5.5 1.7 collective-permute-start.1
  7.2 1.9 %collective-permute-start.2 = (bf16[80,384]{1,0:T(8,128)(2,1)S(1)}, bf16[80,384]{1,0:T(8,128)(2,1)S(1)}, u32[]{:S(2)}, u32[]{:S(2)}) collective-permute-start(bf16[80,384]{1,0:T(8,128)(2,1)S(1)} %pad_maximum_fusion.1), channel_id=1, source_target_pairs={{0,16},{2,66},{4,20},{6,70},{8,24},{10,74},{12,28},{14,78},{16,0},... | collective-permute-start | bytes 184328 | tf_op jit(solution)/shard_map/ppermute | solution.py:69
  9.1 4.0 %collective-permute-start.10 = (bf16[256,384]{1,0:T(8,128)(2,1)S(1)}, bf16[256,384]{1,0:T(8,128)(2,1)S(1)}, u32[]{:S(2)}, u32[]{:S(2)}) collective-permute-start(bf16[256,384]{1,0:T(8,128)(2,1)S(1)} %bitcast.25), channel_id=1, source_target_pairs={{0,96},{2,26},{4,100},{6,30},{8,104},{10,2},{12,108},{14,6},{16,11... | collective-permute-start | bytes 589832 | tf_op jit(solution)/shard_map/ppermute | solution.py:69
  13.1 1.3 collective-permute-start.9
  15.0 2.6 %collective-permute-start.4 = (bf16[256,384]{1,0:T(8,128)(2,1)S(1)}, bf16[256,384]{1,0:T(8,128)(2,1)S(1)}, u32[]{:S(2)}, u32[]{:S(2)}) collective-permute-start(bf16[256,384]{1,0:T(8,128)(2,1)S(1)} %bitcast.18), channel_id=1, source_target_pairs={{0,24},{2,98},{4,28},{6,102},{8,0},{10,106},{12,4},{14,110},{16,8}... | collective-permute-start | bytes 589832 | tf_op jit(solution)/shard_map/ppermute | solution.py:69
  17.8 1.4 collective-permute-done.10.refs_10_.refs_7_.refs_9_
  19.2 1.7 collective-permute-start.5
  21.6 2.0 %collective-permute-start.18 = (bf16[256,384]{1,0:T(8,128)(2,1)S(1)}, bf16[256,384]{1,0:T(8,128)(2,1)}, u32[]{:S(2)}, u32[]{:S(2)}) collective-permute-start(bf16[256,384]{1,0:T(8,128)(2,1)S(1)} %bitcast.31), channel_id=1, source_target_pairs={{0,32},{2,10},{4,36},{6,14},{8,40},{10,18},{12,44},{14,22},{16,48}... | collective-permute-start | bytes 589832 | tf_op jit(solution)/shard_map/ppermute | solution.py:69
  23.6 1.3 collective-permute-done.9.refs_9_.refs_6_.refs_8_
  26.2 3.2 %collective-permute-start.7 = (bf16[256,384]{1,0:T(8,128)(2,1)S(1)}, bf16[256,384]{1,0:T(8,128)(2,1)}, u32[]{:S(2)}, u32[]{:S(2)}) collective-permute-start(bf16[256,384]{1,0:T(8,128)(2,1)S(1)} %pad_maximum_fusion.refs_4_), channel_id=1, source_target_pairs={{0,96},{2,26},{4,100},{6,30},{8,104},{10,2},{12,108},{14,6},{16,11... | collective-permute-start | bytes 589832 | tf_op jit(solution)/shard_map/ppermute | solution.py:69
  30.1 2.9 %collective-permute-start.8 = (bf16[256,384]{1,0:T(8,128)(2,1)S(1)}, bf16[256,384]{1,0:T(8,128)(2,1)}, u32[]{:S(2)}, u32[]{:S(2)}) collective-permute-start(bf16[256,384]{1,0:T(8,128)(2,1)S(1)} %pad_maximum_fusion.refs_4_), channel_id=1, source_target_pairs={{0,64},{2,18},{4,68},{6,22},{8,72},{10,26},{12,76},{14,30},{16,80}... | collective-permute-start | bytes 589832 | tf_op jit(solution)/shard_map/ppermute | solution.py:69
  33.7 0.9 collective-permute-start.20
  34.5 1.0 collective-permute-start.15
  35.5 2.2 %collective-permute-start.16 = (bf16[256,384]{1,0:T(8,128)(2,1)S(1)}, bf16[256,384]{1,0:T(8,128)(2,1)S(1)}, u32[]{:S(2)}, u32[]{:S(2)}) collective-permute-start(bf16[256,384]{1,0:T(8,128)(2,1)S(1)} %bitcast.22), channel_id=1, source_target_pairs={{0,24},{2,98},{4,28},{6,102},{8,0},{10,106},{12,4},{14,110},{16,8}... | collective-permute-start | bytes 589832 | tf_op jit(solution)/shard_map/ppermute | solution.py:69
  37.8 1.9 %collective-permute-done.8.refs_7_ = bf16[256,384]{1,0:T(8,128)(2,1)} collective-permute-done((bf16[256,384]{1,0:T(8,128)(2,1)S(1)}, bf16[256,384]{1,0:T(8,128)(2,1)}, u32[]{:S(2)}, u32[]{:S(2)}) %collective-permute-start.8) | collective-permute-done | bytes 196640 | tf_op jit(solution)/shard_map/ppermute | solution.py:69
  39.7 2.0 %collective-permute-start.17 = (bf16[256,384]{1,0:T(8,128)(2,1)S(1)}, bf16[256,384]{1,0:T(8,128)(2,1)S(1)}, u32[]{:S(2)}, u32[]{:S(2)}) collective-permute-start(bf16[256,384]{1,0:T(8,128)(2,1)S(1)} %bitcast.23), channel_id=1, source_target_pairs={{0,16},{2,66},{4,20},{6,70},{8,24},{10,74},{12,28},{14,78},{16,0},... | collective-permute-start | bytes 589832 | tf_op jit(solution)/shard_map/ppermute | solution.py:69
  41.7 0.7 fusion.9.info
  44.4 0.9 copy-done.14
  45.4 0.9 copy-done.17
  46.3 0.9 copy-done.27
  47.2 0.9 copy-done.29
  48.1 8.7 %scores.1 = (bf16[1024,384]{1,0:T(8,128)(2,1)S(1)}, f32[8,1024]{1,0:T(8,128)S(1)}) custom-call(s32[64]{0:T(128)S(1)} %fusion.9.info, s32[16,128]{1,0:T(8,128)S(1)} %maximum_convert_fusion.lists, bf16[256,384]{1,0:T(8,128)(2,1)S(1)} %bitcast.20, bf16[256,384]{1,0:T(8,128)(2,1)S(1)} %copy-done.27, bf16[256,384]{1,0:T(8,128)(2,1)S(1)} %copy-done.29, ...), custom_call_target="tpu_custom_call" | custom-call | flops 402653184 | bytes 4194304 | tf_op jit(solution)/shard_map/scores/pallas_call | solution.py:279
  57.0 3.2 %collective-permute-start.13 = (f32[8,1024]{1,0:T(8,128)S(1)}, f32[8,1024]{1,0:T(8,128)S(1)}, u32[]{:S(2)}, u32[]{:S(2)}) collective-permute-start(f32[8,1024]{1,0:T(8,128)S(1)} %get-tuple-element.33.refs_0_), channel_id=1, source_target_pairs={{0,24},{2,98},{4,28},{6,102},{8,0},{10,106},{12,4},{14,110},{16,8}... | collective-permute-start | bytes 98312 | tf_op jit(solution)/shard_map/ppermute | solution.py:69
  60.5 1.5 collective-permute-done.12.refs_1_
  62.1 3.5 %collective-permute-done.14.refs_3_ = f32[8,1024]{1,0:T(8,128)S(1)} collective-permute-done((f32[8,1024]{1,0:T(8,128)S(1)}, f32[8,1024]{1,0:T(8,128)S(1)}, u32[]{:S(2)}, u32[]{:S(2)}) %collective-permute-start.14) | collective-permute-done | bytes 32800 | tf_op jit(solution)/shard_map/ppermute | solution.py:69
  65.6 0.9 copy-done.12
  66.5 15.3 %values.1 = (bf16[256,384]{1,0:T(8,128)(2,1)S(1)}, bf16[256,384]{1,0:T(8,128)(2,1)}, bf16[256,384]{1,0:T(8,128)(2,1)}, bf16[256,384]{1,0:T(8,128)(2,1)}, f32[8,1...) custom-call(s32[64]{0:T(128)S(1)} %fusion.9.info, s32[16,128]{1,0:T(8,128)S(1)} %maximum_convert_fusion.lists, ...), custom_call_target="tpu_custom_call" | custom-call | flops 1207959552 | bytes 6291456 | tf_op jit(solution)/shard_map/values/pallas_call | solution.py:279
  81.8 3.2 %collective-permute-start.22 = (f32[8,1024]{1,0:T(8,128)S(1)}, f32[8,1024]{1,0:T(8,128)S(1)}, u32[]{:S(2)}, u32[]{:S(2)}) collective-permute-start(f32[8,1024]{1,0:T(8,128)S(1)} %get-tuple-element.36.refs_1_), channel_id=1, source_target_pairs={{0,24},{2,98},{4,28},{6,102},{8,0},{10,106},{12,4},{14,110},{16,8}... | collective-permute-start | bytes 98312 | tf_op jit(solution)/shard_map/ppermute | solution.py:69
  85.0 1.9 %collective-permute-done.21.refs_2_ = f32[8,1024]{1,0:T(8,128)S(1)} collective-permute-done((f32[8,1024]{1,0:T(8,128)S(1)}, f32[8,1024]{1,0:T(8,128)S(1)}, u32[]{:S(2)}, u32[]{:S(2)}) %collective-permute-start.21) | collective-permute-done | bytes 32800 | tf_op jit(solution)/shard_map/ppermute | solution.py:69
  86.9 3.5 %collective-permute-done.23.refs_4_ = f32[8,1024]{1,0:T(8,128)S(1)} collective-permute-done((f32[8,1024]{1,0:T(8,128)S(1)}, f32[8,1024]{1,0:T(8,128)S(1)}, u32[]{:S(2)}, u32[]{:S(2)}) %collective-permute-start.23) | collective-permute-done | bytes 32800 | tf_op jit(solution)/shard_map/ppermute | solution.py:69
  90.5 17.7 %grads.1 = (bf16[256,384]{1,0:T(8,128)(2,1)S(1)}, bf16[256,384]{1,0:T(8,128)(2,1)S(1)}, bf16[256,384]{1,0:T(8,128)(2,1)S(1)}, bf16[256,384]{1,0:T(8,128)(2,1)S(1...) custom-call(s32[64]{0:T(128)S(1)} %fusion.9.info, ...), custom_call_target="tpu_custom_call" | custom-call | flops 1610612736 | bytes 7340032 | tf_op jit(solution)/shard_map/grads/pallas_call | solution.py:279
  108.4 2.0 %collective-permute-start.34 = (bf16[256,384]{1,0:T(8,128)(2,1)S(1)}, bf16[256,384]{1,0:T(8,128)(2,1)S(1)}, u32[]{:S(2)}, u32[]{:S(2)}) collective-permute-start(bf16[256,384]{1,0:T(8,128)(2,1)S(1)} %get-tuple-element.52), channel_id=1, source_target_pairs={{0,8},{2,34},{4,12},{6,38},{8,16},{10,42},{12,20},{14,46},{16,24},... | collective-permute-start | bytes 589832 | tf_op jit(solution)/shard_map/ppermute | solution.py:69
  110.3 1.4 tokens.1
  111.7 1.0 collective-permute-start.39
  112.8 2.2 %collective-permute-start.40 = (bf16[64,1024]{1,0:T(8,128)(2,1)S(1)}, bf16[64,1024]{1,0:T(8,128)(2,1)S(1)}, u32[]{:S(2)}, u32[]{:S(2)}) collective-permute-start(bf16[64,1024]{1,0:T(8,128)(2,1)S(1)} %get-tuple-element.56), channel_id=1, source_target_pairs={{0,96},{2,26},{4,100},{6,30},{8,104},{10,2},{12,108},{14,6},{16,11... | collective-permute-start | bytes 393224 | tf_op jit(solution)/shard_map/ppermute | solution.py:69
  115.0 1.3 collective-permute-start.30
  116.3 6.4 %collective-permute-done.34 = bf16[256,384]{1,0:T(8,128)(2,1)S(1)} collective-permute-done((bf16[256,384]{1,0:T(8,128)(2,1)S(1)}, bf16[256,384]{1,0:T(8,128)(2,1)S(1)}, u32[]{:S(2)}, u32[]{:S(2)}) %collective-permute-start.34) | collective-permute-done | bytes 196640 | tf_op jit(solution)/shard_map/ppermute | solution.py:69
  122.7 1.6 collective-permute-start.32
  125.1 2.5 %collective-permute-start.36 = (bf16[256,384]{1,0:T(8,128)(2,1)S(1)}, bf16[256,384]{1,0:T(8,128)(2,1)S(1)}, u32[]{:S(2)}, u32[]{:S(2)}) collective-permute-start(bf16[256,384]{1,0:T(8,128)(2,1)S(1)} %add_convert_fusion.refs_0_), channel_id=1, source_target_pairs={{0,32},{2,10},{4,36},{6,14},{8,40},{10,18},{12,44},{14,22},{16,48}... | collective-permute-start | bytes 589832 | tf_op jit(solution)/shard_map/ppermute | solution.py:69
  128.2 0.7 collective-permute-start.41
  128.9 6.4 %collective-permute-done.41.refs_7_ = bf16[64,1024]{1,0:T(8,128)(2,1)} collective-permute-done((bf16[64,1024]{1,0:T(8,128)(2,1)}, bf16[64,1024]{1,0:T(8,128)(2,1)}, u32[]{:S(2)}, u32[]{:S(2)}) %collective-permute-start.41) | collective-permute-done | bytes 131104 | tf_op jit(solution)/shard_map/ppermute | solution.py:69
  135.9 1.5 collective-permute-start.28
  137.4 1.3 collective-permute-start.29
  138.7 2.5 %collective-permute-start.37 = (bf16[256,384]{1,0:T(8,128)(2,1)S(1)}, bf16[256,384]{1,0:T(8,128)(2,1)S(1)}, u32[]{:S(2)}, u32[]{:S(2)}) collective-permute-start(bf16[256,384]{1,0:T(8,128)(2,1)S(1)} %add_convert_fusion.refs_0_), channel_id=1, source_target_pairs={{0,96},{2,26},{4,100},{6,30},{8,104},{10,2},{12,108},{14,6},{16,11... | collective-permute-start | bytes 589832 | tf_op jit(solution)/shard_map/ppermute | solution.py:69
  141.2 0.8 collective-permute-start.38
  142.0 1.9 %fusion.2 = bf16[1,256,384]{2,1,0:T(8,128)(2,1)} fusion(bf16[256,384]{1,0:T(8,128)(2,1)} %collective-permute-done.32, bf16[256,384]{1,0:T(8,128)(2,1)} %collective-permute-done.31, bf16[256,384]{1,0:T(8,128)(2,1)} %collective-permute-done.30, bf16[256,384]{1,0:T(8,128)(2,1)S(1)} %get-tuple-element.46), kind=kLoop, calls=%fused_computation.8 | loop fusion | flops 786432 | bytes 983040 | tf_op jit(solution)/shard_map/broadcast_in_dim | solution.py:391
  143.9 6.8 %collective-permute-done.37.refs_2_ = bf16[256,384]{1,0:T(8,128)(2,1)S(1)} collective-permute-done((bf16[256,384]{1,0:T(8,128)(2,1)S(1)}, bf16[256,384]{1,0:T(8,128)(2,1)S(1)}, u32[]{:S(2)}, u32[]{:S(2)}) %collective-permute-start.37) | collective-permute-done | bytes 196640 | tf_op jit(solution)/shard_map/ppermute | solution.py:69
  150.7 1.3 collective-permute-done.38.refs_3_
  152.0 0.7 collective-permute-start.25
  152.8 0.9 copy-done.3
  153.7 0.9 copy-done.5
  154.6 1.4 weights.1
  156.0 2.6 %collective-permute-start.42 = (bf16[192,384]{1,0:T(8,128)(2,1)S(1)}, bf16[192,384]{1,0:T(8,128)(2,1)S(1)}, u32[]{:S(2)}, u32[]{:S(2)}) collective-permute-start(bf16[192,384]{1,0:T(8,128)(2,1)S(1)} %get-tuple-element.59), channel_id=1, source_target_pairs={{0,24},{2,98},{4,28},{6,102},{8,0},{10,106},{12,4},{14,110},{16,8}... | collective-permute-start | bytes 442376 | tf_op jit(solution)/shard_map/ppermute | solution.py:69
  158.6 1.5 collective-permute-start.44
  160.2 0.8 fusion.1
  161.3 1.9 %collective-permute-start.26 = (bf16[256,384]{1,0:T(8,128)(2,1)S(1)}, bf16[256,384]{1,0:T(8,128)(2,1)S(1)}, u32[]{:S(2)}, u32[]{:S(2)}) collective-permute-start(bf16[256,384]{1,0:T(8,128)(2,1)S(1)} %copy-done.20), channel_id=1, source_target_pairs={{0,16},{2,66},{4,20},{6,70},{8,24},{10,74},{12,28},{14,78},{16,0},... | collective-permute-start | bytes 589832 | tf_op jit(solution)/shard_map/ppermute | solution.py:69
  163.2 5.5 %collective-permute-done.43 = bf16[192,384]{1,0:T(8,128)(2,1)S(1)} collective-permute-done((bf16[192,384]{1,0:T(8,128)(2,1)S(1)}, bf16[192,384]{1,0:T(8,128)(2,1)S(1)}, u32[]{:S(2)}, u32[]{:S(2)}) %collective-permute-start.43) | collective-permute-done | bytes 147488 | tf_op jit(solution)/shard_map/ppermute | solution.py:69
  168.8 3.3 %collective-permute-start.45 = (bf16[96,384]{1,0:T(8,128)(2,1)S(1)}, bf16[96,384]{1,0:T(8,128)(2,1)S(1)}, u32[]{:S(2)}, u32[]{:S(2)}) collective-permute-start(bf16[96,384]{1,0:T(8,128)(2,1)S(1)} %dynamic-slice_convert_fusion), channel_id=1, source_target_pairs={{0,1},{1,0},{2,3},{3,2},{4,5},{5,4},{6,7},{7,6},{8,9},{9,8},{10,11... | collective-permute-start | bytes 221192 | tf_op jit(solution)/shard_map/ppermute | solution.py:388
  172.0 0.8 fusion
  172.8 1.9 %collective-permute-done.45 = bf16[96,384]{1,0:T(8,128)(2,1)S(1)} collective-permute-done((bf16[96,384]{1,0:T(8,128)(2,1)S(1)}, bf16[96,384]{1,0:T(8,128)(2,1)S(1)}, u32[]{:S(2)}, u32[]{:S(2)}) %collective-permute-start.45) | collective-permute-done | bytes 73760 | tf_op jit(solution)/shard_map/ppermute | solution.py:388
  (122 shorter events, 10.0 us)
Async XLA Ops:
  0.6 8.4 %copy-start.8 = (bf16[1,256,384]{2,1,0:T(8,128)(2,1)S(1)}, bf16[1,256,384]{2,1,0:T(8,128)(2,1)}, u32[]{:S(2)}) copy-start(bf16[1,256,384]{2,1,0:T(8,128)(2,1)} %param.10) | copy-start | bytes 589828
  0.7 13.7 %copy-start.6 = (bf16[1,256,384]{2,1,0:T(8,128)(2,1)S(1)}, bf16[1,256,384]{2,1,0:T(8,128)(2,1)}, u32[]{:S(2)}) copy-start(bf16[1,256,384]{2,1,0:T(8,128)(2,1)} %param.9) | copy-start | bytes 589828
  0.7 20.9 %copy-start.9 = (bf16[1,256,384]{2,1,0:T(8,128)(2,1)S(1)}, bf16[1,256,384]{2,1,0:T(8,128)(2,1)}, u32[]{:S(2)}) copy-start(bf16[1,256,384]{2,1,0:T(8,128)(2,1)} %param.11) | copy-start | bytes 589828
  0.7 33.8 %copy-start.7 = (bf16[1,256,384]{2,1,0:T(8,128)(2,1)S(1)}, bf16[1,256,384]{2,1,0:T(8,128)(2,1)}, u32[]{:S(2)}) copy-start(bf16[1,256,384]{2,1,0:T(8,128)(2,1)} %param.12) | copy-start | bytes 589828
  3.9 9.2 %collective-permute-start = (bf16[80,384]{1,0:T(8,128)(2,1)S(1)}, bf16[80,384]{1,0:T(8,128)(2,1)S(1)}, u32[]{:S(2)}, u32[]{:S(2)}) collective-permute-start(bf16[80,384]{1,0:T(8,128)(2,1)S(1)} %pad_maximum_fusion.1), channel_id=1, source_target_pairs={{0,8},{2,34},{4,12},{6,38},{8,16},{10,42},{12,20},{14,46},{16,24},... | collective-permute-start | bytes 184328 | tf_op jit(solution)/shard_map/ppermute | solution.py:69
  5.5 8.9 %collective-permute-start.1 = (bf16[80,384]{1,0:T(8,128)(2,1)S(1)}, bf16[80,384]{1,0:T(8,128)(2,1)S(1)}, u32[]{:S(2)}, u32[]{:S(2)}) collective-permute-start(bf16[80,384]{1,0:T(8,128)(2,1)S(1)} %pad_maximum_fusion.1), channel_id=1, source_target_pairs={{0,24},{2,98},{4,28},{6,102},{8,0},{10,106},{12,4},{14,110},{16,8}... | collective-permute-start | bytes 184328 | tf_op jit(solution)/shard_map/ppermute | solution.py:69
  7.2 7.9 %collective-permute-start.2 = (bf16[80,384]{1,0:T(8,128)(2,1)S(1)}, bf16[80,384]{1,0:T(8,128)(2,1)S(1)}, u32[]{:S(2)}, u32[]{:S(2)}) collective-permute-start(bf16[80,384]{1,0:T(8,128)(2,1)S(1)} %pad_maximum_fusion.1), channel_id=1, source_target_pairs={{0,16},{2,66},{4,20},{6,70},{8,24},{10,74},{12,28},{14,78},{16,0},... | collective-permute-start | bytes 184328 | tf_op jit(solution)/shard_map/ppermute | solution.py:69
  9.1 10.1 %collective-permute-start.10 = (bf16[256,384]{1,0:T(8,128)(2,1)S(1)}, bf16[256,384]{1,0:T(8,128)(2,1)S(1)}, u32[]{:S(2)}, u32[]{:S(2)}) collective-permute-start(bf16[256,384]{1,0:T(8,128)(2,1)S(1)} %bitcast.25), channel_id=1, source_target_pairs={{0,96},{2,26},{4,100},{6,30},{8,104},{10,2},{12,108},{14,6},{16,11... | collective-permute-start | bytes 589832 | tf_op jit(solution)/shard_map/ppermute | solution.py:69
  13.1 7.8 %collective-permute-start.11 = (bf16[256,384]{1,0:T(8,128)(2,1)S(1)}, bf16[256,384]{1,0:T(8,128)(2,1)S(1)}, u32[]{:S(2)}, u32[]{:S(2)}) collective-permute-start(bf16[256,384]{1,0:T(8,128)(2,1)S(1)} %bitcast.26), channel_id=1, source_target_pairs={{0,64},{2,18},{4,68},{6,22},{8,72},{10,26},{12,76},{14,30},{16,80}... | collective-permute-start | bytes 589832 | tf_op jit(solution)/shard_map/ppermute | solution.py:69
  13.1 4.6 %copy-start.30 = (bf16[80,384]{1,0:T(8,128)(2,1)}, bf16[80,384]{1,0:T(8,128)(2,1)S(1)}, u32[]{:S(2)}) copy-start(bf16[80,384]{1,0:T(8,128)(2,1)S(1)} %collective-permute-done) | copy-start | bytes 184324
  13.1 11.7 %collective-permute-start.9 = (bf16[256,384]{1,0:T(8,128)(2,1)S(1)}, bf16[256,384]{1,0:T(8,128)(2,1)S(1)}, u32[]{:S(2)}, u32[]{:S(2)}) collective-permute-start(bf16[256,384]{1,0:T(8,128)(2,1)S(1)} %bitcast.27), channel_id=1, source_target_pairs={{0,32},{2,10},{4,36},{6,14},{8,40},{10,18},{12,44},{14,22},{16,48}... | collective-permute-start | bytes 589832 | tf_op jit(solution)/shard_map/ppermute | solution.py:69
  14.4 3.3 %copy-start.31 = (bf16[80,384]{1,0:T(8,128)(2,1)}, bf16[80,384]{1,0:T(8,128)(2,1)S(1)}, u32[]{:S(2)}) copy-start(bf16[80,384]{1,0:T(8,128)(2,1)S(1)} %collective-permute-done.1) | copy-start | bytes 184324
  14.4 11.1 %collective-permute-start.3 = (bf16[256,384]{1,0:T(8,128)(2,1)S(1)}, bf16[256,384]{1,0:T(8,128)(2,1)S(1)}, u32[]{:S(2)}, u32[]{:S(2)}) collective-permute-start(bf16[256,384]{1,0:T(8,128)(2,1)S(1)} %bitcast.17), channel_id=1, source_target_pairs={{0,8},{2,34},{4,12},{6,38},{8,16},{10,42},{12,20},{14,46},{16,24},... | collective-permute-start | bytes 589832 | tf_op jit(solution)/shard_map/ppermute | solution.py:69
  15.0 14.4 %collective-permute-start.4 = (bf16[256,384]{1,0:T(8,128)(2,1)S(1)}, bf16[256,384]{1,0:T(8,128)(2,1)S(1)}, u32[]{:S(2)}, u32[]{:S(2)}) collective-permute-start(bf16[256,384]{1,0:T(8,128)(2,1)S(1)} %bitcast.18), channel_id=1, source_target_pairs={{0,24},{2,98},{4,28},{6,102},{8,0},{10,106},{12,4},{14,110},{16,8}... | collective-permute-start | bytes 589832 | tf_op jit(solution)/shard_map/ppermute | solution.py:69
  19.2 46.4 %copy-start.11 = (bf16[256,384]{1,0:T(8,128)(2,1)}, bf16[256,384]{1,0:T(8,128)(2,1)S(1)}, u32[]{:S(2)}) copy-start(bf16[256,384]{1,0:T(8,128)(2,1)S(1)} %collective-permute-done.10.refs_10_.refs_7_.refs_9_) | copy-start | bytes 589828
  19.2 13.9 %collective-permute-start.5 = (bf16[256,384]{1,0:T(8,128)(2,1)S(1)}, bf16[256,384]{1,0:T(8,128)(2,1)}, u32[]{:S(2)}, u32[]{:S(2)}) collective-permute-start(bf16[256,384]{1,0:T(8,128)(2,1)S(1)} %bitcast.19), channel_id=1, source_target_pairs={{0,16},{2,66},{4,20},{6,70},{8,24},{10,74},{12,28},{14,78},{16,0},... | collective-permute-start | bytes 589832 | tf_op jit(solution)/shard_map/ppermute | solution.py:69
  21.6 12.1 %collective-permute-start.18 = (bf16[256,384]{1,0:T(8,128)(2,1)S(1)}, bf16[256,384]{1,0:T(8,128)(2,1)}, u32[]{:S(2)}, u32[]{:S(2)}) collective-permute-start(bf16[256,384]{1,0:T(8,128)(2,1)S(1)} %bitcast.31), channel_id=1, source_target_pairs={{0,32},{2,10},{4,36},{6,14},{8,40},{10,18},{12,44},{14,22},{16,48}... | collective-permute-start | bytes 589832 | tf_op jit(solution)/shard_map/ppermute | solution.py:69
  25.5 9.0 %collective-permute-start.6 = (bf16[256,384]{1,0:T(8,128)(2,1)S(1)}, bf16[256,384]{1,0:T(8,128)(2,1)}, u32[]{:S(2)}, u32[]{:S(2)}) collective-permute-start(bf16[256,384]{1,0:T(8,128)(2,1)S(1)} %pad_maximum_fusion.refs_4_), channel_id=1, source_target_pairs={{0,32},{2,10},{4,36},{6,14},{8,40},{10,18},{12,44},{14,22},{16,48}... | collective-permute-start | bytes 589832 | tf_op jit(solution)/shard_map/ppermute | solution.py:69
  26.2 9.3 %collective-permute-start.7 = (bf16[256,384]{1,0:T(8,128)(2,1)S(1)}, bf16[256,384]{1,0:T(8,128)(2,1)}, u32[]{:S(2)}, u32[]{:S(2)}) collective-permute-start(bf16[256,384]{1,0:T(8,128)(2,1)S(1)} %pad_maximum_fusion.refs_4_), channel_id=1, source_target_pairs={{0,96},{2,26},{4,100},{6,30},{8,104},{10,2},{12,108},{14,6},{16,11... | collective-permute-start | bytes 589832 | tf_op jit(solution)/shard_map/ppermute | solution.py:69
  30.1 9.6 %collective-permute-start.8 = (bf16[256,384]{1,0:T(8,128)(2,1)S(1)}, bf16[256,384]{1,0:T(8,128)(2,1)}, u32[]{:S(2)}, u32[]{:S(2)}) collective-permute-start(bf16[256,384]{1,0:T(8,128)(2,1)S(1)} %pad_maximum_fusion.refs_4_), channel_id=1, source_target_pairs={{0,64},{2,18},{4,68},{6,22},{8,72},{10,26},{12,76},{14,30},{16,80}... | collective-permute-start | bytes 589832 | tf_op jit(solution)/shard_map/ppermute | solution.py:69
  33.0 23.8 %collective-permute-start.19 = (bf16[256,384]{1,0:T(8,128)(2,1)S(1)}, bf16[256,384]{1,0:T(8,128)(2,1)S(1)}, u32[]{:S(2)}, u32[]{:S(2)}) collective-permute-start(bf16[256,384]{1,0:T(8,128)(2,1)S(1)} %bitcast.32), channel_id=1, source_target_pairs={{0,96},{2,26},{4,100},{6,30},{8,104},{10,2},{12,108},{14,6},{16,11... | collective-permute-start | bytes 589832 | tf_op jit(solution)/shard_map/ppermute | solution.py:69
  33.7 23.3 %collective-permute-start.20 = (bf16[256,384]{1,0:T(8,128)(2,1)S(1)}, bf16[256,384]{1,0:T(8,128)(2,1)S(1)}, u32[]{:S(2)}, u32[]{:S(2)}) collective-permute-start(bf16[256,384]{1,0:T(8,128)(2,1)S(1)} %bitcast.33), channel_id=1, source_target_pairs={{0,64},{2,18},{4,68},{6,22},{8,72},{10,26},{12,76},{14,30},{16,80}... | collective-permute-start | bytes 589832 | tf_op jit(solution)/shard_map/ppermute | solution.py:69
  34.5 25.7 %collective-permute-start.15 = (bf16[256,384]{1,0:T(8,128)(2,1)S(1)}, bf16[256,384]{1,0:T(8,128)(2,1)S(1)}, u32[]{:S(2)}, u32[]{:S(2)}) collective-permute-start(bf16[256,384]{1,0:T(8,128)(2,1)S(1)} %bitcast.21), channel_id=1, source_target_pairs={{0,8},{2,34},{4,12},{6,38},{8,16},{10,42},{12,20},{14,46},{16,24},... | collective-permute-start | bytes 589832 | tf_op jit(solution)/shard_map/ppermute | solution.py:69
  35.5 25.0 %collective-permute-start.16 = (bf16[256,384]{1,0:T(8,128)(2,1)S(1)}, bf16[256,384]{1,0:T(8,128)(2,1)S(1)}, u32[]{:S(2)}, u32[]{:S(2)}) collective-permute-start(bf16[256,384]{1,0:T(8,128)(2,1)S(1)} %bitcast.22), channel_id=1, source_target_pairs={{0,24},{2,98},{4,28},{6,102},{8,0},{10,106},{12,4},{14,110},{16,8}... | collective-permute-start | bytes 589832 | tf_op jit(solution)/shard_map/ppermute | solution.py:69
  39.7 20.8 %collective-permute-start.17 = (bf16[256,384]{1,0:T(8,128)(2,1)S(1)}, bf16[256,384]{1,0:T(8,128)(2,1)S(1)}, u32[]{:S(2)}, u32[]{:S(2)}) collective-permute-start(bf16[256,384]{1,0:T(8,128)(2,1)S(1)} %bitcast.23), channel_id=1, source_target_pairs={{0,16},{2,66},{4,20},{6,70},{8,24},{10,74},{12,28},{14,78},{16,0},... | collective-permute-start | bytes 589832 | tf_op jit(solution)/shard_map/ppermute | solution.py:69
  48.1 17.5 %copy-start.15 = (bf16[256,384]{1,0:T(8,128)(2,1)S(1)}, bf16[256,384]{1,0:T(8,128)(2,1)}, u32[]{:S(2)}) copy-start(bf16[256,384]{1,0:T(8,128)(2,1)} %copy-done.13) | copy-start | bytes 589828
  48.1 17.5 %copy-start.18 = (bf16[256,384]{1,0:T(8,128)(2,1)S(1)}, bf16[256,384]{1,0:T(8,128)(2,1)}, u32[]{:S(2)}) copy-start(bf16[256,384]{1,0:T(8,128)(2,1)} %copy-done.16) | copy-start | bytes 589828
  56.9 33.6 %copy-start.10 = (bf16[1,256,384]{2,1,0:T(8,128)(2,1)S(1)}, bf16[1,256,384]{2,1,0:T(8,128)(2,1)}, u32[]{:S(2)}) copy-start(bf16[1,256,384]{2,1,0:T(8,128)(2,1)} %param.11) | copy-start | bytes 589828
  56.9 5.2 %collective-permute-start.12 = (f32[8,1024]{1,0:T(8,128)S(1)}, f32[8,1024]{1,0:T(8,128)S(1)}, u32[]{:S(2)}, u32[]{:S(2)}) collective-permute-start(f32[8,1024]{1,0:T(8,128)S(1)} %get-tuple-element.33.refs_0_), channel_id=1, source_target_pairs={{0,8},{2,34},{4,12},{6,38},{8,16},{10,42},{12,20},{14,46},{16,24},... | collective-permute-start | bytes 98312 | tf_op jit(solution)/shard_map/ppermute | solution.py:69
  57.0 5.1 %collective-permute-start.13 = (f32[8,1024]{1,0:T(8,128)S(1)}, f32[8,1024]{1,0:T(8,128)S(1)}, u32[]{:S(2)}, u32[]{:S(2)}) collective-permute-start(f32[8,1024]{1,0:T(8,128)S(1)} %get-tuple-element.33.refs_0_), channel_id=1, source_target_pairs={{0,24},{2,98},{4,28},{6,102},{8,0},{10,106},{12,4},{14,110},{16,8}... | collective-permute-start | bytes 98312 | tf_op jit(solution)/shard_map/ppermute | solution.py:69
  60.2 5.4 %collective-permute-start.14 = (f32[8,1024]{1,0:T(8,128)S(1)}, f32[8,1024]{1,0:T(8,128)S(1)}, u32[]{:S(2)}, u32[]{:S(2)}) collective-permute-start(f32[8,1024]{1,0:T(8,128)S(1)} %get-tuple-element.33.refs_0_), channel_id=1, source_target_pairs={{0,16},{2,66},{4,20},{6,70},{8,24},{10,74},{12,28},{14,78},{16,0},... | collective-permute-start | bytes 98312 | tf_op jit(solution)/shard_map/ppermute | solution.py:69
  81.8 5.1 %collective-permute-start.21 = (f32[8,1024]{1,0:T(8,128)S(1)}, f32[8,1024]{1,0:T(8,128)S(1)}, u32[]{:S(2)}, u32[]{:S(2)}) collective-permute-start(f32[8,1024]{1,0:T(8,128)S(1)} %get-tuple-element.36.refs_1_), channel_id=1, source_target_pairs={{0,8},{2,34},{4,12},{6,38},{8,16},{10,42},{12,20},{14,46},{16,24},... | collective-permute-start | bytes 98312 | tf_op jit(solution)/shard_map/ppermute | solution.py:69
  81.8 5.1 %collective-permute-start.22 = (f32[8,1024]{1,0:T(8,128)S(1)}, f32[8,1024]{1,0:T(8,128)S(1)}, u32[]{:S(2)}, u32[]{:S(2)}) collective-permute-start(f32[8,1024]{1,0:T(8,128)S(1)} %get-tuple-element.36.refs_1_), channel_id=1, source_target_pairs={{0,24},{2,98},{4,28},{6,102},{8,0},{10,106},{12,4},{14,110},{16,8}... | collective-permute-start | bytes 98312 | tf_op jit(solution)/shard_map/ppermute | solution.py:69
  85.0 5.4 %collective-permute-start.23 = (f32[8,1024]{1,0:T(8,128)S(1)}, f32[8,1024]{1,0:T(8,128)S(1)}, u32[]{:S(2)}, u32[]{:S(2)}) collective-permute-start(f32[8,1024]{1,0:T(8,128)S(1)} %get-tuple-element.36.refs_1_), channel_id=1, source_target_pairs={{0,16},{2,66},{4,20},{6,70},{8,24},{10,74},{12,28},{14,78},{16,0},... | collective-permute-start | bytes 98312 | tf_op jit(solution)/shard_map/ppermute | solution.py:69
  90.5 19.9 %copy-start.1 = (bf16[1,64,3072]{2,1,0:T(8,128)(2,1)S(1)}, bf16[1,64,3072]{2,1,0:T(8,128)(2,1)}, u32[]{:S(2)}) copy-start(bf16[1,64,3072]{2,1,0:T(8,128)(2,1)} %param.15) | copy-start | bytes 1179652
  108.2 19.4 %copy-start.19 = (bf16[256,384]{1,0:T(8,128)(2,1)}, bf16[256,384]{1,0:T(8,128)(2,1)S(1)}, u32[]{:S(2)}) copy-start(bf16[256,384]{1,0:T(8,128)(2,1)S(1)} %get-tuple-element.41) | copy-start | bytes 589828
  108.2 20.0 %copy-start.21 = (bf16[256,384]{1,0:T(8,128)(2,1)}, bf16[256,384]{1,0:T(8,128)(2,1)S(1)}, u32[]{:S(2)}) copy-start(bf16[256,384]{1,0:T(8,128)(2,1)S(1)} %get-tuple-element.40) | copy-start | bytes 589828
  108.2 20.0 %copy-start.22 = (bf16[256,384]{1,0:T(8,128)(2,1)}, bf16[256,384]{1,0:T(8,128)(2,1)S(1)}, u32[]{:S(2)}) copy-start(bf16[256,384]{1,0:T(8,128)(2,1)S(1)} %get-tuple-element.39) | copy-start | bytes 589828
  108.2 20.0 %copy-start.23 = (bf16[256,384]{1,0:T(8,128)(2,1)}, bf16[256,384]{1,0:T(8,128)(2,1)S(1)}, u32[]{:S(2)}) copy-start(bf16[256,384]{1,0:T(8,128)(2,1)S(1)} %get-tuple-element.45) | copy-start | bytes 589828
  108.2 20.0 %copy-start.24 = (bf16[256,384]{1,0:T(8,128)(2,1)}, bf16[256,384]{1,0:T(8,128)(2,1)S(1)}, u32[]{:S(2)}) copy-start(bf16[256,384]{1,0:T(8,128)(2,1)S(1)} %get-tuple-element.44) | copy-start | bytes 589828
  108.2 20.0 %copy-start.25 = (bf16[256,384]{1,0:T(8,128)(2,1)}, bf16[256,384]{1,0:T(8,128)(2,1)S(1)}, u32[]{:S(2)}) copy-start(bf16[256,384]{1,0:T(8,128)(2,1)S(1)} %get-tuple-element.43) | copy-start | bytes 589828
  108.2 6.7 %collective-permute-start.33 = (bf16[256,384]{1,0:T(8,128)(2,1)S(1)}, bf16[256,384]{1,0:T(8,128)(2,1)S(1)}, u32[]{:S(2)}, u32[]{:S(2)}) collective-permute-start(bf16[256,384]{1,0:T(8,128)(2,1)S(1)} %get-tuple-element.51), channel_id=1, source_target_pairs={{0,24},{2,98},{4,28},{6,102},{8,0},{10,106},{12,4},{14,110},{16,8}... | collective-permute-start | bytes 589832 | tf_op jit(solution)/shard_map/ppermute | solution.py:69
  108.4 14.3 %collective-permute-start.34 = (bf16[256,384]{1,0:T(8,128)(2,1)S(1)}, bf16[256,384]{1,0:T(8,128)(2,1)S(1)}, u32[]{:S(2)}, u32[]{:S(2)}) collective-permute-start(bf16[256,384]{1,0:T(8,128)(2,1)S(1)} %get-tuple-element.52), channel_id=1, source_target_pairs={{0,8},{2,34},{4,12},{6,38},{8,16},{10,42},{12,20},{14,46},{16,24},... | collective-permute-start | bytes 589832 | tf_op jit(solution)/shard_map/ppermute | solution.py:69
  110.3 12.4 %collective-permute-start.35 = (bf16[256,384]{1,0:T(8,128)(2,1)S(1)}, bf16[256,384]{1,0:T(8,128)(2,1)S(1)}, u32[]{:S(2)}, u32[]{:S(2)}) collective-permute-start(bf16[256,384]{1,0:T(8,128)(2,1)S(1)} %get-tuple-element.53), channel_id=1, source_target_pairs={{0,16},{2,66},{4,20},{6,70},{8,24},{10,74},{12,28},{14,78},{16,0},... | collective-permute-start | bytes 589832 | tf_op jit(solution)/shard_map/ppermute | solution.py:69
  111.7 12.7 %collective-permute-start.39 = (bf16[64,1024]{1,0:T(8,128)(2,1)S(1)}, bf16[64,1024]{1,0:T(8,128)(2,1)S(1)}, u32[]{:S(2)}, u32[]{:S(2)}) collective-permute-start(bf16[64,1024]{1,0:T(8,128)(2,1)S(1)} %get-tuple-element.55), channel_id=1, source_target_pairs={{0,32},{2,10},{4,36},{6,14},{8,40},{10,18},{12,44},{14,22},{16,48}... | collective-permute-start | bytes 393224 | tf_op jit(solution)/shard_map/ppermute | solution.py:69
  112.8 14.8 %collective-permute-start.40 = (bf16[64,1024]{1,0:T(8,128)(2,1)S(1)}, bf16[64,1024]{1,0:T(8,128)(2,1)S(1)}, u32[]{:S(2)}, u32[]{:S(2)}) collective-permute-start(bf16[64,1024]{1,0:T(8,128)(2,1)S(1)} %get-tuple-element.56), channel_id=1, source_target_pairs={{0,96},{2,26},{4,100},{6,30},{8,104},{10,2},{12,108},{14,6},{16,11... | collective-permute-start | bytes 393224 | tf_op jit(solution)/shard_map/ppermute | solution.py:69
  115.0 20.9 %collective-permute-start.30 = (bf16[256,384]{1,0:T(8,128)(2,1)}, bf16[256,384]{1,0:T(8,128)(2,1)}, u32[]{:S(2)}, u32[]{:S(2)}) collective-permute-start(bf16[256,384]{1,0:T(8,128)(2,1)} %get-tuple-element.47), channel_id=1, source_target_pairs={{0,96},{2,26},{4,100},{6,30},{8,104},{10,2},{12,108},{14,6},{16,11... | collective-permute-start | bytes 589832 | tf_op jit(solution)/shard_map/ppermute | solution.py:69
  122.7 14.7 %collective-permute-start.31 = (bf16[256,384]{1,0:T(8,128)(2,1)}, bf16[256,384]{1,0:T(8,128)(2,1)}, u32[]{:S(2)}, u32[]{:S(2)}) collective-permute-start(bf16[256,384]{1,0:T(8,128)(2,1)} %get-tuple-element.48), channel_id=1, source_target_pairs={{0,32},{2,10},{4,36},{6,14},{8,40},{10,18},{12,44},{14,22},{16,48}... | collective-permute-start | bytes 589832 | tf_op jit(solution)/shard_map/ppermute | solution.py:69
  122.7 16.0 %collective-permute-start.32 = (bf16[256,384]{1,0:T(8,128)(2,1)}, bf16[256,384]{1,0:T(8,128)(2,1)}, u32[]{:S(2)}, u32[]{:S(2)}) collective-permute-start(bf16[256,384]{1,0:T(8,128)(2,1)} %get-tuple-element.49), channel_id=1, source_target_pairs={{0,64},{2,18},{4,68},{6,22},{8,72},{10,26},{12,76},{14,30},{16,80}... | collective-permute-start | bytes 589832 | tf_op jit(solution)/shard_map/ppermute | solution.py:69
  125.1 16.2 %collective-permute-start.36 = (bf16[256,384]{1,0:T(8,128)(2,1)S(1)}, bf16[256,384]{1,0:T(8,128)(2,1)S(1)}, u32[]{:S(2)}, u32[]{:S(2)}) collective-permute-start(bf16[256,384]{1,0:T(8,128)(2,1)S(1)} %add_convert_fusion.refs_0_), channel_id=1, source_target_pairs={{0,32},{2,10},{4,36},{6,14},{8,40},{10,18},{12,44},{14,22},{16,48}... | collective-permute-start | bytes 589832 | tf_op jit(solution)/shard_map/ppermute | solution.py:69
  128.2 7.1 %collective-permute-start.41 = (bf16[64,1024]{1,0:T(8,128)(2,1)}, bf16[64,1024]{1,0:T(8,128)(2,1)}, u32[]{:S(2)}, u32[]{:S(2)}) collective-permute-start(bf16[64,1024]{1,0:T(8,128)(2,1)} %get-tuple-element.57), channel_id=1, source_target_pairs={{0,64},{2,18},{4,68},{6,22},{8,72},{10,26},{12,76},{14,30},{16,80}... | collective-permute-start | bytes 393224 | tf_op jit(solution)/shard_map/ppermute | solution.py:69
  128.9 32.4 %copy-start.20 = (bf16[256,384]{1,0:T(8,128)(2,1)S(1)}, bf16[256,384]{1,0:T(8,128)(2,1)}, u32[]{:S(2)}) copy-start(bf16[256,384]{1,0:T(8,128)(2,1)} %copy-done.19) | copy-start | bytes 589828
  135.3 20.7 %collective-permute-start.27 = (bf16[256,384]{1,0:T(8,128)(2,1)}, bf16[256,384]{1,0:T(8,128)(2,1)S(1)}, u32[]{:S(2)}, u32[]{:S(2)}) collective-permute-start(bf16[256,384]{1,0:T(8,128)(2,1)} %copy-done.25), channel_id=1, source_target_pairs={{0,96},{2,26},{4,100},{6,30},{8,104},{10,2},{12,108},{14,6},{16,11... | collective-permute-start | bytes 589832 | tf_op jit(solution)/shard_map/ppermute | solution.py:69
  135.9 22.7 %collective-permute-start.28 = (bf16[256,384]{1,0:T(8,128)(2,1)}, bf16[256,384]{1,0:T(8,128)(2,1)S(1)}, u32[]{:S(2)}, u32[]{:S(2)}) collective-permute-start(bf16[256,384]{1,0:T(8,128)(2,1)} %copy-done.24), channel_id=1, source_target_pairs={{0,32},{2,10},{4,36},{6,14},{8,40},{10,18},{12,44},{14,22},{16,48}... | collective-permute-start | bytes 589832 | tf_op jit(solution)/shard_map/ppermute | solution.py:69
  137.4 21.2 %collective-permute-start.29 = (bf16[256,384]{1,0:T(8,128)(2,1)}, bf16[256,384]{1,0:T(8,128)(2,1)S(1)}, u32[]{:S(2)}, u32[]{:S(2)}) collective-permute-start(bf16[256,384]{1,0:T(8,128)(2,1)} %copy-done.23), channel_id=1, source_target_pairs={{0,64},{2,18},{4,68},{6,22},{8,72},{10,26},{12,76},{14,30},{16,80}... | collective-permute-start | bytes 589832 | tf_op jit(solution)/shard_map/ppermute | solution.py:69
  138.7 12.1 %collective-permute-start.37 = (bf16[256,384]{1,0:T(8,128)(2,1)S(1)}, bf16[256,384]{1,0:T(8,128)(2,1)S(1)}, u32[]{:S(2)}, u32[]{:S(2)}) collective-permute-start(bf16[256,384]{1,0:T(8,128)(2,1)S(1)} %add_convert_fusion.refs_0_), channel_id=1, source_target_pairs={{0,96},{2,26},{4,100},{6,30},{8,104},{10,2},{12,108},{14,6},{16,11... | collective-permute-start | bytes 589832 | tf_op jit(solution)/shard_map/ppermute | solution.py:69
  141.2 10.8 %collective-permute-start.38 = (bf16[256,384]{1,0:T(8,128)(2,1)S(1)}, bf16[256,384]{1,0:T(8,128)(2,1)S(1)}, u32[]{:S(2)}, u32[]{:S(2)}) collective-permute-start(bf16[256,384]{1,0:T(8,128)(2,1)S(1)} %add_convert_fusion.refs_0_), channel_id=1, source_target_pairs={{0,64},{2,18},{4,68},{6,22},{8,72},{10,26},{12,76},{14,30},{16,80}... | collective-permute-start | bytes 589832 | tf_op jit(solution)/shard_map/ppermute | solution.py:69
  150.7 21.3 %collective-permute-start.24 = (bf16[256,384]{1,0:T(8,128)(2,1)}, bf16[256,384]{1,0:T(8,128)(2,1)S(1)}, u32[]{:S(2)}, u32[]{:S(2)}) collective-permute-start(bf16[256,384]{1,0:T(8,128)(2,1)} %copy-done.22), channel_id=1, source_target_pairs={{0,24},{2,98},{4,28},{6,102},{8,0},{10,106},{12,4},{14,110},{16,8}... | collective-permute-start | bytes 589832 | tf_op jit(solution)/shard_map/ppermute | solution.py:69
  152.0 20.0 %collective-permute-start.25 = (bf16[256,384]{1,0:T(8,128)(2,1)}, bf16[256,384]{1,0:T(8,128)(2,1)S(1)}, u32[]{:S(2)}, u32[]{:S(2)}) collective-permute-start(bf16[256,384]{1,0:T(8,128)(2,1)} %copy-done.21), channel_id=1, source_target_pairs={{0,8},{2,34},{4,12},{6,38},{8,16},{10,42},{12,20},{14,46},{16,24},... | collective-permute-start | bytes 589832 | tf_op jit(solution)/shard_map/ppermute | solution.py:69
  156.0 5.2 %collective-permute-start.42 = (bf16[192,384]{1,0:T(8,128)(2,1)S(1)}, bf16[192,384]{1,0:T(8,128)(2,1)S(1)}, u32[]{:S(2)}, u32[]{:S(2)}) collective-permute-start(bf16[192,384]{1,0:T(8,128)(2,1)S(1)} %get-tuple-element.59), channel_id=1, source_target_pairs={{0,24},{2,98},{4,28},{6,102},{8,0},{10,106},{12,4},{14,110},{16,8}... | collective-permute-start | bytes 442376 | tf_op jit(solution)/shard_map/ppermute | solution.py:69
  158.6 10.0 %collective-permute-start.43 = (bf16[192,384]{1,0:T(8,128)(2,1)S(1)}, bf16[192,384]{1,0:T(8,128)(2,1)S(1)}, u32[]{:S(2)}, u32[]{:S(2)}) collective-permute-start(bf16[192,384]{1,0:T(8,128)(2,1)S(1)} %get-tuple-element.60), channel_id=1, source_target_pairs={{0,8},{2,34},{4,12},{6,38},{8,16},{10,42},{12,20},{14,46},{16,24},... | collective-permute-start | bytes 442376 | tf_op jit(solution)/shard_map/ppermute | solution.py:69
  158.6 10.0 %collective-permute-start.44 = (bf16[192,384]{1,0:T(8,128)(2,1)S(1)}, bf16[192,384]{1,0:T(8,128)(2,1)S(1)}, u32[]{:S(2)}, u32[]{:S(2)}) collective-permute-start(bf16[192,384]{1,0:T(8,128)(2,1)S(1)} %get-tuple-element.61), channel_id=1, source_target_pairs={{0,16},{2,66},{4,20},{6,70},{8,24},{10,74},{12,28},{14,78},{16,0},... | collective-permute-start | bytes 442376 | tf_op jit(solution)/shard_map/ppermute | solution.py:69
  161.3 10.8 %collective-permute-start.26 = (bf16[256,384]{1,0:T(8,128)(2,1)S(1)}, bf16[256,384]{1,0:T(8,128)(2,1)S(1)}, u32[]{:S(2)}, u32[]{:S(2)}) collective-permute-start(bf16[256,384]{1,0:T(8,128)(2,1)S(1)} %copy-done.20), channel_id=1, source_target_pairs={{0,16},{2,66},{4,20},{6,70},{8,24},{10,74},{12,28},{14,78},{16,0},... | collective-permute-start | bytes 589832 | tf_op jit(solution)/shard_map/ppermute | solution.py:69
  168.8 5.9 %collective-permute-start.45 = (bf16[96,384]{1,0:T(8,128)(2,1)S(1)}, bf16[96,384]{1,0:T(8,128)(2,1)S(1)}, u32[]{:S(2)}, u32[]{:S(2)}) collective-permute-start(bf16[96,384]{1,0:T(8,128)(2,1)S(1)} %dynamic-slice_convert_fusion), channel_id=1, source_target_pairs={{0,1},{1,0},{2,3},{3,2},{4,5},{5,4},{6,7},{7,6},{8,9},{9,8},{10,11... | collective-permute-start | bytes 221192 | tf_op jit(solution)/shard_map/ppermute | solution.py:388
  (15 other events, 14.8 us)

commit v2 on v0

v2 whole, which is shorter than its diff:
```python
import math

import jax
import jax.numpy as jnp
import numpy as np
from jax import lax
from jax.experimental import pallas as pl
from jax.experimental.pallas import tpu as pltpu
from jax.sharding import PartitionSpec as P

HD = 128
BLK = 64
PER = 2
HEADS = 3
WIDTH = HEADS * HD
SIDE = 4
ROWS = 1024
SCALE = 1.0 / math.sqrt(HD)
LOG2E = 1.4426950408889634
SCALE2 = SCALE * LOG2E
MASKS = (0, 1, 3, 2)
SLOT_OF = {0: 0, 1: 1, 3: 2, 2: 3}
BF16 = jnp.bfloat16
F32 = jnp.float32
MIB = 1 << 20
CHUNK = 192
PADDED = 256
PAIRS = 2


def roles(ctx, core):
    z, x = divmod(ctx, SIDE)
    return (x, z) if core == 0 else (z, x)


def ctx_of(u, v, core):
    return v * SIDE + u if core == 0 else u * SIDE + v


def info_table():
    table = np.zeros((2, SIDE * SIDE, 64), np.int32)
    for core in range(2):
        for ctx in range(SIDE * SIDE):
            u, v = roles(ctx, core)
            row = table[core, ctx]
            for slot, mask in enumerate(MASKS):
                row[slot] = ctx_of(u, v ^ mask, core)
                row[52 + slot] = v ^ mask
            for owner in range(SIDE * SIDE):
                uo, vo = roles(owner, core)
                place = SLOT_OF[vo ^ v] * SIDE + SLOT_OF[uo ^ u]
                row[4 + owner] = place
                row[20 + place] = owner
                row[36 + owner] = SLOT_OF[uo ^ u] * SIDE + vo
    return table


INFO = info_table()


def send(array, role, mask, clip=0):
    pairs = []
    for ctx in range(SIDE * SIDE):
        for head in range(4):
            core = head % 2
            u, v = roles(ctx, core)
            target = ctx_of(u ^ mask, v, core) if role == "u" else ctx_of(u, v ^ mask, core)
            for dp in range(2):
                source = (ctx * 4 + head) * 2 + dp
                pairs.append((source, (target * 4 + head) * 2 + (dp ^ clip)))
    return lax.ppermute(array, ("ctx", "head", "dp"), pairs)


def gathered(array, role):
    return [array] + [send(array, role, mask) for mask in MASKS[1:]]


def scattered(parts, role):
    return parts[:1] + [send(parts[slot], role, MASKS[slot]) for slot in range(1, SIDE)]


def halved(near, away, role, first, second):
    half = near.shape[0] // 2
    come = send(away, role, first)

    on = (near[half:].astype(F32) + come[half:].astype(F32)).astype(BF16)
    return [near[:half], come[:half], send(on, role, second)], on


def summed(parts):
    total = parts[0].astype(F32)
    for part in parts[1:]:
        total = total + part.astype(F32)
    return total


def aligned(ref, mask):
    parts = []
    for mine in MASKS:
        slot = SLOT_OF[mine ^ mask]
        parts.append(ref[:, slot * 256 : (slot + 1) * 256])
    return jnp.concatenate(parts, axis=1)


def nt(a, b):
    return lax.dot_general(a, b, (((1,), (1,)), ((), ())), preferred_element_type=F32)


def nn(a, b):
    return lax.dot_general(a, b, (((1,), (0,)), ((), ())), preferred_element_type=F32)


def tn(a, b):
    return lax.dot_general(a, b, (((0,), (0,)), ((), ())), preferred_element_type=F32)


def picks(info, lists, pair, slot):
    shard = info[slot]
    starts = []
    for block in range(2):
        row = (pair // 2) * 8 + (pair % 2) * 2 + block
        local = [lists[row, shard * PER + j] - shard * SIDE for j in range(PER)]
        starts.append([pl.multiple_of(at * BLK, BLK) for at in local])
    return starts


def columns(head):
    return slice(head * HD, (head + 1) * HD)


def taken(source, starts, head):
    ref, first = source
    at = columns(head)
    rows = [
        jnp.concatenate(
            [ref[pl.ds(first + starts[block][j], BLK), at] for block in range(2)], axis=1
        )
        for j in range(PER)
    ]
    return jnp.concatenate(rows, axis=0)


def diagonal(pair_rows):
    nothing = jnp.zeros((BLK, HD), pair_rows.dtype)
    return jnp.concatenate(
        [
            jnp.concatenate([pair_rows[:BLK], nothing], axis=1),
            jnp.concatenate([nothing, pair_rows[BLK:]], axis=1),
        ],
        axis=0,
    )


def all_taken(sources, starts, head):
    return jnp.concatenate(
        [taken(sources[slot], starts[slot], head) for slot in range(SIDE)], axis=0
    )


def spread(acc, starts, head, part):
    at = columns(head)
    for slot in range(SIDE):
        for j in range(PER):
            for block in range(2):
                row = slot * HD + j * BLK
                piece = part[row : row + BLK, block * HD : (block + 1) * HD]
                acc[slot][pl.ds(starts[slot][block][j], BLK), at] += piece


def covers(lists, block):
    return [lists[(block // 4) * 8 + 4 + j, block % 4] for j in range(2)]


def cover_places(info, lists, block):
    return [info[4 + owner] for owner in covers(lists, block)]


def pack_kernel(queries, grads, cond, kv_list, cover_lists, out, row, lists):
    lists[...] = jnp.zeros_like(lists)
    lists[0:4, 0:32] = kv_list[...].astype(F32)
    lists[4:6, 0:4] = cover_lists[...].astype(F32)
    row[0:BLK, :] = cond[...]
    row[BLK : BLK + 16, :] = lists[...].astype(BF16)
    out[0:256, :] = queries[...]
    out[256:512, :] = grads[...]
    out[512:592, :] = row[...]


def stack_kernel(upper, lower, _, out):
    half = upper.shape[0]
    out[0:half, :] = upper[...]
    out[half:, :] = lower[...]


def token_kernel(info, tokens, *refs):
    out, held, padded, sem = refs[0:4], refs[4], refs[5], refs[6]
    copy = pltpu.make_async_copy(tokens, held, sem)
    copy.start()
    copy.wait()
    for n in range(16):
        padded[:, n * PADDED : n * PADDED + CHUNK] = held[:, n * CHUNK : (n + 1) * CHUNK]
    for sv in range(SIDE):
        for su in range(SIDE):
            start = pl.multiple_of(info[20 + sv * SIDE + su] * PADDED, PADDED)
            columns_here = padded[:, pl.ds(start, PADDED)]
            row = (su // 2) * BLK
            at = (su % 2) * CHUNK
            out[sv][row : row + BLK, at : at + CHUNK] = columns_here[:, 0:CHUNK]


def join_kernel(*refs):
    parts, tokens, out, lists = refs[0:4], refs[4:8], refs[8:12], refs[12]
    for slot in range(SIDE):
        first = parts[slot].shape[0] - BLK - 16
        rows = parts[slot][first + BLK : first + BLK + 16, 0:HD].astype(F32)
        lists[slot * 8 : (slot + 1) * 8, :] = rows[0:8, :].astype(jnp.int32)
        for other in range(SIDE):
            out[other][slot * BLK : (slot + 1) * BLK, :] = parts[slot][first : first + BLK, :]
        out[slot][256:384, :] = tokens[slot][...]


def sum_kernel(*refs):
    total = refs[0][...].astype(F32)
    for part in refs[1:4]:
        total = total + part[...].astype(F32)
    refs[-1][...] = total.astype(refs[-1].dtype)


def split_kernel(clip, *refs):
    mine, other, total = refs[-3:]
    total[...] = refs[0][...].astype(F32)
    for part in refs[1:4]:
        total[...] += part[...].astype(F32)
    mine[...] = total[pl.ds(pl.multiple_of(clip[0] * 96, 96), 96), :]
    other[...] = total[pl.ds(pl.multiple_of(96 - clip[0] * 96, 96), 96), :].astype(BF16)


def slope_kernel(info, lists, *refs):
    qg, kv, slope_out, grad_out = refs[0:4], refs[4:8], refs[8], refs[9]
    grads = refs[10]
    step = pl.program_id(0)
    values = [(ref, 256) for ref in kv]

    @pl.when(step == 0)
    def _():
        for slot in range(SIDE):
            grads[slot * 256 : (slot + 1) * 256, :] = qg[slot][256:512, :]

    for n in range(PAIRS):
        pair = step * PAIRS + n
        rows = pl.ds(pl.multiple_of(pair * HD, HD), HD)
        grad = grads[rows, :]
        grad_out[n * HD : (n + 1) * HD, :] = grad
        starts = [picks(info, lists, pair, slot) for slot in range(SIDE)]
        for head in range(HEADS):
            slope_out[n, head] = nt(
                all_taken(values, starts, head), diagonal(grad[:, columns(head)])
            )


def score_kernel(info, lists, *refs):
    qg, kv, conds, slope = refs[0:4], refs[4:8], refs[8:12], refs[12]
    qeff, stat, probs_out, tokens = refs[13:17]
    queries, cond, sems = refs[17:]
    step = pl.program_id(0)
    copies = []
    for slot in range(SIDE):
        for half in range(2):
            source = conds[slot].at[256 + half * BLK : 256 + (half + 1) * BLK, :]
            to = tokens.at[half, slot * BLK : (slot + 1) * BLK, :]
            copies.append(pltpu.make_async_copy(source, to, sems.at[2 * slot + half]))
    keys = [(ref, 0) for ref in kv]

    @pl.when(step == 0)
    def _():
        for copy in copies:
            copy.start()
        for slot in range(SIDE):
            at = slice(slot * 256, (slot + 1) * 256)
            queries[at, :] = qg[slot][0:256, :]
            cond[at, :] = conds[slot][0:256, :]

    for n in range(PAIRS):
        pair = step * PAIRS + n
        rows = pl.ds(pl.multiple_of(pair * HD, HD), HD)
        here = slice(n * HD, (n + 1) * HD)
        lifted = []
        for block in range(2):
            places = cover_places(info, lists, 2 * pair + block)
            parts = [
                cond[pl.ds(pl.multiple_of(at * BLK, BLK), BLK), :].astype(F32) for at in places
            ]
            lifted.append(parts[0] + parts[1])
        query = (queries[rows, :].astype(F32) + jnp.concatenate(lifted, axis=0)).astype(BF16)
        qeff[here, :] = query
        starts = [picks(info, lists, pair, slot) for slot in range(SIDE)]
        tops, totals, weighted = [], [], []
        for head in range(HEADS):
            scores = nt(all_taken(keys, starts, head), diagonal(query[:, columns(head)]))
            top = jnp.max(scores, axis=0, keepdims=True)
            probs = jnp.exp2((scores - top) * SCALE2)
            tops.append(top)
            totals.append(jnp.sum(probs, axis=0, keepdims=True))
            weighted.append(jnp.sum(probs * slope[n, head], axis=0, keepdims=True))
            probs_out[n, head] = probs.astype(BF16)
        nothing = [jnp.zeros((16 - 3 * HEADS, HD), F32)]
        stat[:, here] = jnp.concatenate(tops + totals + weighted + nothing, axis=0)

    @pl.when(step == 8 // PAIRS - 1)
    def _():
        for copy in copies:
            copy.wait()


def turn_kernel(*refs):
    kv, low, high = refs[0:4], refs[5], refs[6]
    left = lax.broadcasted_iota(jnp.int32, (HD, HD), 1) < BLK

    def turn(head, carry):
        at = pl.ds(pl.multiple_of(head * HD, HD), HD)
        for slot in range(SIDE):
            for half in range(2):
                tile = kv[slot][half * HD : (half + 1) * HD, at].astype(F32).T
                rolled = pltpu.roll(tile, BLK, 1)
                block = slot * SIDE + 2 * half
                low[block, at, :] = jnp.where(left, tile, 0.0).astype(BF16)
                high[block, at, :] = jnp.where(left, 0.0, rolled).astype(BF16)
                low[block + 1, at, :] = jnp.where(left, rolled, 0.0).astype(BF16)
                high[block + 1, at, :] = jnp.where(left, 0.0, tile).astype(BF16)
        return carry

    lax.fori_loop(0, HEADS, turn, 0)


def query_kernel(info, lists, *refs):
    stats, probs_in, slope_in = refs[0:4], refs[4], refs[5]
    low, high = refs[6], refs[7]
    cg, dq, probs_out, score_out = refs[8:12], refs[12:14], refs[14], refs[15]
    factors, deltas, cond, qbuf = refs[16:]
    step = pl.program_id(0)

    @pl.when(step == 0)
    def _():
        stat = [stats[0][...]] + [aligned(stats[slot], MASKS[slot]) for slot in range(1, SIDE)]
        tops = [s[0:HEADS] for s in stat]
        top = jnp.maximum(jnp.maximum(tops[0], tops[1]), jnp.maximum(tops[2], tops[3]))
        total = jnp.zeros_like(top)
        weighted = jnp.zeros_like(top)
        for s, t in zip(stat, tops):
            share = jnp.exp2((t - top) * SCALE2)
            total = total + s[HEADS : 2 * HEADS] * share
            weighted = weighted + s[2 * HEADS : 3 * HEADS] * share
        factors[0:HEADS, :] = jnp.exp2((tops[0] - top) * SCALE2) / total
        deltas[0:HEADS, :] = weighted / total
        cond[...] = jnp.zeros_like(cond)

    left = lax.broadcasted_iota(jnp.int32, (HD, HD), 1) < BLK
    for n in range(PAIRS):
        pair = step * PAIRS + n
        rows = pl.ds(pl.multiple_of(pair * HD, HD), HD)
        starts = [picks(info, lists, pair, slot) for slot in range(SIDE)]
        parts = []
        for head in range(HEADS):
            at = columns(head)
            factor, delta = factors[head : head + 1, rows], deltas[head : head + 1, rows]
            probs = probs_in[n, head].astype(F32) * factor
            score = (probs * (slope_in[n, head] - delta) * SCALE).astype(BF16)
            probs_out[n, head] = probs.astype(BF16)
            score_out[n, head] = score
            keys = []
            for block in range(2):
                across = []
                for slot in range(SIDE):
                    one = [slot * SIDE + (starts[slot][block][j] >> 6) for j in range(PER)]
                    across.append(low[one[0], at, :] + high[one[1], at, :])
                keys.append(jnp.concatenate(across, axis=1))
            turned = nn(jnp.concatenate(keys, axis=0), score)
            parts.append(jnp.where(left, turned[:HD], turned[HD:]).T)
        query_part = jnp.concatenate(parts, axis=1)
        qbuf[rows, :] = query_part.astype(BF16)
        for block in range(2):
            for owner in covers(lists, 2 * pair + block):
                to = info[36 + owner]
                cond[pl.ds(pl.multiple_of(to * BLK, BLK), BLK), :] += query_part[
                    block * BLK : (block + 1) * BLK
                ]

    @pl.when(step == 8 // PAIRS - 1)
    def _():
        for slot in range(SIDE):
            at = slice(slot * 256, (slot + 1) * 256)
            cg[slot][...] = cond[at, :].astype(BF16)
            dq[slot // 2][(slot % 2) * 256 : (slot % 2 + 1) * 256, :] = qbuf[at, :]


def key_kernel(info, lists, probs_in, score_in, qeff, grads, *refs):
    dkv, flag, dk, dv = refs[0:2], refs[2], refs[3:7], refs[7:11]
    step = pl.program_id(0)

    @pl.when(step == 0)
    def _():
        flag[...] = jnp.zeros_like(flag)
        for one in dk + dv:
            one[...] = jnp.zeros_like(one)

    for n in range(PAIRS):
        pair = step * PAIRS + n
        here = slice(n * HD, (n + 1) * HD)
        starts = [picks(info, lists, pair, slot) for slot in range(SIDE)]
        for head in range(HEADS):
            at = columns(head)
            spread(dk, starts, head, nn(score_in[n, head], diagonal(qeff[here, at])))
            spread(dv, starts, head, nn(probs_in[n, head], diagonal(grads[here, at])))

    @pl.when(step == 8 // PAIRS - 1)
    def _():
        for slot in range(SIDE):
            half = (slot // 2) * 512
            dkv[slot % 2][half : half + 256, :] = dk[slot][...].astype(BF16)
            dkv[slot % 2][half + 256 : half + 512, :] = dv[slot][...].astype(BF16)


def weight_kernel(info, *refs):
    cond, tokens, out = refs[0], refs[1], refs[2:6]
    whole, stacked, sem = refs[6:]
    copy = pltpu.make_async_copy(tokens, stacked, sem)
    copy.start()
    rows = []
    for slot in range(SIDE):
        rows.append(cond[pl.ds(pl.multiple_of(info[52 + slot] * BLK, BLK), BLK), :])
    half_sums = jnp.concatenate(rows, axis=0)
    copy.wait()
    for half in range(2):
        whole[...] = tn(stacked[half], half_sums)
        for n in range(2):
            out[2 * half + n][...] = whole[n * CHUNK : (n + 1) * CHUNK, :].astype(BF16)


VMEM = pl.BlockSpec(memory_space=pltpu.VMEM)
SMEM = pl.BlockSpec(memory_space=pltpu.SMEM)
ANY = pl.BlockSpec(memory_space=pl.ANY)
HBM = pl.BlockSpec(memory_space=pltpu.HBM)
TILES = pl.BlockSpec((PAIRS, HEADS, 512, HD), lambda i: (i, 0, 0, 0))
LINES = pl.BlockSpec((PAIRS * HD, WIDTH), lambda i: (i, 0))
STATS = pl.BlockSpec((16, PAIRS * HD), lambda i: (0, i))


def call(kernel, name, operands, in_specs, outs, out_specs, scratch, limit, grid=(), cost=1, alias=None):
    results = pl.pallas_call(
        kernel,
        name=name,
        grid=grid,
        out_shape=[jax.ShapeDtypeStruct(shape, dtype) for shape, dtype in outs],
        in_specs=in_specs,
        out_specs=out_specs,
        scratch_shapes=[
            one if not isinstance(one, tuple) else pltpu.VMEM(*one) for one in scratch
        ],
        compiler_params=pltpu.CompilerParams(vmem_limit_bytes=limit * MIB),
        input_output_aliases=alias or {},
        cost_estimate=pl.CostEstimate(
            flops=int(cost * FLOPS), bytes_accessed=0, transcendentals=0
        ),
    )(*operands)
    return list(results)


FLOPS = 1.15e9
GRID = (8 // PAIRS,)
SHARD = ((256, WIDTH), BF16)
WHOLE = ((ROWS, WIDTH), BF16)
PROBS = ((8, HEADS, 512, HD), BF16)
SLOPE = ((8, HEADS, 512, HD), F32)


def pack_call(queries, grads, cond, kv_list, cover_lists):
    return call(
        pack_kernel,
        "pack",
        [queries, grads, cond, kv_list, cover_lists],
        [VMEM] * 5,
        [((592, WIDTH), BF16), ((BLK + 16, WIDTH), BF16)],
        [VMEM] * 2,
        [((16, WIDTH), F32)],
        4,
    )


def stack_call(upper, lower, after):
    return call(
        stack_kernel,
        "stack",
        [upper, lower, after],
        [VMEM] * 2 + [ANY],
        [((512, WIDTH), BF16)],
        [VMEM],
        [],
        2,
    )[0]


def token_call(info, tokens):
    return call(
        token_kernel,
        "tokens",
        [info, tokens],
        [SMEM, HBM],
        [((128, WIDTH), BF16)] * 4,
        [VMEM] * 4,
        [((BLK, 16 * CHUNK), BF16), ((BLK, 16 * PADDED), BF16), pltpu.SemaphoreType.DMA],
        4,
    )


def join_call(parts, tokens):
    return call(
        join_kernel,
        "join",
        parts + tokens,
        [VMEM] * 8,
        [((384, WIDTH), BF16)] * 4 + [((32, HD), jnp.int32)],
        [VMEM] * 5,
        [],
        4,
    )


def tie_kernel(*refs):
    pass


def tied(arrays, after):
    count = len(arrays)
    return call(
        tie_kernel,
        "tie",
        arrays + after,
        [ANY] * count + [VMEM] * len(after),
        [(one.shape, one.dtype) for one in arrays],
        [ANY] * count,
        [],
        4,
        (),
        0.1,
        {n: n for n in range(count)},
    )


def sum_call(parts, after):
    return call(
        sum_kernel,
        "sum",
        parts + after,
        [VMEM] * (4 + len(after)),
        [(parts[0].shape, BF16)],
        [VMEM],
        [],
        4,
    )[0]


def split_call(clip, parts, after):
    return call(
        split_kernel,
        "split",
        [clip] + parts + after,
        [SMEM] + [VMEM] * (4 + len(after)),
        [((96, WIDTH), F32), ((96, WIDTH), BF16)],
        [VMEM] * 2,
        [((CHUNK, WIDTH), F32)],
        4,
    )


def slope_call(info, lists, qg, kv):
    return call(
        slope_kernel,
        "slopes",
        [info, lists] + qg + kv,
        [SMEM] * 2 + [VMEM] * 8,
        [SLOPE, WHOLE],
        [TILES, LINES],
        [WHOLE],
        12,
        GRID,
        4,
    )


def scores_call(info, lists, qg, kv, conds, slope):
    return call(
        score_kernel,
        "scores",
        [info, lists] + qg + kv + conds + [slope],
        [SMEM] * 2 + [VMEM] * 12 + [TILES],
        [WHOLE, ((16, ROWS), F32), PROBS, ((2, 256, WIDTH), BF16)],
        [LINES, STATS, TILES, HBM],
        [WHOLE] * 2 + [pltpu.SemaphoreType.DMA((8,))],
        14,
        GRID,
        5,
    )


def turn_call(kv, after):
    return call(
        turn_kernel,
        "turn",
        kv + after,
        [VMEM] * 5,
        [((16, WIDTH, HD), BF16)] * 2,
        [VMEM] * 2,
        [],
        4,
        (),
        1.2,
    )


def query_call(info, lists, stats, probs, slope, low, high):
    return call(
        query_kernel,
        "query_grads",
        [info, lists] + stats + [probs, slope, low, high],
        [SMEM] * 2 + [VMEM] * 4 + [TILES] * 2 + [VMEM] * 2,
        [SHARD] * 4 + [((512, WIDTH), BF16)] * 2 + [PROBS] * 2,
        [VMEM] * 6 + [TILES] * 2,
        [((8, ROWS), F32)] * 2 + [((ROWS, WIDTH), F32), WHOLE],
        14,
        GRID,
        4.5,
    )


def key_call(info, lists, probs, score, qeff, grads):
    return call(
        key_kernel,
        "key_grads",
        [info, lists, probs, score, qeff, grads],
        [SMEM] * 2 + [TILES] * 2 + [LINES] * 2,
        [WHOLE] * 2 + [((8, HD), F32)],
        [VMEM] * 3,
        [((256, WIDTH), F32)] * 8,
        12,
        GRID,
        5,
    )


def weight_call(info, cond, tokens):
    return call(
        weight_kernel,
        "weights",
        [info, cond, tokens],
        [SMEM, VMEM, HBM],
        [((CHUNK, WIDTH), BF16)] * 4,
        [VMEM] * 4,
        [
            ((2 * CHUNK, WIDTH), F32),
            ((2, 256, 2 * CHUNK), BF16),
            pltpu.SemaphoreType.DMA,
        ],
        8,
        (),
        1,
    )


def body(queries, keys, values, grad_out, kv_list, cover_lists, cond_tokens, cond_weight):
    ctx = lax.axis_index("ctx")
    core = lax.axis_index("head") % 2
    info = lax.dynamic_slice(jnp.asarray(INFO), (core, ctx, 0), (1, 1, 64)).reshape(64)
    cond = jnp.dot(cond_tokens[0], cond_weight, preferred_element_type=F32).astype(BF16)
    kv = stack_call(keys[0], values[0], keys[0])
    qg, row = pack_call(queries[0], grad_out[0], cond, kv_list, cover_lists.T)
    qg1, qg3, row2 = send(qg, "u", 1), send(qg, "u", 3), send(row, "u", 2)
    kv3, kv1 = send(kv, "v", 3), send(kv, "v", 1)
    qg1, kv3 = tied([qg1, kv3], [row2, qg3, kv1])
    out = join_call([qg, qg1, qg3, row2], token_call(info, cond_tokens[0]))
    conds, lists = scattered(out[0:4], "v"), out[4]
    qg = [qg, qg1, qg3, send(qg1, "u", 3)]
    kv = [kv, kv1, kv3, send(kv3, "v", 1)]
    slope, grads = slope_call(info, lists, qg, kv)
    qeff, stat, probs, tokens = scores_call(info, lists, qg, kv, conds, slope)
    stats = gathered(stat, "u")
    low, high = turn_call(kv, [stat])
    out = query_call(info, lists, stats, probs, slope, low, high)
    cg, dq, probs, score = out[0:4], out[4:6], out[6], out[7]
    cg = scattered(cg, "u")
    dkv = key_call(info, lists, probs, score, qeff, grads)
    cg = gathered(sum_call(cg, [dkv[2]]), "v")
    cg = sum_call(cg, [])
    away, = tied([dkv[1]], [cg])
    dkv, on = halved(dkv[0], away, "v", 1, 3)
    dq, dq_on = halved(dq[0], dq[1], "u", 3, 1)
    weight = scattered(weight_call(info, cg, tokens), "u")
    mine, other = split_call(lax.axis_index("dp").reshape(1), weight, [on, dq_on])
    grad_cond_weight = mine + lax.ppermute(other, "dp", [(0, 1), (1, 0)]).astype(F32)
    grad_query = summed(dq).astype(BF16)[None]
    grad_key = summed([part[:256] for part in dkv]).astype(BF16)[None]
    grad_value = summed([part[256:] for part in dkv]).astype(BF16)[None]
    return (grad_query, grad_key, grad_value, grad_cond_weight)


def solution(mesh):
    return jax.shard_map(
        body,
        mesh=mesh,
        in_specs=(
            P("dp", "ctx", "head"),
            P("dp", "ctx", "head"),
            P("dp", "ctx", "head"),
            P("dp", "ctx", "head"),
            P("ctx", None),
            P("ctx", None),
            P("dp", "ctx", None),
            P(None, "head"),
        ),
        out_specs=(
            P("dp", "ctx", "head"),
            P("dp", "ctx", "head"),
            P("dp", "ctx", "head"),
            P(("ctx", "dp"), "head"),
        ),
        check_vma=False,
    )
```

time: 1320 us -> 113 us (0.09)
  waiting for transfers between devices: 689 us -> 25.4 us
  local copies, waits for them, and re-layouts: 344 us -> 7.73 us
  matrix products: 130 us -> 1.44 us
  other arithmetic: 105 us -> 6.34 us
  starting transfers between devices: 1.52 us -> 44.8 us
  blocking collectives: 25.9 us -> 0 us
  Pallas kernels: 0 us -> 25.4 us
  between operations: 14.2 us -> 0.98 us
    ppermute x48 -> x27, waiting for transfers between devices: 399 us -> 25.4 us  [the longest x26 24.4 us: send(): return lax.ppermute(array, ('ctx', 'head', 'dp'), pairs)]
    unnamed x3 -> x0, waiting for transfers between devices: 221 us -> none
    reshape x81 -> x1, local copies, waits for them, and re-layouts: 163 us -> 0.69 us  [body(): lax.dynamic_slice(jnp.asarray(INFO), (core, ctx, 0), (1, 1, 64)).reshape(64)]
    dot_general x132 -> x1, matrix products: 130 us -> 1.44 us  [body(): jnp.dot(cond_tokens[0], cond_weight, preferred_element_type=F32)]
    reduce_scatter x1 -> x0, waiting for transfers between devices: 69.3 us -> none  [body(): lax.psum_scatter(term_rows.reshape(BLK * lax.axis_size('ctx'), feature_wi...]
    while x433 -> x0, local copies, waits for them, and re-layouts: 68.4 us -> none
    select_n x64 -> x0, other arithmetic: 43.4 us -> none  [picked_blocks(): picked = jnp.take(blocks, chosen.reshape(-1), axis=0)]
    ppermute x48 -> x27, starting transfers between devices: 1.44 us -> 44.8 us  [the longest x26 41.5 us: send(): return lax.ppermute(array, ('ctx', 'head', 'dp'), pairs)]
  transfers between devices with their start and end apart: 50 -> 27, of which waited for: 34 -> 13; matrix products, arithmetic and copies ran while one was open for 13% -> 5% of each run, Pallas kernels for 0% -> 12%
where the time goes in v2:
time: 113 us; the launch traced here: 112 us
  starting transfers between devices  44.8 us (40%)
  Pallas kernels  25.4 us (22%)
  waiting for transfers between devices  25.4 us (22%)
  local copies, waits for them, and re-layouts  7.73 us (7%)
  other arithmetic  6.34 us (6%)
  matrix products  1.44 us (1%)
    ppermute x26, starting transfers between devices, send(): return lax.ppermute(array, ('ctx', 'head', 'dp'), pairs)  41.5 us
    pallas_call x15, Pallas kernels, call(): pl.pallas_call(kernel, name=name, grid=grid, out_shape=[jax.ShapeDtypeStr...  25.4 us
    ppermute x26, waiting for transfers between devices, send(): return lax.ppermute(array, ('ctx', 'head', 'dp'), pairs)  24.4 us
    unnamed x40, local copies, waits for them, and re-layouts  7.04 us
    ppermute x1, starting transfers between devices, body(): lax.ppermute(other, 'dp', [(0, 1), (1, 0)]).astype(F32)  3.28 us
  transfers between devices with their start and end apart: 27, of which 13 were waited for; matrix products, arithmetic and copies ran while one was open for 5% of the time, Pallas kernels for 12%

profile of v2, /device:TPU:0, one launch (start us, length us, event | category | flops | bytes accessed | tf_op | source)
XLA Modules:
  0.0 112.1 jit_solution(14211989632497360328)
XLA Ops:
  0.7 1.6 %copy-done = bf16[3072,384]{1,0:T(8,128)(2,1)S(1)} copy-done((bf16[3072,384]{1,0:T(8,128)(2,1)S(1)}, bf16[3072,384]{1,0:T(8,128)(2,1)}, u32[]{:S(2)}) %copy-start) | copy-done | bytes 2359320
  2.3 1.4 %convolution_convert_fusion.cond = bf16[64,384]{1,0:T(8,128)(2,1)S(1)} fusion(bf16[3072,384]{1,0:T(8,128)(2,1)S(1)} %copy-done, bf16[1,64,3072]{2,1,0:T(8,128)(2,1)} %param.15), kind=kOutput, calls=%fused_computation | convolution fusion | flops 151019520 | bytes 2801664 | tf_op jit(solution)/shard_map/dot_general | solution.py:673
  3.9 2.9 %collective-permute-start.3 = (bf16[592,384]{1,0:T(8,128)(2,1)S(1)}, bf16[592,384]{1,0:T(8,128)(2,1)S(1)}, u32[]{:S(2)}, u32[]{:S(2)}) collective-permute-start(bf16[592,384]{1,0:T(8,128)(2,1)S(1)} %get-tuple-element.42.refs_0_), channel_id=1, source_target_pairs={{0,24},{1,25},{2,98},{3,99},{4,28},{5,29},{6,102},{7,103},{8,16},{... | collective-permute-start | bytes 1363976 | tf_op jit(solution)/shard_map/ppermute | solution.py:71
  6.8 0.2 collective-permute-start
  7.1 2.0 %collective-permute-start.4 = (bf16[512,384]{1,0:T(8,128)(2,1)S(1)}, bf16[512,384]{1,0:T(8,128)(2,1)S(1)}, u32[]{:S(2)}, u32[]{:S(2)}) collective-permute-start(bf16[512,384]{1,0:T(8,128)(2,1)S(1)} %stack.1.refs_4_.refs_0_), channel_id=1, source_target_pairs={{0,32},{1,33},{2,10},{3,11},{4,36},{5,37},{6,14},{7,15},{8,40},{9,... | collective-permute-start | bytes 1179656 | tf_op jit(solution)/shard_map/ppermute | solution.py:71
  9.1 2.5 %collective-permute-start.1 = (bf16[512,384]{1,0:T(8,128)(2,1)S(1)}, bf16[512,384]{1,0:T(8,128)(2,1)}, u32[]{:S(2)}, u32[]{:S(2)}) collective-permute-start(bf16[512,384]{1,0:T(8,128)(2,1)S(1)} %stack.1.refs_4_.refs_0_), channel_id=1, source_target_pairs={{0,96},{1,97},{2,26},{3,27},{4,100},{5,101},{6,30},{7,31},{8,104},... | collective-permute-start | bytes 1179656 | tf_op jit(solution)/shard_map/ppermute | solution.py:71
  11.6 0.7 copy-done.10
  12.3 1.7 %collective-permute-start.2 = (bf16[80,384]{1,0:T(8,128)(2,1)S(1)}, bf16[80,384]{1,0:T(8,128)(2,1)S(1)}, u32[]{:S(2)}, u32[]{:S(2)}) collective-permute-start(bf16[80,384]{1,0:T(8,128)(2,1)S(1)} %get-tuple-element.43), channel_id=1, source_target_pairs={{0,16},{1,17},{2,66},{3,67},{4,20},{5,21},{6,70},{7,71},{8,24},{9,... | collective-permute-start | bytes 184328 | tf_op jit(solution)/shard_map/ppermute | solution.py:71
  14.1 4.8 %collective-permute-done.2.refs_2_.refs_3_ = bf16[80,384]{1,0:T(8,128)(2,1)S(1)} collective-permute-done((bf16[80,384]{1,0:T(8,128)(2,1)S(1)}, bf16[80,384]{1,0:T(8,128)(2,1)S(1)}, u32[]{:S(2)}, u32[]{:S(2)}) %collective-permute-start.2) | collective-permute-done | bytes 61472 | tf_op jit(solution)/shard_map/ppermute | solution.py:71
  18.8 0.2 collective-permute-done.4.refs_4_.refs_5_.refs_1_
  19.1 0.4 collective-permute-done.refs_0_
  19.5 0.4 copy-done.3
  19.8 3.7 %collective-permute-start.5 = (bf16[592,384]{1,0:T(8,128)(2,1)S(1)}, bf16[592,384]{1,0:T(8,128)(2,1)}, u32[]{:S(2)}, u32[]{:S(2)}) collective-permute-start(bf16[592,384]{1,0:T(8,128)(2,1)S(1)} %get-tuple-element.44.refs_1_), channel_id=1, source_target_pairs={{0,24},{1,25},{2,98},{3,99},{4,28},{5,29},{6,102},{7,103},{8,16},{... | collective-permute-start | bytes 1363976 | tf_op jit(solution)/shard_map/ppermute | solution.py:71
  23.5 1.7 %collective-permute-start.6 = (bf16[512,384]{1,0:T(8,128)(2,1)}, bf16[512,384]{1,0:T(8,128)(2,1)}, u32[]{:S(2)}, u32[]{:S(2)}) collective-permute-start(bf16[512,384]{1,0:T(8,128)(2,1)} %get-tuple-element.50.refs_6_.refs_2_), channel_id=1, source_target_pairs={{0,32},{1,33},{2,10},{3,11},{4,36},{5,37},{6,14},{7,15},{8,40},{9,... | collective-permute-start | bytes 1179656 | tf_op jit(solution)/shard_map/ppermute | solution.py:71
  25.3 0.7 dynamic-slice_bitcast_fusion.info
  26.0 1.0 copy-done.5
  27.0 1.0 tokens.1
  28.0 0.1 join.1
  28.1 0.4 collective-permute-start.7
  28.5 1.9 %collective-permute-start.8 = (bf16[384,384]{1,0:T(8,128)(2,1)S(1)}, bf16[384,384]{1,0:T(8,128)(2,1)S(1)}, u32[]{:S(2)}, u32[]{:S(2)}) collective-permute-start(bf16[384,384]{1,0:T(8,128)(2,1)S(1)} %get-tuple-element.53), channel_id=1, source_target_pairs={{0,96},{1,97},{2,26},{3,27},{4,100},{5,101},{6,30},{7,31},{8,104},... | collective-permute-start | bytes 884744 | tf_op jit(solution)/shard_map/ppermute | solution.py:71
  30.4 1.9 %collective-permute-start.9 = (bf16[384,384]{1,0:T(8,128)(2,1)S(1)}, bf16[384,384]{1,0:T(8,128)(2,1)S(1)}, u32[]{:S(2)}, u32[]{:S(2)}) collective-permute-start(bf16[384,384]{1,0:T(8,128)(2,1)S(1)} %get-tuple-element.54), channel_id=1, source_target_pairs={{0,64},{1,65},{2,18},{3,19},{4,68},{5,69},{6,22},{7,23},{8,72},{9,... | collective-permute-start | bytes 884744 | tf_op jit(solution)/shard_map/ppermute | solution.py:71
  32.3 3.8 %slopes.1 = (f32[8,3,512,128]{3,2,1,0:T(8,128)S(1)}, bf16[1024,384]{1,0:T(8,128)(2,1)S(1)}) custom-call(s32[64]{0:T(128)S(1)} %dynamic-slice_bitcast_fusion.info, s32[32,128]{1,0:T(8,128)S(1)} %get-tuple-element.49.lists, bf16[592,384]{1,0:T(8,128)(2,1)S(1)} %copy-done.9, bf16[592,384]{1,0:T(8,128)(2,1)S(1)} %get-tuple-element.44.refs_1_, ...), custom_call_target="tpu_custom_call" | custom-call | flops 4600000000 | tf_op jit(solution)/shard_map/slopes/pallas_call | solution.py:449
  36.1 3.5 %collective-permute-done.8.refs_10_ = bf16[384,384]{1,0:T(8,128)(2,1)S(1)} collective-permute-done((bf16[384,384]{1,0:T(8,128)(2,1)S(1)}, bf16[384,384]{1,0:T(8,128)(2,1)S(1)}, u32[]{:S(2)}, u32[]{:S(2)}) %collective-permute-start.8) | collective-permute-done | bytes 294944 | tf_op jit(solution)/shard_map/ppermute | solution.py:71
  39.6 6.0 %scores.1 = (bf16[1024,384]{1,0:T(8,128)(2,1)S(1)}, f32[16,1024]{1,0:T(8,128)S(1)}, bf16[8,3,512,128]{3,2,1,0:T(8,128)(2,1)S(1)}, bf16[2,256,384]{2,1,0:T(8,128)(2,1)S(1)}) custom-call(s32[64]{0:T(128)S(1)} %dynamic-slice_bitcast_fusion.info, s32[32,128]{1,0:T(8,128)S(1)} %get-tuple-element.49.lists, bf16[592,384]{1,0:T(8,128)(2,1)S(1)} %copy-done.9, ...), custom_call_target="tpu_custom_call" | custom-call | flops 5750000128 | tf_op jit(solution)/shard_map/scores/pallas_call | solution.py:449
  45.6 0.8 copy-done.18
  46.4 0.7 collective-permute-start.12
  47.1 1.3 %collective-permute-start.11 = (f32[16,1024]{1,0:T(8,128)S(1)}, f32[16,1024]{1,0:T(8,128)S(1)}, u32[]{:S(2)}, u32[]{:S(2)}) collective-permute-start(f32[16,1024]{1,0:T(8,128)S(1)} %get-tuple-element.56.refs_4_.refs_0_), channel_id=1, source_target_pairs={{0,24},{1,25},{2,98},{3,99},{4,28},{5,29},{6,102},{7,103},{8,16},{... | collective-permute-start | bytes 196616 | tf_op jit(solution)/shard_map/ppermute | solution.py:71
  48.3 1.6 %collective-permute-start.10 = (f32[16,1024]{1,0:T(8,128)S(1)}, f32[16,1024]{1,0:T(8,128)S(1)}, u32[]{:S(2)}, u32[]{:S(2)}) collective-permute-start(f32[16,1024]{1,0:T(8,128)S(1)} %get-tuple-element.56.refs_4_.refs_0_), channel_id=1, source_target_pairs={{0,8},{1,9},{2,34},{3,35},{4,12},{5,13},{6,38},{7,39},{8,0},{9,1},... | collective-permute-start | bytes 196616 | tf_op jit(solution)/shard_map/ppermute | solution.py:71
  49.9 2.2 %turn.1 = (bf16[16,384,128]{2,1,0:T(8,128)(2,1)S(1)}, bf16[16,384,128]{2,1,0:T(8,128)(2,1)S(1)}) custom-call(bf16[512,384]{1,0:T(8,128)(2,1)S(1)} %copy-done.11, bf16[512,384]{1,0:T(8,128)(2,1)S(1)} %copy-done.4, bf16[512,384]{1,0:T(8,128)(2,1)} %get-tuple-element.50.refs_6_.refs_2_, bf16[512,384]{1,0:T(8,128)(2,1)} %collective-permute-done.6.refs_7_.refs_3_, ...), custom_call_target="tpu_custom_call" | custom-call | flops 1380000000 | tf_op jit(solution)/shard_map/turn/pallas_call | solution.py:449
  52.1 0.1 collective-permute-done.12.refs_3_
  52.2 0.7 collective-permute-done.11.refs_2_
  52.9 5.4 %query_grads.1 = (bf16[256,384]{1,0:T(8,128)(2,1)S(1)}, bf16[256,384]{1,0:T(8,128)(2,1)S(1)}, bf16[256,384]{1,0:T(8,128)(2,1)S(1)}, bf16[256,384]{1,0:T(8,128)(2...) custom-call(s32[64]{0:T(128)S(1)} %dynamic-slice_bitcast_fusion.info, ...), custom_call_target="tpu_custom_call" | custom-call | flops 5175000064 | tf_op jit(solution)/shard_map/query_grads/pallas_call | solution.py:449
  58.3 1.3 %collective-permute-start.15 = (bf16[256,384]{1,0:T(8,128)(2,1)S(1)}, bf16[256,384]{1,0:T(8,128)(2,1)S(1)}, u32[]{:S(2)}, u32[]{:S(2)}) collective-permute-start(bf16[256,384]{1,0:T(8,128)(2,1)S(1)} %get-tuple-element.69), channel_id=1, source_target_pairs={{0,8},{1,9},{2,34},{3,35},{4,12},{5,13},{6,38},{7,39},{8,0},{9,1},... | collective-permute-start | bytes 589832 | tf_op jit(solution)/shard_map/ppermute | solution.py:71
  59.5 1.6 %collective-permute-start.16 = (bf16[256,384]{1,0:T(8,128)(2,1)S(1)}, bf16[256,384]{1,0:T(8,128)(2,1)S(1)}, u32[]{:S(2)}, u32[]{:S(2)}) collective-permute-start(bf16[256,384]{1,0:T(8,128)(2,1)S(1)} %get-tuple-element.70), channel_id=1, source_target_pairs={{0,24},{1,25},{2,98},{3,99},{4,28},{5,29},{6,102},{7,103},{8,16},{... | collective-permute-start | bytes 589832 | tf_op jit(solution)/shard_map/ppermute | solution.py:71
  61.2 1.2 %collective-permute-start.17 = (bf16[256,384]{1,0:T(8,128)(2,1)S(1)}, bf16[256,384]{1,0:T(8,128)(2,1)S(1)}, u32[]{:S(2)}, u32[]{:S(2)}) collective-permute-start(bf16[256,384]{1,0:T(8,128)(2,1)S(1)} %get-tuple-element.71), channel_id=1, source_target_pairs={{0,16},{1,17},{2,66},{3,67},{4,20},{5,21},{6,70},{7,71},{8,24},{9,... | collective-permute-start | bytes 589832 | tf_op jit(solution)/shard_map/ppermute | solution.py:71
  62.4 5.3 %key_grads.1 = (bf16[1024,384]{1,0:T(8,128)(2,1)S(1)}, bf16[1024,384]{1,0:T(8,128)(2,1)S(1)}, f32[8,128]{1,0:T(8,128)S(1)}) custom-call(s32[64]{0:T(128)S(1)} %dynamic-slice_bitcast_fusion.info, s32[32,128]{1,0:T(8,128)S(1)} %get-tuple-element.49.lists, bf16[8,3,512,128]{3,2,1,0:T(8,128)(2,1)S(1)} %get-tuple-element.62.probs_in, ...), custom_call_target="tpu_custom_call" | custom-call | flops 5750000128 | tf_op jit(solution)/shard_map/key_grads/pallas_call | solution.py:449
  67.7 0.8 collective-permute-done.16.refs_2_
  68.5 0.1 sum.2.refs_0_
  68.6 7.9 %collective-permute-start.20 = (bf16[256,384]{1,0:T(8,128)(2,1)S(1)}, bf16[256,384]{1,0:T(8,128)(2,1)S(1)}, u32[]{:S(2)}, u32[]{:S(2)}) collective-permute-start(bf16[256,384]{1,0:T(8,128)(2,1)S(1)} %sum.2.refs_0_), channel_id=1, source_target_pairs={{0,64},{1,65},{2,18},{3,19},{4,68},{5,69},{6,22},{7,23},{8,72},{9,... | collective-permute-start | bytes 589832 | tf_op jit(solution)/shard_map/ppermute | solution.py:71
  76.6 3.7 %collective-permute-done.20.refs_3_ = bf16[256,384]{1,0:T(8,128)(2,1)S(1)} collective-permute-done((bf16[256,384]{1,0:T(8,128)(2,1)S(1)}, bf16[256,384]{1,0:T(8,128)(2,1)S(1)}, u32[]{:S(2)}, u32[]{:S(2)}) %collective-permute-start.20) | collective-permute-done | bytes 196640 | tf_op jit(solution)/shard_map/ppermute | solution.py:71
  80.3 5.3 %collective-permute-done.19.refs_2_ = bf16[256,384]{1,0:T(8,128)(2,1)S(1)} collective-permute-done((bf16[256,384]{1,0:T(8,128)(2,1)S(1)}, bf16[256,384]{1,0:T(8,128)(2,1)S(1)}, u32[]{:S(2)}, u32[]{:S(2)}) %collective-permute-start.19) | collective-permute-done | bytes 196640 | tf_op jit(solution)/shard_map/ppermute | solution.py:71
  85.6 0.1 sum.3.refs_1_.refs_0_
  85.7 0.1 collective-permute-start.21
  85.8 0.6 copy-done.6
  86.4 0.2 collective-permute-start.13
  86.7 0.9 copy-done.7
  87.6 1.0 copy-done.19
  88.6 1.2 %weights.1 = (bf16[192,384]{1,0:T(8,128)(2,1)S(1)}, bf16[192,384]{1,0:T(8,128)(2,1)S(1)}, bf16[192,384]{1,0:T(8,128)(2,1)S(1)}, bf16[192,384]{1,0:T(8,128)(2,1)S(1)}) custom-call(s32[64]{0:T(128)S(1)} %dynamic-slice_bitcast_fusion.info, bf16[256,384]{1,0:T(8,128)(2,1)S(1)} %copy-done.7, bf16[2,256,384]{2,1,0:T(8,128)(2,1)S(1)} %copy-done.19), custom_call_target="tpu_custom_call" | custom-call | flops 1150000000 | tf_op jit(solution)/shard_map/weights/pallas_call | solution.py:449
  89.7 0.1 collective-permute-start.23
  89.8 3.1 %collective-permute-start.24 = (bf16[192,384]{1,0:T(8,128)(2,1)S(1)}, bf16[192,384]{1,0:T(8,128)(2,1)S(1)}, u32[]{:S(2)}, u32[]{:S(2)}) collective-permute-start(bf16[192,384]{1,0:T(8,128)(2,1)S(1)} %get-tuple-element.76), channel_id=1, source_target_pairs={{0,24},{1,25},{2,98},{3,99},{4,28},{5,29},{6,102},{7,103},{8,16},{... | collective-permute-start | bytes 442376 | tf_op jit(solution)/shard_map/ppermute | solution.py:71
  92.9 1.4 %collective-permute-start.25 = (bf16[192,384]{1,0:T(8,128)(2,1)S(1)}, bf16[192,384]{1,0:T(8,128)(2,1)S(1)}, u32[]{:S(2)}, u32[]{:S(2)}) collective-permute-start(bf16[192,384]{1,0:T(8,128)(2,1)S(1)} %get-tuple-element.77), channel_id=1, source_target_pairs={{0,16},{1,17},{2,66},{3,67},{4,20},{5,21},{6,70},{7,71},{8,24},{9,... | collective-permute-start | bytes 442376 | tf_op jit(solution)/shard_map/ppermute | solution.py:71
  94.3 3.2 %collective-permute-done.13 = bf16[512,384]{1,0:T(8,128)(2,1)} collective-permute-done((bf16[512,384]{1,0:T(8,128)(2,1)}, bf16[512,384]{1,0:T(8,128)(2,1)}, u32[]{:S(2)}, u32[]{:S(2)}) %collective-permute-start.13) | collective-permute-done | bytes 393248 | tf_op jit(solution)/shard_map/ppermute | solution.py:71
  97.5 1.0 add_convert_fusion.4.refs_5_
  98.5 0.1 collective-permute-start.14
  98.6 1.5 %collective-permute-done.21 = bf16[1024,384]{1,0:T(8,128)(2,1)} collective-permute-done((bf16[1024,384]{1,0:T(8,128)(2,1)S(1)}, bf16[1024,384]{1,0:T(8,128)(2,1)}, u32[]{:S(2)}, u32[]{:S(2)}) %collective-permute-start.21) | collective-permute-done | bytes 786464 | tf_op jit(solution)/shard_map/ppermute | solution.py:71
  100.0 1.1 add_convert_fusion.refs_4_
  101.1 2.0 %collective-permute-start.22 = (bf16[512,384]{1,0:T(8,128)(2,1)S(1)}, bf16[512,384]{1,0:T(8,128)(2,1)S(1)}, u32[]{:S(2)}, u32[]{:S(2)}) collective-permute-start(bf16[512,384]{1,0:T(8,128)(2,1)S(1)} %add_convert_fusion.refs_4_), channel_id=1, source_target_pairs={{0,96},{1,97},{2,26},{3,27},{4,100},{5,101},{6,30},{7,31},{8,104},... | collective-permute-start | bytes 1179656 | tf_op jit(solution)/shard_map/ppermute | solution.py:71
  103.2 0.1 split.1
  103.3 3.3 %collective-permute-start.26 = (bf16[96,384]{1,0:T(8,128)(2,1)S(1)}, bf16[96,384]{1,0:T(8,128)(2,1)S(1)}, u32[]{:S(2)}, u32[]{:S(2)}) collective-permute-start(bf16[96,384]{1,0:T(8,128)(2,1)S(1)} %get-tuple-element.79), channel_id=1, source_target_pairs={{0,1},{1,0},{2,3},{3,2},{4,5},{5,4},{6,7},{7,6},{8,9},{9,8},{10,11... | collective-permute-start | bytes 221192 | tf_op jit(solution)/shard_map/ppermute | solution.py:698
  106.6 1.7 %fusion = bf16[1,256,384]{2,1,0:T(8,128)(2,1)} fusion(bf16[256,384]{1,0:T(8,128)(2,1)S(1)} %collective-permute-done.14, bf16[512,384]{1,0:T(8,128)(2,1)} %collective-permute-done.13, bf16[512,384]{1,0:T(8,128)(2,1)S(1)} %get-tuple-element.60), kind=kLoop, calls=%fused_computation.6 | loop fusion | flops 589824 | bytes 786432 | tf_op jit(solution)/shard_map/broadcast_in_dim | solution.py:699
  108.3 1.0 collective-permute-done.26
  109.2 0.7 convert_add_fusion
  109.9 0.3 collective-permute-done.22
  110.2 1.9 %fusion.2 = (bf16[1,256,384]{2,1,0:T(8,128)(2,1)}, bf16[1,256,384]{2,1,0:T(8,128)(2,1)}) fusion(bf16[512,384]{1,0:T(8,128)(2,1)S(1)} %collective-permute-done.22, bf16[1024,384]{1,0:T(8,128)(2,1)} %collective-permute-done.21, bf16[1024,384]{1,0:T(8,128)(2,1)S(1)} %copy-done.2), kind=kLoop, calls=%fused_computation.8 | loop fusion | flops 1179648 | bytes 1572864 | tf_op jit(solution)/shard_map/broadcast_in_dim | solution.py:701
  (52 shorter events, 0.3 us)
Async XLA Ops:
  0.6 1.7 %copy-start = (bf16[3072,384]{1,0:T(8,128)(2,1)S(1)}, bf16[3072,384]{1,0:T(8,128)(2,1)}, u32[]{:S(2)}) copy-start(bf16[3072,384]{1,0:T(8,128)(2,1)} %param.16) | copy-start | bytes 7077892
  0.6 3.1 %copy-start.17 = (s32[4,2]{0,1:T(2,128)S(1)}, s32[4,2]{0,1:T(2,128)}, u32[]{:S(2)}) copy-start(s32[4,2]{0,1:T(2,128)} %param.14) | copy-start | bytes 100
  0.7 3.1 %copy-start.16 = (s32[4,32]{1,0:T(4,128)S(1)}, s32[4,32]{1,0:T(4,128)}, u32[]{:S(2)}) copy-start(s32[4,32]{1,0:T(4,128)} %kv_list.1) | copy-start | bytes 1540
  0.7 3.1 %copy-start.13 = (bf16[1,256,384]{2,1,0:T(8,128)(2,1)S(1)}, bf16[1,256,384]{2,1,0:T(8,128)(2,1)}, u32[]{:S(2)}) copy-start(bf16[1,256,384]{2,1,0:T(8,128)(2,1)} %param.12) | copy-start | bytes 589828
  0.7 3.1 %copy-start.12 = (bf16[1,256,384]{2,1,0:T(8,128)(2,1)S(1)}, bf16[1,256,384]{2,1,0:T(8,128)(2,1)}, u32[]{:S(2)}) copy-start(bf16[1,256,384]{2,1,0:T(8,128)(2,1)} %param.9) | copy-start | bytes 589828
  3.8 3.3 %copy-start.14 = (bf16[1,256,384]{2,1,0:T(8,128)(2,1)S(1)}, bf16[1,256,384]{2,1,0:T(8,128)(2,1)}, u32[]{:S(2)}) copy-start(bf16[1,256,384]{2,1,0:T(8,128)(2,1)} %param.10) | copy-start | bytes 589828
  3.8 3.3 %copy-start.15 = (bf16[1,256,384]{2,1,0:T(8,128)(2,1)S(1)}, bf16[1,256,384]{2,1,0:T(8,128)(2,1)}, u32[]{:S(2)}) copy-start(bf16[1,256,384]{2,1,0:T(8,128)(2,1)} %param.11) | copy-start | bytes 589828
  3.9 15.2 %copy-start.8 = (bf16[592,384]{1,0:T(8,128)(2,1)}, bf16[592,384]{1,0:T(8,128)(2,1)S(1)}, u32[]{:S(2)}) copy-start(bf16[592,384]{1,0:T(8,128)(2,1)S(1)} %get-tuple-element.42.refs_0_) | copy-start | bytes 1363972
  3.9 15.2 %collective-permute-start.3 = (bf16[592,384]{1,0:T(8,128)(2,1)S(1)}, bf16[592,384]{1,0:T(8,128)(2,1)S(1)}, u32[]{:S(2)}, u32[]{:S(2)}) collective-permute-start(bf16[592,384]{1,0:T(8,128)(2,1)S(1)} %get-tuple-element.42.refs_0_), channel_id=1, source_target_pairs={{0,24},{1,25},{2,98},{3,99},{4,28},{5,29},{6,102},{7,103},{8,16},{... | collective-permute-start | bytes 1363976 | tf_op jit(solution)/shard_map/ppermute | solution.py:71
  6.8 12.6 %collective-permute-start = (bf16[592,384]{1,0:T(8,128)(2,1)S(1)}, bf16[592,384]{1,0:T(8,128)(2,1)S(1)}, u32[]{:S(2)}, u32[]{:S(2)}) collective-permute-start(bf16[592,384]{1,0:T(8,128)(2,1)S(1)} %get-tuple-element.42.refs_0_), channel_id=1, source_target_pairs={{0,8},{1,9},{2,34},{3,35},{4,12},{5,13},{6,38},{7,39},{8,0},{9,1},... | collective-permute-start | bytes 1363976 | tf_op jit(solution)/shard_map/ppermute | solution.py:71
  7.1 12.0 %collective-permute-start.4 = (bf16[512,384]{1,0:T(8,128)(2,1)S(1)}, bf16[512,384]{1,0:T(8,128)(2,1)S(1)}, u32[]{:S(2)}, u32[]{:S(2)}) collective-permute-start(bf16[512,384]{1,0:T(8,128)(2,1)S(1)} %stack.1.refs_4_.refs_0_), channel_id=1, source_target_pairs={{0,32},{1,33},{2,10},{3,11},{4,36},{5,37},{6,14},{7,15},{8,40},{9,... | collective-permute-start | bytes 1179656 | tf_op jit(solution)/shard_map/ppermute | solution.py:71
  9.1 10.0 %collective-permute-start.1 = (bf16[512,384]{1,0:T(8,128)(2,1)S(1)}, bf16[512,384]{1,0:T(8,128)(2,1)}, u32[]{:S(2)}, u32[]{:S(2)}) collective-permute-start(bf16[512,384]{1,0:T(8,128)(2,1)S(1)} %stack.1.refs_4_.refs_0_), channel_id=1, source_target_pairs={{0,96},{1,97},{2,26},{3,27},{4,100},{5,101},{6,30},{7,31},{8,104},... | collective-permute-start | bytes 1179656 | tf_op jit(solution)/shard_map/ppermute | solution.py:71
  11.6 0.7 copy-start.10
  12.3 6.5 %collective-permute-start.2 = (bf16[80,384]{1,0:T(8,128)(2,1)S(1)}, bf16[80,384]{1,0:T(8,128)(2,1)S(1)}, u32[]{:S(2)}, u32[]{:S(2)}) collective-permute-start(bf16[80,384]{1,0:T(8,128)(2,1)S(1)} %get-tuple-element.43), channel_id=1, source_target_pairs={{0,16},{1,17},{2,66},{3,67},{4,20},{5,21},{6,70},{7,71},{8,24},{9,... | collective-permute-start | bytes 184328 | tf_op jit(solution)/shard_map/ppermute | solution.py:71
  19.1 0.7 copy-start.3
  19.8 12.5 %collective-permute-start.5 = (bf16[592,384]{1,0:T(8,128)(2,1)S(1)}, bf16[592,384]{1,0:T(8,128)(2,1)}, u32[]{:S(2)}, u32[]{:S(2)}) collective-permute-start(bf16[592,384]{1,0:T(8,128)(2,1)S(1)} %get-tuple-element.44.refs_1_), channel_id=1, source_target_pairs={{0,24},{1,25},{2,98},{3,99},{4,28},{5,29},{6,102},{7,103},{8,16},{... | collective-permute-start | bytes 1363976 | tf_op jit(solution)/shard_map/ppermute | solution.py:71
  23.5 8.8 %collective-permute-start.6 = (bf16[512,384]{1,0:T(8,128)(2,1)}, bf16[512,384]{1,0:T(8,128)(2,1)}, u32[]{:S(2)}, u32[]{:S(2)}) collective-permute-start(bf16[512,384]{1,0:T(8,128)(2,1)} %get-tuple-element.50.refs_6_.refs_2_), channel_id=1, source_target_pairs={{0,32},{1,33},{2,10},{3,11},{4,36},{5,37},{6,14},{7,15},{8,40},{9,... | collective-permute-start | bytes 1179656 | tf_op jit(solution)/shard_map/ppermute | solution.py:71
  26.0 1.0 copy-start.5
  27.0 1.1 copy-start.9
  28.0 4.3 %copy-start.4 = (bf16[512,384]{1,0:T(8,128)(2,1)S(1)}, bf16[512,384]{1,0:T(8,128)(2,1)}, u32[]{:S(2)}) copy-start(bf16[512,384]{1,0:T(8,128)(2,1)} %copy-done.3) | copy-start | bytes 1179652
  28.0 4.3 %copy-start.11 = (bf16[512,384]{1,0:T(8,128)(2,1)S(1)}, bf16[512,384]{1,0:T(8,128)(2,1)}, u32[]{:S(2)}) copy-start(bf16[512,384]{1,0:T(8,128)(2,1)} %copy-done.10) | copy-start | bytes 1179652
  28.1 8.0 %collective-permute-start.7 = (bf16[384,384]{1,0:T(8,128)(2,1)S(1)}, bf16[384,384]{1,0:T(8,128)(2,1)S(1)}, u32[]{:S(2)}, u32[]{:S(2)}) collective-permute-start(bf16[384,384]{1,0:T(8,128)(2,1)S(1)} %get-tuple-element.52), channel_id=1, source_target_pairs={{0,32},{1,33},{2,10},{3,11},{4,36},{5,37},{6,14},{7,15},{8,40},{9,... | collective-permute-start | bytes 884744 | tf_op jit(solution)/shard_map/ppermute | solution.py:71
  28.5 11.1 %collective-permute-start.8 = (bf16[384,384]{1,0:T(8,128)(2,1)S(1)}, bf16[384,384]{1,0:T(8,128)(2,1)S(1)}, u32[]{:S(2)}, u32[]{:S(2)}) collective-permute-start(bf16[384,384]{1,0:T(8,128)(2,1)S(1)} %get-tuple-element.53), channel_id=1, source_target_pairs={{0,96},{1,97},{2,26},{3,27},{4,100},{5,101},{6,30},{7,31},{8,104},... | collective-permute-start | bytes 884744 | tf_op jit(solution)/shard_map/ppermute | solution.py:71
  30.4 9.2 %collective-permute-start.9 = (bf16[384,384]{1,0:T(8,128)(2,1)S(1)}, bf16[384,384]{1,0:T(8,128)(2,1)S(1)}, u32[]{:S(2)}, u32[]{:S(2)}) collective-permute-start(bf16[384,384]{1,0:T(8,128)(2,1)S(1)} %get-tuple-element.54), channel_id=1, source_target_pairs={{0,64},{1,65},{2,18},{3,19},{4,68},{5,69},{6,22},{7,23},{8,72},{9,... | collective-permute-start | bytes 884744 | tf_op jit(solution)/shard_map/ppermute | solution.py:71
  45.6 0.8 copy-start.18
  46.4 5.8 %collective-permute-start.12 = (f32[16,1024]{1,0:T(8,128)S(1)}, f32[16,1024]{1,0:T(8,128)S(1)}, u32[]{:S(2)}, u32[]{:S(2)}) collective-permute-start(f32[16,1024]{1,0:T(8,128)S(1)} %get-tuple-element.56.refs_4_.refs_0_), channel_id=1, source_target_pairs={{0,16},{1,17},{2,66},{3,67},{4,20},{5,21},{6,70},{7,71},{8,24},{9,... | collective-permute-start | bytes 196616 | tf_op jit(solution)/shard_map/ppermute | solution.py:71
  47.1 5.8 %collective-permute-start.11 = (f32[16,1024]{1,0:T(8,128)S(1)}, f32[16,1024]{1,0:T(8,128)S(1)}, u32[]{:S(2)}, u32[]{:S(2)}) collective-permute-start(f32[16,1024]{1,0:T(8,128)S(1)} %get-tuple-element.56.refs_4_.refs_0_), channel_id=1, source_target_pairs={{0,24},{1,25},{2,98},{3,99},{4,28},{5,29},{6,102},{7,103},{8,16},{... | collective-permute-start | bytes 196616 | tf_op jit(solution)/shard_map/ppermute | solution.py:71
  48.3 4.6 %collective-permute-start.10 = (f32[16,1024]{1,0:T(8,128)S(1)}, f32[16,1024]{1,0:T(8,128)S(1)}, u32[]{:S(2)}, u32[]{:S(2)}) collective-permute-start(f32[16,1024]{1,0:T(8,128)S(1)} %get-tuple-element.56.refs_4_.refs_0_), channel_id=1, source_target_pairs={{0,8},{1,9},{2,34},{3,35},{4,12},{5,13},{6,38},{7,39},{8,0},{9,1},... | collective-permute-start | bytes 196616 | tf_op jit(solution)/shard_map/ppermute | solution.py:71
  58.3 9.4 %collective-permute-start.15 = (bf16[256,384]{1,0:T(8,128)(2,1)S(1)}, bf16[256,384]{1,0:T(8,128)(2,1)S(1)}, u32[]{:S(2)}, u32[]{:S(2)}) collective-permute-start(bf16[256,384]{1,0:T(8,128)(2,1)S(1)} %get-tuple-element.69), channel_id=1, source_target_pairs={{0,8},{1,9},{2,34},{3,35},{4,12},{5,13},{6,38},{7,39},{8,0},{9,1},... | collective-permute-start | bytes 589832 | tf_op jit(solution)/shard_map/ppermute | solution.py:71
  59.5 9.0 %collective-permute-start.16 = (bf16[256,384]{1,0:T(8,128)(2,1)S(1)}, bf16[256,384]{1,0:T(8,128)(2,1)S(1)}, u32[]{:S(2)}, u32[]{:S(2)}) collective-permute-start(bf16[256,384]{1,0:T(8,128)(2,1)S(1)} %get-tuple-element.70), channel_id=1, source_target_pairs={{0,24},{1,25},{2,98},{3,99},{4,28},{5,29},{6,102},{7,103},{8,16},{... | collective-permute-start | bytes 589832 | tf_op jit(solution)/shard_map/ppermute | solution.py:71
  61.2 7.4 %collective-permute-start.17 = (bf16[256,384]{1,0:T(8,128)(2,1)S(1)}, bf16[256,384]{1,0:T(8,128)(2,1)S(1)}, u32[]{:S(2)}, u32[]{:S(2)}) collective-permute-start(bf16[256,384]{1,0:T(8,128)(2,1)S(1)} %get-tuple-element.71), channel_id=1, source_target_pairs={{0,16},{1,17},{2,66},{3,67},{4,20},{5,21},{6,70},{7,71},{8,24},{9,... | collective-permute-start | bytes 589832 | tf_op jit(solution)/shard_map/ppermute | solution.py:71
  67.7 18.0 %copy-start.1 = (bf16[1024,384]{1,0:T(8,128)(2,1)}, bf16[1024,384]{1,0:T(8,128)(2,1)S(1)}, u32[]{:S(2)}) copy-start(bf16[1024,384]{1,0:T(8,128)(2,1)S(1)} %get-tuple-element.66) | copy-start | bytes 2359300
  68.6 11.7 %collective-permute-start.20 = (bf16[256,384]{1,0:T(8,128)(2,1)S(1)}, bf16[256,384]{1,0:T(8,128)(2,1)S(1)}, u32[]{:S(2)}, u32[]{:S(2)}) collective-permute-start(bf16[256,384]{1,0:T(8,128)(2,1)S(1)} %sum.2.refs_0_), channel_id=1, source_target_pairs={{0,64},{1,65},{2,18},{3,19},{4,68},{5,69},{6,22},{7,23},{8,72},{9,... | collective-permute-start | bytes 589832 | tf_op jit(solution)/shard_map/ppermute | solution.py:71
  76.6 9.0 %collective-permute-start.19 = (bf16[256,384]{1,0:T(8,128)(2,1)S(1)}, bf16[256,384]{1,0:T(8,128)(2,1)S(1)}, u32[]{:S(2)}, u32[]{:S(2)}) collective-permute-start(bf16[256,384]{1,0:T(8,128)(2,1)S(1)} %sum.2.refs_0_), channel_id=1, source_target_pairs={{0,96},{1,97},{2,26},{3,27},{4,100},{5,101},{6,30},{7,31},{8,104},... | collective-permute-start | bytes 589832 | tf_op jit(solution)/shard_map/ppermute | solution.py:71
  76.6 9.0 %collective-permute-start.18 = (bf16[256,384]{1,0:T(8,128)(2,1)S(1)}, bf16[256,384]{1,0:T(8,128)(2,1)S(1)}, u32[]{:S(2)}, u32[]{:S(2)}) collective-permute-start(bf16[256,384]{1,0:T(8,128)(2,1)S(1)} %sum.2.refs_0_), channel_id=1, source_target_pairs={{0,32},{1,33},{2,10},{3,11},{4,36},{5,37},{6,14},{7,15},{8,40},{9,... | collective-permute-start | bytes 589832 | tf_op jit(solution)/shard_map/ppermute | solution.py:71
  85.7 0.7 copy-start.6
  85.7 14.3 %collective-permute-start.21 = (bf16[1024,384]{1,0:T(8,128)(2,1)S(1)}, bf16[1024,384]{1,0:T(8,128)(2,1)}, u32[]{:S(2)}, u32[]{:S(2)}) collective-permute-start(bf16[1024,384]{1,0:T(8,128)(2,1)S(1)} %tie.3), channel_id=1, source_target_pairs={{0,32},{1,33},{2,10},{3,11},{4,36},{5,37},{6,14},{7,15},{8,40},{9,... | collective-permute-start | bytes 2359304 | tf_op jit(solution)/shard_map/ppermute | solution.py:71
  86.4 11.1 %collective-permute-start.13 = (bf16[512,384]{1,0:T(8,128)(2,1)}, bf16[512,384]{1,0:T(8,128)(2,1)}, u32[]{:S(2)}, u32[]{:S(2)}) collective-permute-start(bf16[512,384]{1,0:T(8,128)(2,1)} %get-tuple-element.61), channel_id=1, source_target_pairs={{0,24},{1,25},{2,98},{3,99},{4,28},{5,29},{6,102},{7,103},{8,16},{... | collective-permute-start | bytes 1179656 | tf_op jit(solution)/shard_map/ppermute | solution.py:71
  86.7 0.9 copy-start.7
  87.6 1.0 copy-start.19
  88.6 11.5 %copy-start.2 = (bf16[1024,384]{1,0:T(8,128)(2,1)S(1)}, bf16[1024,384]{1,0:T(8,128)(2,1)}, u32[]{:S(2)}) copy-start(bf16[1024,384]{1,0:T(8,128)(2,1)} %copy-done.1) | copy-start | bytes 2359300
  89.7 13.4 %collective-permute-start.23 = (bf16[192,384]{1,0:T(8,128)(2,1)S(1)}, bf16[192,384]{1,0:T(8,128)(2,1)S(1)}, u32[]{:S(2)}, u32[]{:S(2)}) collective-permute-start(bf16[192,384]{1,0:T(8,128)(2,1)S(1)} %get-tuple-element.75), channel_id=1, source_target_pairs={{0,8},{1,9},{2,34},{3,35},{4,12},{5,13},{6,38},{7,39},{8,0},{9,1},... | collective-permute-start | bytes 442376 | tf_op jit(solution)/shard_map/ppermute | solution.py:71
  89.8 13.3 %collective-permute-start.24 = (bf16[192,384]{1,0:T(8,128)(2,1)S(1)}, bf16[192,384]{1,0:T(8,128)(2,1)S(1)}, u32[]{:S(2)}, u32[]{:S(2)}) collective-permute-start(bf16[192,384]{1,0:T(8,128)(2,1)S(1)} %get-tuple-element.76), channel_id=1, source_target_pairs={{0,24},{1,25},{2,98},{3,99},{4,28},{5,29},{6,102},{7,103},{8,16},{... | collective-permute-start | bytes 442376 | tf_op jit(solution)/shard_map/ppermute | solution.py:71
  92.9 10.3 %collective-permute-start.25 = (bf16[192,384]{1,0:T(8,128)(2,1)S(1)}, bf16[192,384]{1,0:T(8,128)(2,1)S(1)}, u32[]{:S(2)}, u32[]{:S(2)}) collective-permute-start(bf16[192,384]{1,0:T(8,128)(2,1)S(1)} %get-tuple-element.77), channel_id=1, source_target_pairs={{0,16},{1,17},{2,66},{3,67},{4,20},{5,21},{6,70},{7,71},{8,24},{9,... | collective-permute-start | bytes 442376 | tf_op jit(solution)/shard_map/ppermute | solution.py:71
  98.5 8.1 %collective-permute-start.14 = (bf16[256,384]{1,0:T(8,128)(2,1)S(1)}, bf16[256,384]{1,0:T(8,128)(2,1)S(1)}, u32[]{:S(2)}, u32[]{:S(2)}) collective-permute-start(bf16[256,384]{1,0:T(8,128)(2,1)S(1)} %add_convert_fusion.4.refs_5_), channel_id=1, source_target_pairs={{0,8},{1,9},{2,34},{3,35},{4,12},{5,13},{6,38},{7,39},{8,0},{9,1},... | collective-permute-start | bytes 589832 | tf_op jit(solution)/shard_map/ppermute | solution.py:71
  101.1 9.1 %collective-permute-start.22 = (bf16[512,384]{1,0:T(8,128)(2,1)S(1)}, bf16[512,384]{1,0:T(8,128)(2,1)S(1)}, u32[]{:S(2)}, u32[]{:S(2)}) collective-permute-start(bf16[512,384]{1,0:T(8,128)(2,1)S(1)} %add_convert_fusion.refs_4_), channel_id=1, source_target_pairs={{0,96},{1,97},{2,26},{3,27},{4,100},{5,101},{6,30},{7,31},{8,104},... | collective-permute-start | bytes 1179656 | tf_op jit(solution)/shard_map/ppermute | solution.py:71
  103.3 5.9 %collective-permute-start.26 = (bf16[96,384]{1,0:T(8,128)(2,1)S(1)}, bf16[96,384]{1,0:T(8,128)(2,1)S(1)}, u32[]{:S(2)}, u32[]{:S(2)}) collective-permute-start(bf16[96,384]{1,0:T(8,128)(2,1)S(1)} %get-tuple-element.79), channel_id=1, source_target_pairs={{0,1},{1,0},{2,3},{3,2},{4,5},{5,4},{6,7},{7,6},{8,9},{9,8},{10,11... | collective-permute-start | bytes 221192 | tf_op jit(solution)/shard_map/ppermute | solution.py:698

commit v3 on v2

--- a/solution.py
+++ b/solution.py
@@ -80,9 +80,9 @@
 
 
 def halved(near, away, role, first, second):
+    come = send(away, role, first)
+
     half = near.shape[0] // 2
-    come = send(away, role, first)
-
     on = (near[half:].astype(F32) + come[half:].astype(F32)).astype(BF16)
     return [near[:half], come[:half], send(on, role, second)], on
 
@@ -193,12 +193,9 @@
 
 
 def token_kernel(info, tokens, *refs):
-    out, held, padded, sem = refs[0:4], refs[4], refs[5], refs[6]
-    copy = pltpu.make_async_copy(tokens, held, sem)
-    copy.start()
-    copy.wait()
+    out, padded = refs[0:4], refs[4]
     for n in range(16):
-        padded[:, n * PADDED : n * PADDED + CHUNK] = held[:, n * CHUNK : (n + 1) * CHUNK]
+        padded[:, n * PADDED : n * PADDED + CHUNK] = tokens[:, n * CHUNK : (n + 1) * CHUNK]
     for sv in range(SIDE):
         for su in range(SIDE):
             start = pl.multiple_of(info[20 + sv * SIDE + su] * PADDED, PADDED)
@@ -220,10 +217,12 @@
 
 
 def sum_kernel(*refs):
+    out, flag = refs[-2:]
     total = refs[0][...].astype(F32)
     for part in refs[1:4]:
         total = total + part[...].astype(F32)
-    refs[-1][...] = total.astype(refs[-1].dtype)
+    out[...] = total.astype(BF16)
+    flag[...] = jnp.zeros_like(flag)
 
 
 def split_kernel(clip, *refs):
@@ -250,10 +249,10 @@
         pair = step * PAIRS + n
         rows = pl.ds(pl.multiple_of(pair * HD, HD), HD)
         grad = grads[rows, :]
-        grad_out[n * HD : (n + 1) * HD, :] = grad
+        grad_out[rows, :] = grad
         starts = [picks(info, lists, pair, slot) for slot in range(SIDE)]
         for head in range(HEADS):
-            slope_out[n, head] = nt(
+            slope_out[pair, head] = nt(
                 all_taken(values, starts, head), diagonal(grad[:, columns(head)])
             )
 
@@ -261,20 +260,16 @@
 def score_kernel(info, lists, *refs):
     qg, kv, conds, slope = refs[0:4], refs[4:8], refs[8:12], refs[12]
     qeff, stat, probs_out, tokens = refs[13:17]
-    queries, cond, sems = refs[17:]
+    queries, cond = refs[17:]
     step = pl.program_id(0)
-    copies = []
-    for slot in range(SIDE):
-        for half in range(2):
-            source = conds[slot].at[256 + half * BLK : 256 + (half + 1) * BLK, :]
-            to = tokens.at[half, slot * BLK : (slot + 1) * BLK, :]
-            copies.append(pltpu.make_async_copy(source, to, sems.at[2 * slot + half]))
     keys = [(ref, 0) for ref in kv]
 
     @pl.when(step == 0)
     def _():
-        for copy in copies:
-            copy.start()
+        for slot in range(SIDE):
+            for half in range(2):
+                first = 256 + half * BLK
+                tokens[half, slot * BLK : (slot + 1) * BLK, :] = conds[slot][first : first + BLK, :]
         for slot in range(SIDE):
             at = slice(slot * 256, (slot + 1) * 256)
             queries[at, :] = qg[slot][0:256, :]
@@ -292,7 +287,7 @@
             ]
             lifted.append(parts[0] + parts[1])
         query = (queries[rows, :].astype(F32) + jnp.concatenate(lifted, axis=0)).astype(BF16)
-        qeff[here, :] = query
+        qeff[rows, :] = query
         starts = [picks(info, lists, pair, slot) for slot in range(SIDE)]
         tops, totals, weighted = [], [], []
         for head in range(HEADS):
@@ -301,15 +296,10 @@
             probs = jnp.exp2((scores - top) * SCALE2)
             tops.append(top)
             totals.append(jnp.sum(probs, axis=0, keepdims=True))
-            weighted.append(jnp.sum(probs * slope[n, head], axis=0, keepdims=True))
-            probs_out[n, head] = probs.astype(BF16)
+            weighted.append(jnp.sum(probs * slope[pair, head], axis=0, keepdims=True))
+            probs_out[pair, head] = probs.astype(BF16)
         nothing = [jnp.zeros((16 - 3 * HEADS, HD), F32)]
-        stat[:, here] = jnp.concatenate(tops + totals + weighted + nothing, axis=0)
-
-    @pl.when(step == 8 // PAIRS - 1)
-    def _():
-        for copy in copies:
-            copy.wait()
+        stat[:, rows] = jnp.concatenate(tops + totals + weighted + nothing, axis=0)
 
 
 def turn_kernel(*refs):
@@ -363,10 +353,10 @@
         for head in range(HEADS):
             at = columns(head)
             factor, delta = factors[head : head + 1, rows], deltas[head : head + 1, rows]
-            probs = probs_in[n, head].astype(F32) * factor
-            score = (probs * (slope_in[n, head] - delta) * SCALE).astype(BF16)
-            probs_out[n, head] = probs.astype(BF16)
-            score_out[n, head] = score
+            probs = probs_in[pair, head].astype(F32) * factor
+            score = (probs * (slope_in[pair, head] - delta) * SCALE).astype(BF16)
+            probs_out[pair, head] = probs.astype(BF16)
+            score_out[pair, head] = score
             keys = []
             for block in range(2):
                 across = []
@@ -405,12 +395,12 @@
 
     for n in range(PAIRS):
         pair = step * PAIRS + n
-        here = slice(n * HD, (n + 1) * HD)
+        rows = pl.ds(pl.multiple_of(pair * HD, HD), HD)
         starts = [picks(info, lists, pair, slot) for slot in range(SIDE)]
         for head in range(HEADS):
             at = columns(head)
-            spread(dk, starts, head, nn(score_in[n, head], diagonal(qeff[here, at])))
-            spread(dv, starts, head, nn(probs_in[n, head], diagonal(grads[here, at])))
+            spread(dk, starts, head, nn(score_in[pair, head], diagonal(qeff[rows, at])))
+            spread(dv, starts, head, nn(probs_in[pair, head], diagonal(grads[rows, at])))
 
     @pl.when(step == 8 // PAIRS - 1)
     def _():
@@ -421,15 +411,11 @@
 
 
 def weight_kernel(info, *refs):
-    cond, tokens, out = refs[0], refs[1], refs[2:6]
-    whole, stacked, sem = refs[6:]
-    copy = pltpu.make_async_copy(tokens, stacked, sem)
-    copy.start()
+    cond, stacked, out, whole = refs[0], refs[1], refs[2:6], refs[6]
     rows = []
     for slot in range(SIDE):
         rows.append(cond[pl.ds(pl.multiple_of(info[52 + slot] * BLK, BLK), BLK), :])
     half_sums = jnp.concatenate(rows, axis=0)
-    copy.wait()
     for half in range(2):
         whole[...] = tn(stacked[half], half_sums)
         for n in range(2):
@@ -439,10 +425,7 @@
 VMEM = pl.BlockSpec(memory_space=pltpu.VMEM)
 SMEM = pl.BlockSpec(memory_space=pltpu.SMEM)
 ANY = pl.BlockSpec(memory_space=pl.ANY)
-HBM = pl.BlockSpec(memory_space=pltpu.HBM)
-TILES = pl.BlockSpec((PAIRS, HEADS, 512, HD), lambda i: (i, 0, 0, 0))
-LINES = pl.BlockSpec((PAIRS * HD, WIDTH), lambda i: (i, 0))
-STATS = pl.BlockSpec((16, PAIRS * HD), lambda i: (0, i))
+TILES = LINES = STATS = VMEM
 
 
 def call(kernel, name, operands, in_specs, outs, out_specs, scratch, limit, grid=(), cost=1, alias=None):
@@ -504,10 +487,10 @@
         token_kernel,
         "tokens",
         [info, tokens],
-        [SMEM, HBM],
+        [SMEM, VMEM],
         [((128, WIDTH), BF16)] * 4,
         [VMEM] * 4,
-        [((BLK, 16 * CHUNK), BF16), ((BLK, 16 * PADDED), BF16), pltpu.SemaphoreType.DMA],
+        [((BLK, 16 * PADDED), BF16)],
         4,
     )
 
@@ -552,11 +535,11 @@
         "sum",
         parts + after,
         [VMEM] * (4 + len(after)),
-        [(parts[0].shape, BF16)],
-        [VMEM],
+        [(parts[0].shape, BF16), ((8, HD), F32)],
+        [VMEM] * 2,
         [],
         4,
-    )[0]
+    )
 
 
 def split_call(clip, parts, after):
@@ -569,6 +552,8 @@
         [VMEM] * 2,
         [((CHUNK, WIDTH), F32)],
         4,
+        (),
+        10,
     )
 
 
@@ -594,8 +579,8 @@
         [info, lists] + qg + kv + conds + [slope],
         [SMEM] * 2 + [VMEM] * 12 + [TILES],
         [WHOLE, ((16, ROWS), F32), PROBS, ((2, 256, WIDTH), BF16)],
-        [LINES, STATS, TILES, HBM],
-        [WHOLE] * 2 + [pltpu.SemaphoreType.DMA((8,))],
+        [LINES, STATS, TILES, VMEM],
+        [WHOLE] * 2,
         14,
         GRID,
         5,
@@ -652,14 +637,10 @@
         weight_kernel,
         "weights",
         [info, cond, tokens],
-        [SMEM, VMEM, HBM],
+        [SMEM] + [VMEM] * 2,
         [((CHUNK, WIDTH), BF16)] * 4,
         [VMEM] * 4,
-        [
-            ((2 * CHUNK, WIDTH), F32),
-            ((2, 256, 2 * CHUNK), BF16),
-            pltpu.SemaphoreType.DMA,
-        ],
+        [((2 * CHUNK, WIDTH), F32)],
         8,
         (),
         1,
@@ -675,8 +656,9 @@
     qg, row = pack_call(queries[0], grad_out[0], cond, kv_list, cover_lists.T)
     qg1, qg3, row2 = send(qg, "u", 1), send(qg, "u", 3), send(row, "u", 2)
     kv3, kv1 = send(kv, "v", 3), send(kv, "v", 1)
+    tokens = token_call(info, cond_tokens[0])
     qg1, kv3 = tied([qg1, kv3], [row2, qg3, kv1])
-    out = join_call([qg, qg1, qg3, row2], token_call(info, cond_tokens[0]))
+    out = join_call([qg, qg1, qg3, row2], tokens)
     conds, lists = scattered(out[0:4], "v"), out[4]
     qg = [qg, qg1, qg3, send(qg1, "u", 3)]
     kv = [kv, kv1, kv3, send(kv3, "v", 1)]
@@ -688,13 +670,13 @@
     cg, dq, probs, score = out[0:4], out[4:6], out[6], out[7]
     cg = scattered(cg, "u")
     dkv = key_call(info, lists, probs, score, qeff, grads)
-    cg = gathered(sum_call(cg, [dkv[2]]), "v")
-    cg = sum_call(cg, [])
-    away, = tied([dkv[1]], [cg])
+    cg, flag = sum_call(cg, [dkv[2]])
+    cg = sum_call(gathered(cg, "v"), [])[0]
+    (away,) = tied([dkv[1]], [flag])
     dkv, on = halved(dkv[0], away, "v", 1, 3)
     dq, dq_on = halved(dq[0], dq[1], "u", 3, 1)
     weight = scattered(weight_call(info, cg, tokens), "u")
-    mine, other = split_call(lax.axis_index("dp").reshape(1), weight, [on, dq_on])
+    mine, other = split_call(lax.axis_index("dp").reshape(1), weight, [on])
     grad_cond_weight = mine + lax.ppermute(other, "dp", [(0, 1), (1, 0)]).astype(F32)
     grad_query = summed(dq).astype(BF16)[None]
     grad_key = summed([part[:256] for part in dkv]).astype(BF16)[None]

time: 113 us -> 109 us (0.965)
  waiting for transfers between devices: 25.4 us -> 20.9 us
  local copies, waits for them, and re-layouts: 7.73 us -> 5.39 us
  Pallas kernels: 25.4 us -> 26.7 us
  starting transfers between devices: 44.8 us -> 46 us
    ppermute x26, waiting for transfers between devices: 24.4 us -> 19.9 us  [send(): return lax.ppermute(array, ('ctx', 'head', 'dp'), pairs)]
    unnamed x40 -> x36, local copies, waits for them, and re-layouts: 7.04 us -> 4.7 us
    pallas_call x15, Pallas kernels: 25.4 us -> 26.7 us  [call(): pl.pallas_call(kernel, name=name, grid=grid, out_shape=[jax.ShapeDtypeStr...]
    ppermute x26, starting transfers between devices: 41.5 us -> 42.7 us  [send(): return lax.ppermute(array, ('ctx', 'head', 'dp'), pairs)]
  transfers between devices with their start and end apart: 27 -> 27, of which waited for: 13 -> 10; matrix products, arithmetic and copies ran while one was open for 5% -> 5% of each run, Pallas kernels for 12% -> 14%
where the time goes in v3:
time: 109 us; the launch traced here: 108 us
  starting transfers between devices  46 us (42%)
  Pallas kernels  26.7 us (24%)
  waiting for transfers between devices  20.9 us (19%)
  other arithmetic  6.34 us (6%)
  local copies, waits for them, and re-layouts  5.39 us (5%)
  matrix products  1.44 us (1%)
    ppermute x26, starting transfers between devices, send(): return lax.ppermute(array, ('ctx', 'head', 'dp'), pairs)  42.7 us
    pallas_call x15, Pallas kernels, call(): pl.pallas_call(kernel, name=name, grid=grid, out_shape=[jax.ShapeDtypeStr...  26.7 us
    ppermute x26, waiting for transfers between devices, send(): return lax.ppermute(array, ('ctx', 'head', 'dp'), pairs)  19.9 us
    unnamed x36, local copies, waits for them, and re-layouts  4.7 us
    ppermute x1, starting transfers between devices, body(): lax.ppermute(other, 'dp', [(0, 1), (1, 0)]).astype(F32)  3.28 us
  transfers between devices with their start and end apart: 27, of which 10 were waited for; matrix products, arithmetic and copies ran while one was open for 5% of the time, Pallas kernels for 14%

profile of v3, /device:TPU:0, one launch (start us, length us, event | category | flops | bytes accessed | tf_op | source)
XLA Modules:
  0.0 107.7 jit_solution(6458344874202819850)
XLA Ops:
  0.6 0.0 copy-start
  0.7 1.6 %copy-done = bf16[3072,384]{1,0:T(8,128)(2,1)S(1)} copy-done((bf16[3072,384]{1,0:T(8,128)(2,1)S(1)}, bf16[3072,384]{1,0:T(8,128)(2,1)}, u32[]{:S(2)}) %copy-start) | copy-done | bytes 2359320
  2.3 1.4 %convolution_convert_fusion.cond = bf16[64,384]{1,0:T(8,128)(2,1)S(1)} fusion(bf16[3072,384]{1,0:T(8,128)(2,1)S(1)} %copy-done, bf16[1,64,3072]{2,1,0:T(8,128)(2,1)} %param.15), kind=kOutput, calls=%fused_computation | convolution fusion | flops 151019520 | bytes 2801664 | tf_op jit(solution)/shard_map/dot_general | solution.py:654
  3.8 0.0 copy-start.13
  3.8 0.1 pack.1
  3.9 2.9 %collective-permute-start.3 = (bf16[592,384]{1,0:T(8,128)(2,1)S(1)}, bf16[592,384]{1,0:T(8,128)(2,1)S(1)}, u32[]{:S(2)}, u32[]{:S(2)}) collective-permute-start(bf16[592,384]{1,0:T(8,128)(2,1)S(1)} %get-tuple-element.45.refs_0_), channel_id=1, source_target_pairs={{0,24},{1,25},{2,98},{3,99},{4,28},{5,29},{6,102},{7,103},{8,16},{... | collective-permute-start | bytes 1363976 | tf_op jit(solution)/shard_map/ppermute | solution.py:71
  6.8 0.2 collective-permute-start
  7.1 2.0 %collective-permute-start.4 = (bf16[512,384]{1,0:T(8,128)(2,1)S(1)}, bf16[512,384]{1,0:T(8,128)(2,1)S(1)}, u32[]{:S(2)}, u32[]{:S(2)}) collective-permute-start(bf16[512,384]{1,0:T(8,128)(2,1)S(1)} %stack.1.refs_4_.refs_0_), channel_id=1, source_target_pairs={{0,32},{1,33},{2,10},{3,11},{4,36},{5,37},{6,14},{7,15},{8,40},{9,... | collective-permute-start | bytes 1179656 | tf_op jit(solution)/shard_map/ppermute | solution.py:71
  9.1 2.5 %collective-permute-start.1 = (bf16[512,384]{1,0:T(8,128)(2,1)S(1)}, bf16[512,384]{1,0:T(8,128)(2,1)}, u32[]{:S(2)}, u32[]{:S(2)}) collective-permute-start(bf16[512,384]{1,0:T(8,128)(2,1)S(1)} %stack.1.refs_4_.refs_0_), channel_id=1, source_target_pairs={{0,96},{1,97},{2,26},{3,27},{4,100},{5,101},{6,30},{7,31},{8,104},... | collective-permute-start | bytes 1179656 | tf_op jit(solution)/shard_map/ppermute | solution.py:71
  11.6 0.8 copy-done.8
  12.4 1.7 %collective-permute-start.2 = (bf16[80,384]{1,0:T(8,128)(2,1)S(1)}, bf16[80,384]{1,0:T(8,128)(2,1)S(1)}, u32[]{:S(2)}, u32[]{:S(2)}) collective-permute-start(bf16[80,384]{1,0:T(8,128)(2,1)S(1)} %get-tuple-element.46), channel_id=1, source_target_pairs={{0,16},{1,17},{2,66},{3,67},{4,20},{5,21},{6,70},{7,71},{8,24},{9,... | collective-permute-start | bytes 184328 | tf_op jit(solution)/shard_map/ppermute | solution.py:71
  14.1 4.8 %collective-permute-done.2.refs_2_.refs_3_ = bf16[80,384]{1,0:T(8,128)(2,1)S(1)} collective-permute-done((bf16[80,384]{1,0:T(8,128)(2,1)S(1)}, bf16[80,384]{1,0:T(8,128)(2,1)S(1)}, u32[]{:S(2)}, u32[]{:S(2)}) %collective-permute-start.2) | collective-permute-done | bytes 61472 | tf_op jit(solution)/shard_map/ppermute | solution.py:71
  18.8 0.2 collective-permute-done.4.refs_4_.refs_5_.refs_1_
  19.1 0.4 collective-permute-done.refs_0_
  19.5 0.4 copy-done.3
  19.8 3.7 %collective-permute-start.5 = (bf16[592,384]{1,0:T(8,128)(2,1)S(1)}, bf16[592,384]{1,0:T(8,128)(2,1)}, u32[]{:S(2)}, u32[]{:S(2)}) collective-permute-start(bf16[592,384]{1,0:T(8,128)(2,1)S(1)} %get-tuple-element.47.refs_1_), channel_id=1, source_target_pairs={{0,24},{1,25},{2,98},{3,99},{4,28},{5,29},{6,102},{7,103},{8,16},{... | collective-permute-start | bytes 1363976 | tf_op jit(solution)/shard_map/ppermute | solution.py:71
  23.5 1.7 %collective-permute-start.6 = (bf16[512,384]{1,0:T(8,128)(2,1)}, bf16[512,384]{1,0:T(8,128)(2,1)}, u32[]{:S(2)}, u32[]{:S(2)}) collective-permute-start(bf16[512,384]{1,0:T(8,128)(2,1)} %get-tuple-element.53.refs_6_.refs_2_), channel_id=1, source_target_pairs={{0,32},{1,33},{2,10},{3,11},{4,36},{5,37},{6,14},{7,15},{8,40},{9,... | collective-permute-start | bytes 1179656 | tf_op jit(solution)/shard_map/ppermute | solution.py:71
  25.3 0.7 dynamic-slice_bitcast_fusion.info
  26.0 1.0 copy-done.5
  27.0 0.8 tokens.1
  27.8 0.2 copy-done.7
  28.0 0.1 join.1
  28.1 0.4 collective-permute-start.7
  28.5 1.9 %collective-permute-start.8 = (bf16[384,384]{1,0:T(8,128)(2,1)S(1)}, bf16[384,384]{1,0:T(8,128)(2,1)S(1)}, u32[]{:S(2)}, u32[]{:S(2)}) collective-permute-start(bf16[384,384]{1,0:T(8,128)(2,1)S(1)} %get-tuple-element.56), channel_id=1, source_target_pairs={{0,96},{1,97},{2,26},{3,27},{4,100},{5,101},{6,30},{7,31},{8,104},... | collective-permute-start | bytes 884744 | tf_op jit(solution)/shard_map/ppermute | solution.py:71
  30.4 1.9 %collective-permute-start.9 = (bf16[384,384]{1,0:T(8,128)(2,1)S(1)}, bf16[384,384]{1,0:T(8,128)(2,1)S(1)}, u32[]{:S(2)}, u32[]{:S(2)}) collective-permute-start(bf16[384,384]{1,0:T(8,128)(2,1)S(1)} %get-tuple-element.57), channel_id=1, source_target_pairs={{0,64},{1,65},{2,18},{3,19},{4,68},{5,69},{6,22},{7,23},{8,72},{9,... | collective-permute-start | bytes 884744 | tf_op jit(solution)/shard_map/ppermute | solution.py:71
  32.3 3.8 %slopes.1 = (f32[8,3,512,128]{3,2,1,0:T(8,128)S(1)}, bf16[1024,384]{1,0:T(8,128)(2,1)S(1)}) custom-call(s32[64]{0:T(128)S(1)} %dynamic-slice_bitcast_fusion.info, s32[32,128]{1,0:T(8,128)S(1)} %get-tuple-element.52.lists, bf16[592,384]{1,0:T(8,128)(2,1)S(1)} %copy-done.7, bf16[592,384]{1,0:T(8,128)(2,1)S(1)} %get-tuple-element.47.refs_1_, ...), custom_call_target="tpu_custom_call" | custom-call | flops 4600000000 | tf_op jit(solution)/shard_map/slopes/pallas_call | solution.py:432
  36.1 3.5 %collective-permute-done.8.refs_10_ = bf16[384,384]{1,0:T(8,128)(2,1)S(1)} collective-permute-done((bf16[384,384]{1,0:T(8,128)(2,1)S(1)}, bf16[384,384]{1,0:T(8,128)(2,1)S(1)}, u32[]{:S(2)}, u32[]{:S(2)}) %collective-permute-start.8) | collective-permute-done | bytes 294944 | tf_op jit(solution)/shard_map/ppermute | solution.py:71
  39.6 5.3 %scores.1 = (bf16[1024,384]{1,0:T(8,128)(2,1)S(1)}, f32[16,1024]{1,0:T(8,128)S(1)}, bf16[8,3,512,128]{3,2,1,0:T(8,128)(2,1)S(1)}, bf16[2,256,384]{2,1,0:T(8,128)(2,1)S(1)}) custom-call(s32[64]{0:T(128)S(1)} %dynamic-slice_bitcast_fusion.info, s32[32,128]{1,0:T(8,128)S(1)} %get-tuple-element.52.lists, bf16[592,384]{1,0:T(8,128)(2,1)S(1)} %copy-done.7, ...), custom_call_target="tpu_custom_call" | custom-call | flops 5750000128 | tf_op jit(solution)/shard_map/scores/pallas_call | solution.py:432
  44.8 0.7 copy-done.16
  45.6 0.7 collective-permute-start.12
  46.3 1.2 %collective-permute-start.11 = (f32[16,1024]{1,0:T(8,128)S(1)}, f32[16,1024]{1,0:T(8,128)S(1)}, u32[]{:S(2)}, u32[]{:S(2)}) collective-permute-start(f32[16,1024]{1,0:T(8,128)S(1)} %get-tuple-element.59.refs_4_.refs_0_), channel_id=1, source_target_pairs={{0,24},{1,25},{2,98},{3,99},{4,28},{5,29},{6,102},{7,103},{8,16},{... | collective-permute-start | bytes 196616 | tf_op jit(solution)/shard_map/ppermute | solution.py:71
  47.6 1.5 %collective-permute-start.10 = (f32[16,1024]{1,0:T(8,128)S(1)}, f32[16,1024]{1,0:T(8,128)S(1)}, u32[]{:S(2)}, u32[]{:S(2)}) collective-permute-start(f32[16,1024]{1,0:T(8,128)S(1)} %get-tuple-element.59.refs_4_.refs_0_), channel_id=1, source_target_pairs={{0,8},{1,9},{2,34},{3,35},{4,12},{5,13},{6,38},{7,39},{8,0},{9,1},... | collective-permute-start | bytes 196616 | tf_op jit(solution)/shard_map/ppermute | solution.py:71
  49.1 2.2 %turn.1 = (bf16[16,384,128]{2,1,0:T(8,128)(2,1)S(1)}, bf16[16,384,128]{2,1,0:T(8,128)(2,1)S(1)}) custom-call(bf16[512,384]{1,0:T(8,128)(2,1)S(1)} %copy-done.9, bf16[512,384]{1,0:T(8,128)(2,1)S(1)} %copy-done.4, bf16[512,384]{1,0:T(8,128)(2,1)} %get-tuple-element.53.refs_6_.refs_2_, bf16[512,384]{1,0:T(8,128)(2,1)} %collective-permute-done.6.refs_7_.refs_3_, ...), custom_call_target="tpu_custom_call" | custom-call | flops 1380000000 | tf_op jit(solution)/shard_map/turn/pallas_call | solution.py:432
  51.3 0.1 collective-permute-done.12.refs_3_
  51.4 0.7 collective-permute-done.11.refs_2_
  52.1 5.5 %query_grads.1 = (bf16[256,384]{1,0:T(8,128)(2,1)S(1)}, bf16[256,384]{1,0:T(8,128)(2,1)S(1)}, bf16[256,384]{1,0:T(8,128)(2,1)S(1)}, bf16[256,384]{1,0:T(8,128)(2...) custom-call(s32[64]{0:T(128)S(1)} %dynamic-slice_bitcast_fusion.info, ...), custom_call_target="tpu_custom_call" | custom-call | flops 5175000064 | tf_op jit(solution)/shard_map/query_grads/pallas_call | solution.py:432
  57.5 1.3 %collective-permute-start.15 = (bf16[256,384]{1,0:T(8,128)(2,1)S(1)}, bf16[256,384]{1,0:T(8,128)(2,1)S(1)}, u32[]{:S(2)}, u32[]{:S(2)}) collective-permute-start(bf16[256,384]{1,0:T(8,128)(2,1)S(1)} %get-tuple-element.72), channel_id=1, source_target_pairs={{0,8},{1,9},{2,34},{3,35},{4,12},{5,13},{6,38},{7,39},{8,0},{9,1},... | collective-permute-start | bytes 589832 | tf_op jit(solution)/shard_map/ppermute | solution.py:71
  58.8 1.7 %collective-permute-start.16 = (bf16[256,384]{1,0:T(8,128)(2,1)S(1)}, bf16[256,384]{1,0:T(8,128)(2,1)S(1)}, u32[]{:S(2)}, u32[]{:S(2)}) collective-permute-start(bf16[256,384]{1,0:T(8,128)(2,1)S(1)} %get-tuple-element.73), channel_id=1, source_target_pairs={{0,24},{1,25},{2,98},{3,99},{4,28},{5,29},{6,102},{7,103},{8,16},{... | collective-permute-start | bytes 589832 | tf_op jit(solution)/shard_map/ppermute | solution.py:71
  60.5 1.1 %collective-permute-start.17 = (bf16[256,384]{1,0:T(8,128)(2,1)S(1)}, bf16[256,384]{1,0:T(8,128)(2,1)S(1)}, u32[]{:S(2)}, u32[]{:S(2)}) collective-permute-start(bf16[256,384]{1,0:T(8,128)(2,1)S(1)} %get-tuple-element.74), channel_id=1, source_target_pairs={{0,16},{1,17},{2,66},{3,67},{4,20},{5,21},{6,70},{7,71},{8,24},{9,... | collective-permute-start | bytes 589832 | tf_op jit(solution)/shard_map/ppermute | solution.py:71
  61.6 5.3 %key_grads.1 = (bf16[1024,384]{1,0:T(8,128)(2,1)S(1)}, bf16[1024,384]{1,0:T(8,128)(2,1)S(1)}, f32[8,128]{1,0:T(8,128)S(1)}) custom-call(s32[64]{0:T(128)S(1)} %dynamic-slice_bitcast_fusion.info, s32[32,128]{1,0:T(8,128)S(1)} %get-tuple-element.52.lists, bf16[8,3,512,128]{3,2,1,0:T(8,128)(2,1)S(1)} %get-tuple-element.65.probs_in, ...), custom_call_target="tpu_custom_call" | custom-call | flops 5750000128 | tf_op jit(solution)/shard_map/key_grads/pallas_call | solution.py:432
  66.9 0.8 collective-permute-done.16.refs_2_
  67.8 0.0 collective-permute-done.17.refs_3_
  67.8 0.8 sum.2
  68.6 2.3 %collective-permute-start.18 = (bf16[1024,384]{1,0:T(8,128)(2,1)S(1)}, bf16[1024,384]{1,0:T(8,128)(2,1)}, u32[]{:S(2)}, u32[]{:S(2)}) collective-permute-start(bf16[1024,384]{1,0:T(8,128)(2,1)S(1)} %tie.3), channel_id=1, source_target_pairs={{0,32},{1,33},{2,10},{3,11},{4,36},{5,37},{6,14},{7,15},{8,40},{9,... | collective-permute-start | bytes 2359304 | tf_op jit(solution)/shard_map/ppermute | solution.py:71
  70.8 3.1 %collective-permute-start.22 = (bf16[256,384]{1,0:T(8,128)(2,1)}, bf16[256,384]{1,0:T(8,128)(2,1)}, u32[]{:S(2)}, u32[]{:S(2)}) collective-permute-start(bf16[256,384]{1,0:T(8,128)(2,1)} %get-tuple-element.77.refs_0_), channel_id=1, source_target_pairs={{0,64},{1,65},{2,18},{3,19},{4,68},{5,69},{6,22},{7,23},{8,72},{9,... | collective-permute-start | bytes 589832 | tf_op jit(solution)/shard_map/ppermute | solution.py:71
  74.0 0.8 collective-permute-start.20
  74.8 2.4 %collective-permute-start.13 = (bf16[512,384]{1,0:T(8,128)(2,1)}, bf16[512,384]{1,0:T(8,128)(2,1)}, u32[]{:S(2)}, u32[]{:S(2)}) collective-permute-start(bf16[512,384]{1,0:T(8,128)(2,1)} %get-tuple-element.64), channel_id=1, source_target_pairs={{0,24},{1,25},{2,98},{3,99},{4,28},{5,29},{6,102},{7,103},{8,16},{... | collective-permute-start | bytes 1179656 | tf_op jit(solution)/shard_map/ppermute | solution.py:71
  77.2 9.0 %collective-permute-done.22.refs_3_ = bf16[256,384]{1,0:T(8,128)(2,1)} collective-permute-done((bf16[256,384]{1,0:T(8,128)(2,1)}, bf16[256,384]{1,0:T(8,128)(2,1)}, u32[]{:S(2)}, u32[]{:S(2)}) %collective-permute-start.22) | collective-permute-done | bytes 196640 | tf_op jit(solution)/shard_map/ppermute | solution.py:71
  86.1 1.8 %sum.3 = (bf16[256,384]{1,0:T(8,128)(2,1)S(1)}, f32[8,128]{1,0:T(8,128)}) custom-call(bf16[256,384]{1,0:T(8,128)(2,1)} %get-tuple-element.77.refs_0_, bf16[256,384]{1,0:T(8,128)(2,1)} %collective-permute-done.20.refs_1_, bf16[256,384]{1,0:T(8,128)(2,1)} %collective-permute-done.21.refs_2_, bf16[256,384]{1,0:T(8,128)(2,1)} %collective-permute-done.22.refs_3_), custom_call_target="tpu_custom_call" | custom-call | flops 1150000000 | tf_op jit(solution)/shard_map/sum/pallas_call | solution.py:432
  88.0 0.9 weights.1
  88.9 0.6 collective-permute-start.23
  89.5 1.3 %collective-permute-start.24 = (bf16[192,384]{1,0:T(8,128)(2,1)S(1)}, bf16[192,384]{1,0:T(8,128)(2,1)S(1)}, u32[]{:S(2)}, u32[]{:S(2)}) collective-permute-start(bf16[192,384]{1,0:T(8,128)(2,1)S(1)} %get-tuple-element.82), channel_id=1, source_target_pairs={{0,24},{1,25},{2,98},{3,99},{4,28},{5,29},{6,102},{7,103},{8,16},{... | collective-permute-start | bytes 442376 | tf_op jit(solution)/shard_map/ppermute | solution.py:71
  90.9 2.2 %collective-permute-start.25 = (bf16[192,384]{1,0:T(8,128)(2,1)S(1)}, bf16[192,384]{1,0:T(8,128)(2,1)S(1)}, u32[]{:S(2)}, u32[]{:S(2)}) collective-permute-start(bf16[192,384]{1,0:T(8,128)(2,1)S(1)} %get-tuple-element.83), channel_id=1, source_target_pairs={{0,16},{1,17},{2,66},{3,67},{4,20},{5,21},{6,70},{7,71},{8,24},{9,... | collective-permute-start | bytes 442376 | tf_op jit(solution)/shard_map/ppermute | solution.py:71
  93.1 1.0 add_convert_fusion.4
  94.1 0.6 collective-permute-start.14
  94.7 1.1 %add_convert_fusion.refs_4_ = bf16[512,384]{1,0:T(8,128)(2,1)S(1)} fusion(bf16[1024,384]{1,0:T(8,128)(2,1)} %collective-permute-done.18, bf16[1024,384]{1,0:T(8,128)(2,1)S(1)} %copy-done.2), kind=kLoop, calls=%fused_computation.1 | loop fusion | flops 786432 | bytes 1179648 | tf_op jit(solution)/shard_map/convert_element_type | solution.py:86
  95.8 2.7 %collective-permute-start.19 = (bf16[512,384]{1,0:T(8,128)(2,1)S(1)}, bf16[512,384]{1,0:T(8,128)(2,1)S(1)}, u32[]{:S(2)}, u32[]{:S(2)}) collective-permute-start(bf16[512,384]{1,0:T(8,128)(2,1)S(1)} %add_convert_fusion.refs_4_), channel_id=1, source_target_pairs={{0,96},{1,97},{2,26},{3,27},{4,100},{5,101},{6,30},{7,31},{8,104},... | collective-permute-start | bytes 1179656 | tf_op jit(solution)/shard_map/ppermute | solution.py:71
  98.6 0.4 collective-permute-done.24.refs_2_
  99.0 0.1 split.1
  99.1 3.3 %collective-permute-start.26 = (bf16[96,384]{1,0:T(8,128)(2,1)S(1)}, bf16[96,384]{1,0:T(8,128)(2,1)S(1)}, u32[]{:S(2)}, u32[]{:S(2)}) collective-permute-start(bf16[96,384]{1,0:T(8,128)(2,1)S(1)} %get-tuple-element.85), channel_id=1, source_target_pairs={{0,1},{1,0},{2,3},{3,2},{4,5},{5,4},{6,7},{7,6},{8,9},{9,8},{10,11... | collective-permute-start | bytes 221192 | tf_op jit(solution)/shard_map/ppermute | solution.py:680
  102.4 1.7 %fusion = bf16[1,256,384]{2,1,0:T(8,128)(2,1)} fusion(bf16[256,384]{1,0:T(8,128)(2,1)S(1)} %collective-permute-done.14, bf16[512,384]{1,0:T(8,128)(2,1)} %collective-permute-done.13, bf16[512,384]{1,0:T(8,128)(2,1)S(1)} %get-tuple-element.63), kind=kLoop, calls=%fused_computation.6 | loop fusion | flops 589824 | bytes 786432 | tf_op jit(solution)/shard_map/broadcast_in_dim | solution.py:681
  104.1 1.0 collective-permute-done.26
  105.1 0.7 convert_add_fusion
  105.7 1.9 %fusion.2 = (bf16[1,256,384]{2,1,0:T(8,128)(2,1)}, bf16[1,256,384]{2,1,0:T(8,128)(2,1)}) fusion(bf16[512,384]{1,0:T(8,128)(2,1)S(1)} %collective-permute-done.19, bf16[1024,384]{1,0:T(8,128)(2,1)} %collective-permute-done.18, bf16[1024,384]{1,0:T(8,128)(2,1)S(1)} %copy-done.2), kind=kLoop, calls=%fused_computation.8 | loop fusion | flops 1179648 | bytes 1572864 | tf_op jit(solution)/shard_map/broadcast_in_dim | solution.py:683
  (48 shorter events, 0.1 us)
Async XLA Ops:
  0.6 1.7 %copy-start = (bf16[3072,384]{1,0:T(8,128)(2,1)S(1)}, bf16[3072,384]{1,0:T(8,128)(2,1)}, u32[]{:S(2)}) copy-start(bf16[3072,384]{1,0:T(8,128)(2,1)} %param.16) | copy-start | bytes 7077892
  0.6 3.1 %copy-start.15 = (s32[4,2]{0,1:T(2,128)S(1)}, s32[4,2]{0,1:T(2,128)}, u32[]{:S(2)}) copy-start(s32[4,2]{0,1:T(2,128)} %param.14) | copy-start | bytes 100
  0.7 3.1 %copy-start.14 = (s32[4,32]{1,0:T(4,128)S(1)}, s32[4,32]{1,0:T(4,128)}, u32[]{:S(2)}) copy-start(s32[4,32]{1,0:T(4,128)} %kv_list.1) | copy-start | bytes 1540
  0.7 3.1 %copy-start.11 = (bf16[1,256,384]{2,1,0:T(8,128)(2,1)S(1)}, bf16[1,256,384]{2,1,0:T(8,128)(2,1)}, u32[]{:S(2)}) copy-start(bf16[1,256,384]{2,1,0:T(8,128)(2,1)} %param.12) | copy-start | bytes 589828
  0.7 3.1 %copy-start.10 = (bf16[1,256,384]{2,1,0:T(8,128)(2,1)S(1)}, bf16[1,256,384]{2,1,0:T(8,128)(2,1)}, u32[]{:S(2)}) copy-start(bf16[1,256,384]{2,1,0:T(8,128)(2,1)} %param.9) | copy-start | bytes 589828
  3.8 3.3 %copy-start.12 = (bf16[1,256,384]{2,1,0:T(8,128)(2,1)S(1)}, bf16[1,256,384]{2,1,0:T(8,128)(2,1)}, u32[]{:S(2)}) copy-start(bf16[1,256,384]{2,1,0:T(8,128)(2,1)} %param.10) | copy-start | bytes 589828
  3.8 3.3 %copy-start.13 = (bf16[1,256,384]{2,1,0:T(8,128)(2,1)S(1)}, bf16[1,256,384]{2,1,0:T(8,128)(2,1)}, u32[]{:S(2)}) copy-start(bf16[1,256,384]{2,1,0:T(8,128)(2,1)} %param.11) | copy-start | bytes 589828
  3.9 15.2 %copy-start.6 = (bf16[592,384]{1,0:T(8,128)(2,1)}, bf16[592,384]{1,0:T(8,128)(2,1)S(1)}, u32[]{:S(2)}) copy-start(bf16[592,384]{1,0:T(8,128)(2,1)S(1)} %get-tuple-element.45.refs_0_) | copy-start | bytes 1363972
  3.9 15.2 %collective-permute-start.3 = (bf16[592,384]{1,0:T(8,128)(2,1)S(1)}, bf16[592,384]{1,0:T(8,128)(2,1)S(1)}, u32[]{:S(2)}, u32[]{:S(2)}) collective-permute-start(bf16[592,384]{1,0:T(8,128)(2,1)S(1)} %get-tuple-element.45.refs_0_), channel_id=1, source_target_pairs={{0,24},{1,25},{2,98},{3,99},{4,28},{5,29},{6,102},{7,103},{8,16},{... | collective-permute-start | bytes 1363976 | tf_op jit(solution)/shard_map/ppermute | solution.py:71
  6.8 12.6 %collective-permute-start = (bf16[592,384]{1,0:T(8,128)(2,1)S(1)}, bf16[592,384]{1,0:T(8,128)(2,1)S(1)}, u32[]{:S(2)}, u32[]{:S(2)}) collective-permute-start(bf16[592,384]{1,0:T(8,128)(2,1)S(1)} %get-tuple-element.45.refs_0_), channel_id=1, source_target_pairs={{0,8},{1,9},{2,34},{3,35},{4,12},{5,13},{6,38},{7,39},{8,0},{9,1},... | collective-permute-start | bytes 1363976 | tf_op jit(solution)/shard_map/ppermute | solution.py:71
  7.1 12.0 %collective-permute-start.4 = (bf16[512,384]{1,0:T(8,128)(2,1)S(1)}, bf16[512,384]{1,0:T(8,128)(2,1)S(1)}, u32[]{:S(2)}, u32[]{:S(2)}) collective-permute-start(bf16[512,384]{1,0:T(8,128)(2,1)S(1)} %stack.1.refs_4_.refs_0_), channel_id=1, source_target_pairs={{0,32},{1,33},{2,10},{3,11},{4,36},{5,37},{6,14},{7,15},{8,40},{9,... | collective-permute-start | bytes 1179656 | tf_op jit(solution)/shard_map/ppermute | solution.py:71
  9.1 10.0 %collective-permute-start.1 = (bf16[512,384]{1,0:T(8,128)(2,1)S(1)}, bf16[512,384]{1,0:T(8,128)(2,1)}, u32[]{:S(2)}, u32[]{:S(2)}) collective-permute-start(bf16[512,384]{1,0:T(8,128)(2,1)S(1)} %stack.1.refs_4_.refs_0_), channel_id=1, source_target_pairs={{0,96},{1,97},{2,26},{3,27},{4,100},{5,101},{6,30},{7,31},{8,104},... | collective-permute-start | bytes 1179656 | tf_op jit(solution)/shard_map/ppermute | solution.py:71
  11.6 0.8 copy-start.8
  12.4 6.5 %collective-permute-start.2 = (bf16[80,384]{1,0:T(8,128)(2,1)S(1)}, bf16[80,384]{1,0:T(8,128)(2,1)S(1)}, u32[]{:S(2)}, u32[]{:S(2)}) collective-permute-start(bf16[80,384]{1,0:T(8,128)(2,1)S(1)} %get-tuple-element.46), channel_id=1, source_target_pairs={{0,16},{1,17},{2,66},{3,67},{4,20},{5,21},{6,70},{7,71},{8,24},{9,... | collective-permute-start | bytes 184328 | tf_op jit(solution)/shard_map/ppermute | solution.py:71
  19.1 0.8 copy-start.3
  19.8 12.5 %collective-permute-start.5 = (bf16[592,384]{1,0:T(8,128)(2,1)S(1)}, bf16[592,384]{1,0:T(8,128)(2,1)}, u32[]{:S(2)}, u32[]{:S(2)}) collective-permute-start(bf16[592,384]{1,0:T(8,128)(2,1)S(1)} %get-tuple-element.47.refs_1_), channel_id=1, source_target_pairs={{0,24},{1,25},{2,98},{3,99},{4,28},{5,29},{6,102},{7,103},{8,16},{... | collective-permute-start | bytes 1363976 | tf_op jit(solution)/shard_map/ppermute | solution.py:71
  23.5 8.7 %collective-permute-start.6 = (bf16[512,384]{1,0:T(8,128)(2,1)}, bf16[512,384]{1,0:T(8,128)(2,1)}, u32[]{:S(2)}, u32[]{:S(2)}) collective-permute-start(bf16[512,384]{1,0:T(8,128)(2,1)} %get-tuple-element.53.refs_6_.refs_2_), channel_id=1, source_target_pairs={{0,32},{1,33},{2,10},{3,11},{4,36},{5,37},{6,14},{7,15},{8,40},{9,... | collective-permute-start | bytes 1179656 | tf_op jit(solution)/shard_map/ppermute | solution.py:71
  26.0 1.0 copy-start.5
  27.0 1.0 copy-start.7
  27.8 4.5 %copy-start.4 = (bf16[512,384]{1,0:T(8,128)(2,1)S(1)}, bf16[512,384]{1,0:T(8,128)(2,1)}, u32[]{:S(2)}) copy-start(bf16[512,384]{1,0:T(8,128)(2,1)} %copy-done.3) | copy-start | bytes 1179652
  27.8 4.5 %copy-start.9 = (bf16[512,384]{1,0:T(8,128)(2,1)S(1)}, bf16[512,384]{1,0:T(8,128)(2,1)}, u32[]{:S(2)}) copy-start(bf16[512,384]{1,0:T(8,128)(2,1)} %copy-done.8) | copy-start | bytes 1179652
  28.1 8.0 %collective-permute-start.7 = (bf16[384,384]{1,0:T(8,128)(2,1)S(1)}, bf16[384,384]{1,0:T(8,128)(2,1)S(1)}, u32[]{:S(2)}, u32[]{:S(2)}) collective-permute-start(bf16[384,384]{1,0:T(8,128)(2,1)S(1)} %get-tuple-element.55), channel_id=1, source_target_pairs={{0,32},{1,33},{2,10},{3,11},{4,36},{5,37},{6,14},{7,15},{8,40},{9,... | collective-permute-start | bytes 884744 | tf_op jit(solution)/shard_map/ppermute | solution.py:71
  28.5 11.1 %collective-permute-start.8 = (bf16[384,384]{1,0:T(8,128)(2,1)S(1)}, bf16[384,384]{1,0:T(8,128)(2,1)S(1)}, u32[]{:S(2)}, u32[]{:S(2)}) collective-permute-start(bf16[384,384]{1,0:T(8,128)(2,1)S(1)} %get-tuple-element.56), channel_id=1, source_target_pairs={{0,96},{1,97},{2,26},{3,27},{4,100},{5,101},{6,30},{7,31},{8,104},... | collective-permute-start | bytes 884744 | tf_op jit(solution)/shard_map/ppermute | solution.py:71
  30.4 9.2 %collective-permute-start.9 = (bf16[384,384]{1,0:T(8,128)(2,1)S(1)}, bf16[384,384]{1,0:T(8,128)(2,1)S(1)}, u32[]{:S(2)}, u32[]{:S(2)}) collective-permute-start(bf16[384,384]{1,0:T(8,128)(2,1)S(1)} %get-tuple-element.57), channel_id=1, source_target_pairs={{0,64},{1,65},{2,18},{3,19},{4,68},{5,69},{6,22},{7,23},{8,72},{9,... | collective-permute-start | bytes 884744 | tf_op jit(solution)/shard_map/ppermute | solution.py:71
  44.8 0.7 copy-start.16
  45.6 5.8 %collective-permute-start.12 = (f32[16,1024]{1,0:T(8,128)S(1)}, f32[16,1024]{1,0:T(8,128)S(1)}, u32[]{:S(2)}, u32[]{:S(2)}) collective-permute-start(f32[16,1024]{1,0:T(8,128)S(1)} %get-tuple-element.59.refs_4_.refs_0_), channel_id=1, source_target_pairs={{0,16},{1,17},{2,66},{3,67},{4,20},{5,21},{6,70},{7,71},{8,24},{9,... | collective-permute-start | bytes 196616 | tf_op jit(solution)/shard_map/ppermute | solution.py:71
  46.3 5.7 %collective-permute-start.11 = (f32[16,1024]{1,0:T(8,128)S(1)}, f32[16,1024]{1,0:T(8,128)S(1)}, u32[]{:S(2)}, u32[]{:S(2)}) collective-permute-start(f32[16,1024]{1,0:T(8,128)S(1)} %get-tuple-element.59.refs_4_.refs_0_), channel_id=1, source_target_pairs={{0,24},{1,25},{2,98},{3,99},{4,28},{5,29},{6,102},{7,103},{8,16},{... | collective-permute-start | bytes 196616 | tf_op jit(solution)/shard_map/ppermute | solution.py:71
  47.6 4.5 %collective-permute-start.10 = (f32[16,1024]{1,0:T(8,128)S(1)}, f32[16,1024]{1,0:T(8,128)S(1)}, u32[]{:S(2)}, u32[]{:S(2)}) collective-permute-start(f32[16,1024]{1,0:T(8,128)S(1)} %get-tuple-element.59.refs_4_.refs_0_), channel_id=1, source_target_pairs={{0,8},{1,9},{2,34},{3,35},{4,12},{5,13},{6,38},{7,39},{8,0},{9,1},... | collective-permute-start | bytes 196616 | tf_op jit(solution)/shard_map/ppermute | solution.py:71
  57.5 9.4 %collective-permute-start.15 = (bf16[256,384]{1,0:T(8,128)(2,1)S(1)}, bf16[256,384]{1,0:T(8,128)(2,1)S(1)}, u32[]{:S(2)}, u32[]{:S(2)}) collective-permute-start(bf16[256,384]{1,0:T(8,128)(2,1)S(1)} %get-tuple-element.72), channel_id=1, source_target_pairs={{0,8},{1,9},{2,34},{3,35},{4,12},{5,13},{6,38},{7,39},{8,0},{9,1},... | collective-permute-start | bytes 589832 | tf_op jit(solution)/shard_map/ppermute | solution.py:71
  58.8 9.0 %collective-permute-start.16 = (bf16[256,384]{1,0:T(8,128)(2,1)S(1)}, bf16[256,384]{1,0:T(8,128)(2,1)S(1)}, u32[]{:S(2)}, u32[]{:S(2)}) collective-permute-start(bf16[256,384]{1,0:T(8,128)(2,1)S(1)} %get-tuple-element.73), channel_id=1, source_target_pairs={{0,24},{1,25},{2,98},{3,99},{4,28},{5,29},{6,102},{7,103},{8,16},{... | collective-permute-start | bytes 589832 | tf_op jit(solution)/shard_map/ppermute | solution.py:71
  60.5 7.3 %collective-permute-start.17 = (bf16[256,384]{1,0:T(8,128)(2,1)S(1)}, bf16[256,384]{1,0:T(8,128)(2,1)S(1)}, u32[]{:S(2)}, u32[]{:S(2)}) collective-permute-start(bf16[256,384]{1,0:T(8,128)(2,1)S(1)} %get-tuple-element.74), channel_id=1, source_target_pairs={{0,16},{1,17},{2,66},{3,67},{4,20},{5,21},{6,70},{7,71},{8,24},{9,... | collective-permute-start | bytes 589832 | tf_op jit(solution)/shard_map/ppermute | solution.py:71
  66.9 1.7 %copy-start.1 = (bf16[1024,384]{1,0:T(8,128)(2,1)}, bf16[1024,384]{1,0:T(8,128)(2,1)S(1)}, u32[]{:S(2)}) copy-start(bf16[1024,384]{1,0:T(8,128)(2,1)S(1)} %get-tuple-element.69) | copy-start | bytes 2359300
  68.6 26.1 %collective-permute-start.18 = (bf16[1024,384]{1,0:T(8,128)(2,1)S(1)}, bf16[1024,384]{1,0:T(8,128)(2,1)}, u32[]{:S(2)}, u32[]{:S(2)}) collective-permute-start(bf16[1024,384]{1,0:T(8,128)(2,1)S(1)} %tie.3), channel_id=1, source_target_pairs={{0,32},{1,33},{2,10},{3,11},{4,36},{5,37},{6,14},{7,15},{8,40},{9,... | collective-permute-start | bytes 2359304 | tf_op jit(solution)/shard_map/ppermute | solution.py:71
  70.8 15.3 %collective-permute-start.22 = (bf16[256,384]{1,0:T(8,128)(2,1)}, bf16[256,384]{1,0:T(8,128)(2,1)}, u32[]{:S(2)}, u32[]{:S(2)}) collective-permute-start(bf16[256,384]{1,0:T(8,128)(2,1)} %get-tuple-element.77.refs_0_), channel_id=1, source_target_pairs={{0,64},{1,65},{2,18},{3,19},{4,68},{5,69},{6,22},{7,23},{8,72},{9,... | collective-permute-start | bytes 589832 | tf_op jit(solution)/shard_map/ppermute | solution.py:71
  74.0 12.2 %collective-permute-start.21 = (bf16[256,384]{1,0:T(8,128)(2,1)}, bf16[256,384]{1,0:T(8,128)(2,1)}, u32[]{:S(2)}, u32[]{:S(2)}) collective-permute-start(bf16[256,384]{1,0:T(8,128)(2,1)} %get-tuple-element.77.refs_0_), channel_id=1, source_target_pairs={{0,96},{1,97},{2,26},{3,27},{4,100},{5,101},{6,30},{7,31},{8,104},... | collective-permute-start | bytes 589832 | tf_op jit(solution)/shard_map/ppermute | solution.py:71
  74.0 12.2 %collective-permute-start.20 = (bf16[256,384]{1,0:T(8,128)(2,1)}, bf16[256,384]{1,0:T(8,128)(2,1)}, u32[]{:S(2)}, u32[]{:S(2)}) collective-permute-start(bf16[256,384]{1,0:T(8,128)(2,1)} %get-tuple-element.77.refs_0_), channel_id=1, source_target_pairs={{0,32},{1,33},{2,10},{3,11},{4,36},{5,37},{6,14},{7,15},{8,40},{9,... | collective-permute-start | bytes 589832 | tf_op jit(solution)/shard_map/ppermute | solution.py:71
  74.8 18.3 %collective-permute-start.13 = (bf16[512,384]{1,0:T(8,128)(2,1)}, bf16[512,384]{1,0:T(8,128)(2,1)}, u32[]{:S(2)}, u32[]{:S(2)}) collective-permute-start(bf16[512,384]{1,0:T(8,128)(2,1)} %get-tuple-element.64), channel_id=1, source_target_pairs={{0,24},{1,25},{2,98},{3,99},{4,28},{5,29},{6,102},{7,103},{8,16},{... | collective-permute-start | bytes 1179656 | tf_op jit(solution)/shard_map/ppermute | solution.py:71
  77.2 10.8 %copy-start.17 = (bf16[2,256,384]{2,1,0:T(8,128)(2,1)S(1)}, bf16[2,256,384]{2,1,0:T(8,128)(2,1)}, u32[]{:S(2)}) copy-start(bf16[2,256,384]{2,1,0:T(8,128)(2,1)} %copy-done.16) | copy-start | bytes 1179652
  88.0 6.8 %copy-start.2 = (bf16[1024,384]{1,0:T(8,128)(2,1)S(1)}, bf16[1024,384]{1,0:T(8,128)(2,1)}, u32[]{:S(2)}) copy-start(bf16[1024,384]{1,0:T(8,128)(2,1)} %copy-done.1) | copy-start | bytes 2359300
  88.9 9.6 %collective-permute-start.23 = (bf16[192,384]{1,0:T(8,128)(2,1)S(1)}, bf16[192,384]{1,0:T(8,128)(2,1)S(1)}, u32[]{:S(2)}, u32[]{:S(2)}) collective-permute-start(bf16[192,384]{1,0:T(8,128)(2,1)S(1)} %get-tuple-element.81), channel_id=1, source_target_pairs={{0,8},{1,9},{2,34},{3,35},{4,12},{5,13},{6,38},{7,39},{8,0},{9,1},... | collective-permute-start | bytes 442376 | tf_op jit(solution)/shard_map/ppermute | solution.py:71
  89.5 9.5 %collective-permute-start.24 = (bf16[192,384]{1,0:T(8,128)(2,1)S(1)}, bf16[192,384]{1,0:T(8,128)(2,1)S(1)}, u32[]{:S(2)}, u32[]{:S(2)}) collective-permute-start(bf16[192,384]{1,0:T(8,128)(2,1)S(1)} %get-tuple-element.82), channel_id=1, source_target_pairs={{0,24},{1,25},{2,98},{3,99},{4,28},{5,29},{6,102},{7,103},{8,16},{... | collective-permute-start | bytes 442376 | tf_op jit(solution)/shard_map/ppermute | solution.py:71
  90.9 8.1 %collective-permute-start.25 = (bf16[192,384]{1,0:T(8,128)(2,1)S(1)}, bf16[192,384]{1,0:T(8,128)(2,1)S(1)}, u32[]{:S(2)}, u32[]{:S(2)}) collective-permute-start(bf16[192,384]{1,0:T(8,128)(2,1)S(1)} %get-tuple-element.83), channel_id=1, source_target_pairs={{0,16},{1,17},{2,66},{3,67},{4,20},{5,21},{6,70},{7,71},{8,24},{9,... | collective-permute-start | bytes 442376 | tf_op jit(solution)/shard_map/ppermute | solution.py:71
  94.1 8.3 %collective-permute-start.14 = (bf16[256,384]{1,0:T(8,128)(2,1)S(1)}, bf16[256,384]{1,0:T(8,128)(2,1)S(1)}, u32[]{:S(2)}, u32[]{:S(2)}) collective-permute-start(bf16[256,384]{1,0:T(8,128)(2,1)S(1)} %add_convert_fusion.4), channel_id=1, source_target_pairs={{0,8},{1,9},{2,34},{3,35},{4,12},{5,13},{6,38},{7,39},{8,0},{9,1},... | collective-permute-start | bytes 589832 | tf_op jit(solution)/shard_map/ppermute | solution.py:71
  95.8 9.9 %collective-permute-start.19 = (bf16[512,384]{1,0:T(8,128)(2,1)S(1)}, bf16[512,384]{1,0:T(8,128)(2,1)S(1)}, u32[]{:S(2)}, u32[]{:S(2)}) collective-permute-start(bf16[512,384]{1,0:T(8,128)(2,1)S(1)} %add_convert_fusion.refs_4_), channel_id=1, source_target_pairs={{0,96},{1,97},{2,26},{3,27},{4,100},{5,101},{6,30},{7,31},{8,104},... | collective-permute-start | bytes 1179656 | tf_op jit(solution)/shard_map/ppermute | solution.py:71
  99.1 5.9 %collective-permute-start.26 = (bf16[96,384]{1,0:T(8,128)(2,1)S(1)}, bf16[96,384]{1,0:T(8,128)(2,1)S(1)}, u32[]{:S(2)}, u32[]{:S(2)}) collective-permute-start(bf16[96,384]{1,0:T(8,128)(2,1)S(1)} %get-tuple-element.85), channel_id=1, source_target_pairs={{0,1},{1,0},{2,3},{3,2},{4,5},{5,4},{6,7},{7,6},{8,9},{9,8},{10,11... | collective-permute-start | bytes 221192 | tf_op jit(solution)/shard_map/ppermute | solution.py:680

commit v4 on v3

--- a/solution.py
+++ b/solution.py
@@ -671,9 +671,8 @@
     cg = scattered(cg, "u")
     dkv = key_call(info, lists, probs, score, qeff, grads)
     cg, flag = sum_call(cg, [dkv[2]])
-    cg = sum_call(gathered(cg, "v"), [])[0]
-    (away,) = tied([dkv[1]], [flag])
-    dkv, on = halved(dkv[0], away, "v", 1, 3)
+    cg = summed(gathered(cg, "v")).astype(BF16)
+    dkv, on = halved(dkv[0], dkv[1], "v", 1, 3)
     dq, dq_on = halved(dq[0], dq[1], "u", 3, 1)
     weight = scattered(weight_call(info, cg, tokens), "u")
     mine, other = split_call(lax.axis_index("dp").reshape(1), weight, [on])

time: 109 us -> 107 us (0.982)
  waiting for transfers between devices: 20.9 us -> 16.1 us
  starting transfers between devices: 46 us -> 47.9 us
  other arithmetic: 6.34 us -> 7.65 us
    ppermute x26, waiting for transfers between devices: 19.9 us -> 15.1 us  [send(): return lax.ppermute(array, ('ctx', 'head', 'dp'), pairs)]
    ppermute x26, starting transfers between devices: 42.7 us -> 44.7 us  [send(): return lax.ppermute(array, ('ctx', 'head', 'dp'), pairs)]
    convert_element_type x0 -> x1, other arithmetic: none -> 1.32 us  [body(): cg = summed(gathered(cg, 'v')).astype(BF16)]
    unnamed x36 -> x32, local copies, waits for them, and re-layouts: 4.7 us -> 5.64 us
    pallas_call x15 -> x13, Pallas kernels: 26.7 us -> 25.7 us  [call(): pl.pallas_call(kernel, name=name, grid=grid, out_shape=[jax.ShapeDtypeStr...]
  transfers between devices with their start and end apart: 27 -> 27, of which waited for: 10 -> 10; matrix products, arithmetic and copies ran while one was open for 5% -> 6% of each run, Pallas kernels for 14% -> 13%
where the time goes in v4:
time: 107 us; the launch traced here: 106 us
  starting transfers between devices  47.9 us (45%)
  Pallas kernels  25.7 us (24%)
  waiting for transfers between devices  16.1 us (15%)
  other arithmetic  7.65 us (7%)
  local copies, waits for them, and re-layouts  6.34 us (6%)
  matrix products  1.44 us (1%)
    ppermute x26, starting transfers between devices, send(): return lax.ppermute(array, ('ctx', 'head', 'dp'), pairs)  44.7 us
    pallas_call x13, Pallas kernels, call(): pl.pallas_call(kernel, name=name, grid=grid, out_shape=[jax.ShapeDtypeStr...  25.7 us
    ppermute x26, waiting for transfers between devices, send(): return lax.ppermute(array, ('ctx', 'head', 'dp'), pairs)  15.1 us
    unnamed x32, local copies, waits for them, and re-layouts  5.64 us
    ppermute x1, starting transfers between devices, body(): lax.ppermute(other, 'dp', [(0, 1), (1, 0)]).astype(F32)  3.28 us
  transfers between devices with their start and end apart: 27, of which 10 were waited for; matrix products, arithmetic and copies ran while one was open for 6% of the time, Pallas kernels for 13%

profile of v4, /device:TPU:0, one launch (start us, length us, event | category | flops | bytes accessed | tf_op | source)
XLA Modules:
  0.0 106.1 jit_solution(7652839590761949817)
XLA Ops:
  0.6 0.0 copy-start
  0.7 1.6 %copy-done = bf16[3072,384]{1,0:T(8,128)(2,1)S(1)} copy-done((bf16[3072,384]{1,0:T(8,128)(2,1)S(1)}, bf16[3072,384]{1,0:T(8,128)(2,1)}, u32[]{:S(2)}) %copy-start) | copy-done | bytes 2359320
  2.3 1.4 %convolution_convert_fusion.cond = bf16[64,384]{1,0:T(8,128)(2,1)S(1)} fusion(bf16[3072,384]{1,0:T(8,128)(2,1)S(1)} %copy-done, bf16[1,64,3072]{2,1,0:T(8,128)(2,1)} %param.15), kind=kOutput, calls=%fused_computation | convolution fusion | flops 151019520 | bytes 2801664 | tf_op jit(solution)/shard_map/dot_general | solution.py:654
  3.8 0.0 copy-start.10
  3.8 0.1 pack.1
  3.9 2.9 %collective-permute-start.3 = (bf16[592,384]{1,0:T(8,128)(2,1)S(1)}, bf16[592,384]{1,0:T(8,128)(2,1)S(1)}, u32[]{:S(2)}, u32[]{:S(2)}) collective-permute-start(bf16[592,384]{1,0:T(8,128)(2,1)S(1)} %get-tuple-element.43.refs_0_), channel_id=1, source_target_pairs={{0,24},{1,25},{2,98},{3,99},{4,28},{5,29},{6,102},{7,103},{8,16},{... | collective-permute-start | bytes 1363976 | tf_op jit(solution)/shard_map/ppermute | solution.py:71
  6.8 0.2 collective-permute-start
  7.1 2.0 %collective-permute-start.4 = (bf16[512,384]{1,0:T(8,128)(2,1)S(1)}, bf16[512,384]{1,0:T(8,128)(2,1)S(1)}, u32[]{:S(2)}, u32[]{:S(2)}) collective-permute-start(bf16[512,384]{1,0:T(8,128)(2,1)S(1)} %stack.1.refs_4_.refs_0_), channel_id=1, source_target_pairs={{0,32},{1,33},{2,10},{3,11},{4,36},{5,37},{6,14},{7,15},{8,40},{9,... | collective-permute-start | bytes 1179656 | tf_op jit(solution)/shard_map/ppermute | solution.py:71
  9.1 2.5 %collective-permute-start.1 = (bf16[512,384]{1,0:T(8,128)(2,1)S(1)}, bf16[512,384]{1,0:T(8,128)(2,1)}, u32[]{:S(2)}, u32[]{:S(2)}) collective-permute-start(bf16[512,384]{1,0:T(8,128)(2,1)S(1)} %stack.1.refs_4_.refs_0_), channel_id=1, source_target_pairs={{0,96},{1,97},{2,26},{3,27},{4,100},{5,101},{6,30},{7,31},{8,104},... | collective-permute-start | bytes 1179656 | tf_op jit(solution)/shard_map/ppermute | solution.py:71
  11.6 0.7 copy-done.6
  12.3 1.7 %collective-permute-start.2 = (bf16[80,384]{1,0:T(8,128)(2,1)S(1)}, bf16[80,384]{1,0:T(8,128)(2,1)S(1)}, u32[]{:S(2)}, u32[]{:S(2)}) collective-permute-start(bf16[80,384]{1,0:T(8,128)(2,1)S(1)} %get-tuple-element.44), channel_id=1, source_target_pairs={{0,16},{1,17},{2,66},{3,67},{4,20},{5,21},{6,70},{7,71},{8,24},{9,... | collective-permute-start | bytes 184328 | tf_op jit(solution)/shard_map/ppermute | solution.py:71
  14.1 4.8 %collective-permute-done.2.refs_2_.refs_3_ = bf16[80,384]{1,0:T(8,128)(2,1)S(1)} collective-permute-done((bf16[80,384]{1,0:T(8,128)(2,1)S(1)}, bf16[80,384]{1,0:T(8,128)(2,1)S(1)}, u32[]{:S(2)}, u32[]{:S(2)}) %collective-permute-start.2) | collective-permute-done | bytes 61472 | tf_op jit(solution)/shard_map/ppermute | solution.py:71
  18.8 0.2 collective-permute-done.4.refs_4_.refs_5_.refs_1_
  19.1 0.4 collective-permute-done.refs_0_
  19.5 0.4 copy-done.1
  19.8 3.7 %collective-permute-start.5 = (bf16[592,384]{1,0:T(8,128)(2,1)S(1)}, bf16[592,384]{1,0:T(8,128)(2,1)}, u32[]{:S(2)}, u32[]{:S(2)}) collective-permute-start(bf16[592,384]{1,0:T(8,128)(2,1)S(1)} %get-tuple-element.45.refs_1_), channel_id=1, source_target_pairs={{0,24},{1,25},{2,98},{3,99},{4,28},{5,29},{6,102},{7,103},{8,16},{... | collective-permute-start | bytes 1363976 | tf_op jit(solution)/shard_map/ppermute | solution.py:71
  23.5 1.7 %collective-permute-start.6 = (bf16[512,384]{1,0:T(8,128)(2,1)}, bf16[512,384]{1,0:T(8,128)(2,1)}, u32[]{:S(2)}, u32[]{:S(2)}) collective-permute-start(bf16[512,384]{1,0:T(8,128)(2,1)} %get-tuple-element.51.refs_6_.refs_2_), channel_id=1, source_target_pairs={{0,32},{1,33},{2,10},{3,11},{4,36},{5,37},{6,14},{7,15},{8,40},{9,... | collective-permute-start | bytes 1179656 | tf_op jit(solution)/shard_map/ppermute | solution.py:71
  25.3 0.7 dynamic-slice_bitcast_fusion.info
  26.0 1.0 copy-done.3
  27.0 0.8 tokens.1
  27.8 0.2 copy-done.5
  28.0 0.1 join.1
  28.1 0.4 collective-permute-start.7
  28.5 1.9 %collective-permute-start.8 = (bf16[384,384]{1,0:T(8,128)(2,1)S(1)}, bf16[384,384]{1,0:T(8,128)(2,1)S(1)}, u32[]{:S(2)}, u32[]{:S(2)}) collective-permute-start(bf16[384,384]{1,0:T(8,128)(2,1)S(1)} %get-tuple-element.54), channel_id=1, source_target_pairs={{0,96},{1,97},{2,26},{3,27},{4,100},{5,101},{6,30},{7,31},{8,104},... | collective-permute-start | bytes 884744 | tf_op jit(solution)/shard_map/ppermute | solution.py:71
  30.4 1.9 %collective-permute-start.9 = (bf16[384,384]{1,0:T(8,128)(2,1)S(1)}, bf16[384,384]{1,0:T(8,128)(2,1)S(1)}, u32[]{:S(2)}, u32[]{:S(2)}) collective-permute-start(bf16[384,384]{1,0:T(8,128)(2,1)S(1)} %get-tuple-element.55), channel_id=1, source_target_pairs={{0,64},{1,65},{2,18},{3,19},{4,68},{5,69},{6,22},{7,23},{8,72},{9,... | collective-permute-start | bytes 884744 | tf_op jit(solution)/shard_map/ppermute | solution.py:71
  32.3 3.8 %slopes.1 = (f32[8,3,512,128]{3,2,1,0:T(8,128)S(1)}, bf16[1024,384]{1,0:T(8,128)(2,1)S(1)}) custom-call(s32[64]{0:T(128)S(1)} %dynamic-slice_bitcast_fusion.info, s32[32,128]{1,0:T(8,128)S(1)} %get-tuple-element.50.lists, bf16[592,384]{1,0:T(8,128)(2,1)S(1)} %copy-done.5, bf16[592,384]{1,0:T(8,128)(2,1)S(1)} %get-tuple-element.45.refs_1_, ...), custom_call_target="tpu_custom_call" | custom-call | flops 4600000000 | tf_op jit(solution)/shard_map/slopes/pallas_call | solution.py:432
  36.0 3.5 %collective-permute-done.8.refs_10_ = bf16[384,384]{1,0:T(8,128)(2,1)S(1)} collective-permute-done((bf16[384,384]{1,0:T(8,128)(2,1)S(1)}, bf16[384,384]{1,0:T(8,128)(2,1)S(1)}, u32[]{:S(2)}, u32[]{:S(2)}) %collective-permute-start.8) | collective-permute-done | bytes 294944 | tf_op jit(solution)/shard_map/ppermute | solution.py:71
  39.5 5.3 %scores.1 = (bf16[1024,384]{1,0:T(8,128)(2,1)S(1)}, f32[16,1024]{1,0:T(8,128)S(1)}, bf16[8,3,512,128]{3,2,1,0:T(8,128)(2,1)S(1)}, bf16[2,256,384]{2,1,0:T(8,128)(2,1)S(1)}) custom-call(s32[64]{0:T(128)S(1)} %dynamic-slice_bitcast_fusion.info, s32[32,128]{1,0:T(8,128)S(1)} %get-tuple-element.50.lists, bf16[592,384]{1,0:T(8,128)(2,1)S(1)} %copy-done.5, ...), custom_call_target="tpu_custom_call" | custom-call | flops 5750000128 | tf_op jit(solution)/shard_map/scores/pallas_call | solution.py:432
  44.8 0.7 copy-done.14
  45.6 0.7 collective-permute-start.12
  46.3 1.2 %collective-permute-start.11 = (f32[16,1024]{1,0:T(8,128)S(1)}, f32[16,1024]{1,0:T(8,128)S(1)}, u32[]{:S(2)}, u32[]{:S(2)}) collective-permute-start(f32[16,1024]{1,0:T(8,128)S(1)} %get-tuple-element.57.refs_4_.refs_0_), channel_id=1, source_target_pairs={{0,24},{1,25},{2,98},{3,99},{4,28},{5,29},{6,102},{7,103},{8,16},{... | collective-permute-start | bytes 196616 | tf_op jit(solution)/shard_map/ppermute | solution.py:71
  47.5 1.5 %collective-permute-start.10 = (f32[16,1024]{1,0:T(8,128)S(1)}, f32[16,1024]{1,0:T(8,128)S(1)}, u32[]{:S(2)}, u32[]{:S(2)}) collective-permute-start(f32[16,1024]{1,0:T(8,128)S(1)} %get-tuple-element.57.refs_4_.refs_0_), channel_id=1, source_target_pairs={{0,8},{1,9},{2,34},{3,35},{4,12},{5,13},{6,38},{7,39},{8,0},{9,1},... | collective-permute-start | bytes 196616 | tf_op jit(solution)/shard_map/ppermute | solution.py:71
  49.1 2.2 %turn.1 = (bf16[16,384,128]{2,1,0:T(8,128)(2,1)S(1)}, bf16[16,384,128]{2,1,0:T(8,128)(2,1)S(1)}) custom-call(bf16[512,384]{1,0:T(8,128)(2,1)S(1)} %copy-done.7, bf16[512,384]{1,0:T(8,128)(2,1)S(1)} %copy-done.2, bf16[512,384]{1,0:T(8,128)(2,1)} %get-tuple-element.51.refs_6_.refs_2_, bf16[512,384]{1,0:T(8,128)(2,1)} %collective-permute-done.6.refs_7_.refs_3_, ...), custom_call_target="tpu_custom_call" | custom-call | flops 1380000000 | tf_op jit(solution)/shard_map/turn/pallas_call | solution.py:432
  51.3 0.1 collective-permute-done.12.refs_3_
  51.4 0.7 collective-permute-done.11.refs_2_
  52.0 5.5 %query_grads.1 = (bf16[256,384]{1,0:T(8,128)(2,1)S(1)}, bf16[256,384]{1,0:T(8,128)(2,1)S(1)}, bf16[256,384]{1,0:T(8,128)(2,1)S(1)}, bf16[256,384]{1,0:T(8,128)(2...) custom-call(s32[64]{0:T(128)S(1)} %dynamic-slice_bitcast_fusion.info, ...), custom_call_target="tpu_custom_call" | custom-call | flops 5175000064 | tf_op jit(solution)/shard_map/query_grads/pallas_call | solution.py:432
  57.5 1.3 %collective-permute-start.17 = (bf16[256,384]{1,0:T(8,128)(2,1)S(1)}, bf16[256,384]{1,0:T(8,128)(2,1)S(1)}, u32[]{:S(2)}, u32[]{:S(2)}) collective-permute-start(bf16[256,384]{1,0:T(8,128)(2,1)S(1)} %get-tuple-element.70), channel_id=1, source_target_pairs={{0,8},{1,9},{2,34},{3,35},{4,12},{5,13},{6,38},{7,39},{8,0},{9,1},... | collective-permute-start | bytes 589832 | tf_op jit(solution)/shard_map/ppermute | solution.py:71
  58.8 1.7 %collective-permute-start.18 = (bf16[256,384]{1,0:T(8,128)(2,1)S(1)}, bf16[256,384]{1,0:T(8,128)(2,1)S(1)}, u32[]{:S(2)}, u32[]{:S(2)}) collective-permute-start(bf16[256,384]{1,0:T(8,128)(2,1)S(1)} %get-tuple-element.71), channel_id=1, source_target_pairs={{0,24},{1,25},{2,98},{3,99},{4,28},{5,29},{6,102},{7,103},{8,16},{... | collective-permute-start | bytes 589832 | tf_op jit(solution)/shard_map/ppermute | solution.py:71
  60.5 1.1 %collective-permute-start.19 = (bf16[256,384]{1,0:T(8,128)(2,1)S(1)}, bf16[256,384]{1,0:T(8,128)(2,1)S(1)}, u32[]{:S(2)}, u32[]{:S(2)}) collective-permute-start(bf16[256,384]{1,0:T(8,128)(2,1)S(1)} %get-tuple-element.72), channel_id=1, source_target_pairs={{0,16},{1,17},{2,66},{3,67},{4,20},{5,21},{6,70},{7,71},{8,24},{9,... | collective-permute-start | bytes 589832 | tf_op jit(solution)/shard_map/ppermute | solution.py:71
  61.6 6.2 %key_grads.1 = (bf16[1024,384]{1,0:T(8,128)(2,1)S(1)}, bf16[1024,384]{1,0:T(8,128)(2,1)}, f32[8,128]{1,0:T(8,128)S(1)}) custom-call(s32[64]{0:T(128)S(1)} %dynamic-slice_bitcast_fusion.info, s32[32,128]{1,0:T(8,128)S(1)} %get-tuple-element.50.lists, bf16[8,3,512,128]{3,2,1,0:T(8,128)(2,1)S(1)} %get-tuple-element.63.probs_in, ...), custom_call_target="tpu_custom_call" | custom-call | flops 5750000128 | tf_op jit(solution)/shard_map/key_grads/pallas_call | solution.py:432
  67.8 0.8 sum.1
  68.6 4.8 %collective-permute-start.22 = (bf16[256,384]{1,0:T(8,128)(2,1)}, bf16[256,384]{1,0:T(8,128)(2,1)}, u32[]{:S(2)}, u32[]{:S(2)}) collective-permute-start(bf16[256,384]{1,0:T(8,128)(2,1)} %get-tuple-element.74), channel_id=1, source_target_pairs={{0,64},{1,65},{2,18},{3,19},{4,68},{5,69},{6,22},{7,23},{8,72},{9,... | collective-permute-start | bytes 589832 | tf_op jit(solution)/shard_map/ppermute | solution.py:71
  73.4 0.1 collective-permute-start.21
  73.5 2.0 %collective-permute-start.15 = (bf16[1024,384]{1,0:T(8,128)(2,1)}, bf16[1024,384]{1,0:T(8,128)(2,1)}, u32[]{:S(2)}, u32[]{:S(2)}) collective-permute-start(bf16[1024,384]{1,0:T(8,128)(2,1)} %get-tuple-element.68), channel_id=1, source_target_pairs={{0,32},{1,33},{2,10},{3,11},{4,36},{5,37},{6,14},{7,15},{8,40},{9,... | collective-permute-start | bytes 2359304 | tf_op jit(solution)/shard_map/ppermute | solution.py:71
  75.5 1.8 %collective-permute-start.13 = (bf16[512,384]{1,0:T(8,128)(2,1)}, bf16[512,384]{1,0:T(8,128)(2,1)}, u32[]{:S(2)}, u32[]{:S(2)}) collective-permute-start(bf16[512,384]{1,0:T(8,128)(2,1)} %get-tuple-element.62), channel_id=1, source_target_pairs={{0,24},{1,25},{2,98},{3,99},{4,28},{5,29},{6,102},{7,103},{8,16},{... | collective-permute-start | bytes 1179656 | tf_op jit(solution)/shard_map/ppermute | solution.py:71
  77.3 0.1 collective-permute-done.22
  77.4 4.7 %collective-permute-done.21 = bf16[256,384]{1,0:T(8,128)(2,1)} collective-permute-done((bf16[256,384]{1,0:T(8,128)(2,1)}, bf16[256,384]{1,0:T(8,128)(2,1)}, u32[]{:S(2)}, u32[]{:S(2)}) %collective-permute-start.21) | collective-permute-done | bytes 196640 | tf_op jit(solution)/shard_map/ppermute | solution.py:71
  82.2 1.3 %add_convert_fusion.1.refs_0_ = bf16[256,384]{1,0:T(8,128)(2,1)S(1)} fusion(bf16[256,384]{1,0:T(8,128)(2,1)} %collective-permute-done.22, bf16[256,384]{1,0:T(8,128)(2,1)} %collective-permute-done.21, bf16[256,384]{1,0:T(8,128)(2,1)} %collective-permute-done.20, bf16[256,384]{1,0:T(8,128)(2,1)} %get-tuple-element.74), kind=kLoop, calls=%fused_computation.2 | loop fusion | flops 786432 | bytes 983040 | tf_op jit(solution)/shard_map/convert_element_type | solution.py:674
  83.5 1.0 copy-done.15
  84.5 0.9 weights.1
  85.4 1.9 %collective-permute-start.23 = (bf16[192,384]{1,0:T(8,128)(2,1)S(1)}, bf16[192,384]{1,0:T(8,128)(2,1)S(1)}, u32[]{:S(2)}, u32[]{:S(2)}) collective-permute-start(bf16[192,384]{1,0:T(8,128)(2,1)S(1)} %get-tuple-element.77), channel_id=1, source_target_pairs={{0,8},{1,9},{2,34},{3,35},{4,12},{5,13},{6,38},{7,39},{8,0},{9,1},... | collective-permute-start | bytes 442376 | tf_op jit(solution)/shard_map/ppermute | solution.py:71
  87.4 0.6 collective-permute-start.24
  88.0 1.6 %collective-permute-start.25 = (bf16[192,384]{1,0:T(8,128)(2,1)S(1)}, bf16[192,384]{1,0:T(8,128)(2,1)S(1)}, u32[]{:S(2)}, u32[]{:S(2)}) collective-permute-start(bf16[192,384]{1,0:T(8,128)(2,1)S(1)} %get-tuple-element.79), channel_id=1, source_target_pairs={{0,16},{1,17},{2,66},{3,67},{4,20},{5,21},{6,70},{7,71},{8,24},{9,... | collective-permute-start | bytes 442376 | tf_op jit(solution)/shard_map/ppermute | solution.py:71
  89.6 1.0 add_convert_fusion.5
  90.6 1.9 %collective-permute-start.14 = (bf16[256,384]{1,0:T(8,128)(2,1)S(1)}, bf16[256,384]{1,0:T(8,128)(2,1)S(1)}, u32[]{:S(2)}, u32[]{:S(2)}) collective-permute-start(bf16[256,384]{1,0:T(8,128)(2,1)S(1)} %add_convert_fusion.5), channel_id=1, source_target_pairs={{0,8},{1,9},{2,34},{3,35},{4,12},{5,13},{6,38},{7,39},{8,0},{9,1},... | collective-permute-start | bytes 589832 | tf_op jit(solution)/shard_map/ppermute | solution.py:71
  92.6 0.6 collective-permute-done.15
  93.2 1.1 %add_convert_fusion.refs_4_ = bf16[512,384]{1,0:T(8,128)(2,1)S(1)} fusion(bf16[1024,384]{1,0:T(8,128)(2,1)} %collective-permute-done.15, bf16[1024,384]{1,0:T(8,128)(2,1)S(1)} %get-tuple-element.67), kind=kLoop, calls=%fused_computation.1 | loop fusion | flops 786432 | bytes 1179648 | tf_op jit(solution)/shard_map/convert_element_type | solution.py:86
  94.3 3.2 %collective-permute-start.16 = (bf16[512,384]{1,0:T(8,128)(2,1)S(1)}, bf16[512,384]{1,0:T(8,128)(2,1)S(1)}, u32[]{:S(2)}, u32[]{:S(2)}) collective-permute-start(bf16[512,384]{1,0:T(8,128)(2,1)S(1)} %add_convert_fusion.refs_4_), channel_id=1, source_target_pairs={{0,96},{1,97},{2,26},{3,27},{4,100},{5,101},{6,30},{7,31},{8,104},... | collective-permute-start | bytes 1179656 | tf_op jit(solution)/shard_map/ppermute | solution.py:71
  97.5 0.1 split.1
  97.6 3.3 %collective-permute-start.26 = (bf16[96,384]{1,0:T(8,128)(2,1)S(1)}, bf16[96,384]{1,0:T(8,128)(2,1)S(1)}, u32[]{:S(2)}, u32[]{:S(2)}) collective-permute-start(bf16[96,384]{1,0:T(8,128)(2,1)S(1)} %get-tuple-element.81), channel_id=1, source_target_pairs={{0,1},{1,0},{2,3},{3,2},{4,5},{5,4},{6,7},{7,6},{8,9},{9,8},{10,11... | collective-permute-start | bytes 221192 | tf_op jit(solution)/shard_map/ppermute | solution.py:679
  100.9 1.7 %fusion = bf16[1,256,384]{2,1,0:T(8,128)(2,1)} fusion(bf16[256,384]{1,0:T(8,128)(2,1)S(1)} %collective-permute-done.14, bf16[512,384]{1,0:T(8,128)(2,1)} %collective-permute-done.13, bf16[512,384]{1,0:T(8,128)(2,1)S(1)} %get-tuple-element.61), kind=kLoop, calls=%fused_computation.7 | loop fusion | flops 589824 | bytes 786432 | tf_op jit(solution)/shard_map/broadcast_in_dim | solution.py:680
  102.6 1.0 collective-permute-done.26
  103.5 0.7 convert_add_fusion
  104.2 1.9 %fusion.2 = (bf16[1,256,384]{2,1,0:T(8,128)(2,1)}, bf16[1,256,384]{2,1,0:T(8,128)(2,1)}) fusion(bf16[512,384]{1,0:T(8,128)(2,1)S(1)} %collective-permute-done.16, bf16[1024,384]{1,0:T(8,128)(2,1)} %collective-permute-done.15, bf16[1024,384]{1,0:T(8,128)(2,1)S(1)} %get-tuple-element.67), kind=kLoop, calls=%fused_computation.9 | loop fusion | flops 1179648 | bytes 1572864 | tf_op jit(solution)/shard_map/broadcast_in_dim | solution.py:682
  (43 shorter events, 0.1 us)
Async XLA Ops:
  0.6 1.7 %copy-start = (bf16[3072,384]{1,0:T(8,128)(2,1)S(1)}, bf16[3072,384]{1,0:T(8,128)(2,1)}, u32[]{:S(2)}) copy-start(bf16[3072,384]{1,0:T(8,128)(2,1)} %param.16) | copy-start | bytes 7077892
  0.6 3.1 %copy-start.13 = (s32[4,2]{0,1:T(2,128)S(1)}, s32[4,2]{0,1:T(2,128)}, u32[]{:S(2)}) copy-start(s32[4,2]{0,1:T(2,128)} %param.14) | copy-start | bytes 100
  0.7 3.1 %copy-start.12 = (s32[4,32]{1,0:T(4,128)S(1)}, s32[4,32]{1,0:T(4,128)}, u32[]{:S(2)}) copy-start(s32[4,32]{1,0:T(4,128)} %kv_list.1) | copy-start | bytes 1540
  0.7 3.1 %copy-start.9 = (bf16[1,256,384]{2,1,0:T(8,128)(2,1)S(1)}, bf16[1,256,384]{2,1,0:T(8,128)(2,1)}, u32[]{:S(2)}) copy-start(bf16[1,256,384]{2,1,0:T(8,128)(2,1)} %param.12) | copy-start | bytes 589828
  0.7 3.1 %copy-start.8 = (bf16[1,256,384]{2,1,0:T(8,128)(2,1)S(1)}, bf16[1,256,384]{2,1,0:T(8,128)(2,1)}, u32[]{:S(2)}) copy-start(bf16[1,256,384]{2,1,0:T(8,128)(2,1)} %param.9) | copy-start | bytes 589828
  3.8 3.3 %copy-start.10 = (bf16[1,256,384]{2,1,0:T(8,128)(2,1)S(1)}, bf16[1,256,384]{2,1,0:T(8,128)(2,1)}, u32[]{:S(2)}) copy-start(bf16[1,256,384]{2,1,0:T(8,128)(2,1)} %param.10) | copy-start | bytes 589828
  3.8 3.3 %copy-start.11 = (bf16[1,256,384]{2,1,0:T(8,128)(2,1)S(1)}, bf16[1,256,384]{2,1,0:T(8,128)(2,1)}, u32[]{:S(2)}) copy-start(bf16[1,256,384]{2,1,0:T(8,128)(2,1)} %param.11) | copy-start | bytes 589828
  3.9 15.2 %copy-start.4 = (bf16[592,384]{1,0:T(8,128)(2,1)}, bf16[592,384]{1,0:T(8,128)(2,1)S(1)}, u32[]{:S(2)}) copy-start(bf16[592,384]{1,0:T(8,128)(2,1)S(1)} %get-tuple-element.43.refs_0_) | copy-start | bytes 1363972
  3.9 15.2 %collective-permute-start.3 = (bf16[592,384]{1,0:T(8,128)(2,1)S(1)}, bf16[592,384]{1,0:T(8,128)(2,1)S(1)}, u32[]{:S(2)}, u32[]{:S(2)}) collective-permute-start(bf16[592,384]{1,0:T(8,128)(2,1)S(1)} %get-tuple-element.43.refs_0_), channel_id=1, source_target_pairs={{0,24},{1,25},{2,98},{3,99},{4,28},{5,29},{6,102},{7,103},{8,16},{... | collective-permute-start | bytes 1363976 | tf_op jit(solution)/shard_map/ppermute | solution.py:71
  6.8 12.6 %collective-permute-start = (bf16[592,384]{1,0:T(8,128)(2,1)S(1)}, bf16[592,384]{1,0:T(8,128)(2,1)S(1)}, u32[]{:S(2)}, u32[]{:S(2)}) collective-permute-start(bf16[592,384]{1,0:T(8,128)(2,1)S(1)} %get-tuple-element.43.refs_0_), channel_id=1, source_target_pairs={{0,8},{1,9},{2,34},{3,35},{4,12},{5,13},{6,38},{7,39},{8,0},{9,1},... | collective-permute-start | bytes 1363976 | tf_op jit(solution)/shard_map/ppermute | solution.py:71
  7.1 12.0 %collective-permute-start.4 = (bf16[512,384]{1,0:T(8,128)(2,1)S(1)}, bf16[512,384]{1,0:T(8,128)(2,1)S(1)}, u32[]{:S(2)}, u32[]{:S(2)}) collective-permute-start(bf16[512,384]{1,0:T(8,128)(2,1)S(1)} %stack.1.refs_4_.refs_0_), channel_id=1, source_target_pairs={{0,32},{1,33},{2,10},{3,11},{4,36},{5,37},{6,14},{7,15},{8,40},{9,... | collective-permute-start | bytes 1179656 | tf_op jit(solution)/shard_map/ppermute | solution.py:71
  9.1 10.0 %collective-permute-start.1 = (bf16[512,384]{1,0:T(8,128)(2,1)S(1)}, bf16[512,384]{1,0:T(8,128)(2,1)}, u32[]{:S(2)}, u32[]{:S(2)}) collective-permute-start(bf16[512,384]{1,0:T(8,128)(2,1)S(1)} %stack.1.refs_4_.refs_0_), channel_id=1, source_target_pairs={{0,96},{1,97},{2,26},{3,27},{4,100},{5,101},{6,30},{7,31},{8,104},... | collective-permute-start | bytes 1179656 | tf_op jit(solution)/shard_map/ppermute | solution.py:71
  11.6 0.7 copy-start.6
  12.3 6.5 %collective-permute-start.2 = (bf16[80,384]{1,0:T(8,128)(2,1)S(1)}, bf16[80,384]{1,0:T(8,128)(2,1)S(1)}, u32[]{:S(2)}, u32[]{:S(2)}) collective-permute-start(bf16[80,384]{1,0:T(8,128)(2,1)S(1)} %get-tuple-element.44), channel_id=1, source_target_pairs={{0,16},{1,17},{2,66},{3,67},{4,20},{5,21},{6,70},{7,71},{8,24},{9,... | collective-permute-start | bytes 184328 | tf_op jit(solution)/shard_map/ppermute | solution.py:71
  19.1 0.7 copy-start.1
  19.8 12.5 %collective-permute-start.5 = (bf16[592,384]{1,0:T(8,128)(2,1)S(1)}, bf16[592,384]{1,0:T(8,128)(2,1)}, u32[]{:S(2)}, u32[]{:S(2)}) collective-permute-start(bf16[592,384]{1,0:T(8,128)(2,1)S(1)} %get-tuple-element.45.refs_1_), channel_id=1, source_target_pairs={{0,24},{1,25},{2,98},{3,99},{4,28},{5,29},{6,102},{7,103},{8,16},{... | collective-permute-start | bytes 1363976 | tf_op jit(solution)/shard_map/ppermute | solution.py:71
  23.5 8.7 %collective-permute-start.6 = (bf16[512,384]{1,0:T(8,128)(2,1)}, bf16[512,384]{1,0:T(8,128)(2,1)}, u32[]{:S(2)}, u32[]{:S(2)}) collective-permute-start(bf16[512,384]{1,0:T(8,128)(2,1)} %get-tuple-element.51.refs_6_.refs_2_), channel_id=1, source_target_pairs={{0,32},{1,33},{2,10},{3,11},{4,36},{5,37},{6,14},{7,15},{8,40},{9,... | collective-permute-start | bytes 1179656 | tf_op jit(solution)/shard_map/ppermute | solution.py:71
  26.0 1.0 copy-start.3
  27.0 1.0 copy-start.5
  27.8 4.5 %copy-start.2 = (bf16[512,384]{1,0:T(8,128)(2,1)S(1)}, bf16[512,384]{1,0:T(8,128)(2,1)}, u32[]{:S(2)}) copy-start(bf16[512,384]{1,0:T(8,128)(2,1)} %copy-done.1) | copy-start | bytes 1179652
  27.8 4.5 %copy-start.7 = (bf16[512,384]{1,0:T(8,128)(2,1)S(1)}, bf16[512,384]{1,0:T(8,128)(2,1)}, u32[]{:S(2)}) copy-start(bf16[512,384]{1,0:T(8,128)(2,1)} %copy-done.6) | copy-start | bytes 1179652
  28.1 8.0 %collective-permute-start.7 = (bf16[384,384]{1,0:T(8,128)(2,1)S(1)}, bf16[384,384]{1,0:T(8,128)(2,1)S(1)}, u32[]{:S(2)}, u32[]{:S(2)}) collective-permute-start(bf16[384,384]{1,0:T(8,128)(2,1)S(1)} %get-tuple-element.53), channel_id=1, source_target_pairs={{0,32},{1,33},{2,10},{3,11},{4,36},{5,37},{6,14},{7,15},{8,40},{9,... | collective-permute-start | bytes 884744 | tf_op jit(solution)/shard_map/ppermute | solution.py:71
  28.5 11.1 %collective-permute-start.8 = (bf16[384,384]{1,0:T(8,128)(2,1)S(1)}, bf16[384,384]{1,0:T(8,128)(2,1)S(1)}, u32[]{:S(2)}, u32[]{:S(2)}) collective-permute-start(bf16[384,384]{1,0:T(8,128)(2,1)S(1)} %get-tuple-element.54), channel_id=1, source_target_pairs={{0,96},{1,97},{2,26},{3,27},{4,100},{5,101},{6,30},{7,31},{8,104},... | collective-permute-start | bytes 884744 | tf_op jit(solution)/shard_map/ppermute | solution.py:71
  30.4 9.2 %collective-permute-start.9 = (bf16[384,384]{1,0:T(8,128)(2,1)S(1)}, bf16[384,384]{1,0:T(8,128)(2,1)S(1)}, u32[]{:S(2)}, u32[]{:S(2)}) collective-permute-start(bf16[384,384]{1,0:T(8,128)(2,1)S(1)} %get-tuple-element.55), channel_id=1, source_target_pairs={{0,64},{1,65},{2,18},{3,19},{4,68},{5,69},{6,22},{7,23},{8,72},{9,... | collective-permute-start | bytes 884744 | tf_op jit(solution)/shard_map/ppermute | solution.py:71
  44.8 0.7 copy-start.14
  45.6 5.8 %collective-permute-start.12 = (f32[16,1024]{1,0:T(8,128)S(1)}, f32[16,1024]{1,0:T(8,128)S(1)}, u32[]{:S(2)}, u32[]{:S(2)}) collective-permute-start(f32[16,1024]{1,0:T(8,128)S(1)} %get-tuple-element.57.refs_4_.refs_0_), channel_id=1, source_target_pairs={{0,16},{1,17},{2,66},{3,67},{4,20},{5,21},{6,70},{7,71},{8,24},{9,... | collective-permute-start | bytes 196616 | tf_op jit(solution)/shard_map/ppermute | solution.py:71
  46.3 5.7 %collective-permute-start.11 = (f32[16,1024]{1,0:T(8,128)S(1)}, f32[16,1024]{1,0:T(8,128)S(1)}, u32[]{:S(2)}, u32[]{:S(2)}) collective-permute-start(f32[16,1024]{1,0:T(8,128)S(1)} %get-tuple-element.57.refs_4_.refs_0_), channel_id=1, source_target_pairs={{0,24},{1,25},{2,98},{3,99},{4,28},{5,29},{6,102},{7,103},{8,16},{... | collective-permute-start | bytes 196616 | tf_op jit(solution)/shard_map/ppermute | solution.py:71
  47.5 4.5 %collective-permute-start.10 = (f32[16,1024]{1,0:T(8,128)S(1)}, f32[16,1024]{1,0:T(8,128)S(1)}, u32[]{:S(2)}, u32[]{:S(2)}) collective-permute-start(f32[16,1024]{1,0:T(8,128)S(1)} %get-tuple-element.57.refs_4_.refs_0_), channel_id=1, source_target_pairs={{0,8},{1,9},{2,34},{3,35},{4,12},{5,13},{6,38},{7,39},{8,0},{9,1},... | collective-permute-start | bytes 196616 | tf_op jit(solution)/shard_map/ppermute | solution.py:71
  57.5 10.3 %collective-permute-start.17 = (bf16[256,384]{1,0:T(8,128)(2,1)S(1)}, bf16[256,384]{1,0:T(8,128)(2,1)S(1)}, u32[]{:S(2)}, u32[]{:S(2)}) collective-permute-start(bf16[256,384]{1,0:T(8,128)(2,1)S(1)} %get-tuple-element.70), channel_id=1, source_target_pairs={{0,8},{1,9},{2,34},{3,35},{4,12},{5,13},{6,38},{7,39},{8,0},{9,1},... | collective-permute-start | bytes 589832 | tf_op jit(solution)/shard_map/ppermute | solution.py:71
  58.8 9.0 %collective-permute-start.18 = (bf16[256,384]{1,0:T(8,128)(2,1)S(1)}, bf16[256,384]{1,0:T(8,128)(2,1)S(1)}, u32[]{:S(2)}, u32[]{:S(2)}) collective-permute-start(bf16[256,384]{1,0:T(8,128)(2,1)S(1)} %get-tuple-element.71), channel_id=1, source_target_pairs={{0,24},{1,25},{2,98},{3,99},{4,28},{5,29},{6,102},{7,103},{8,16},{... | collective-permute-start | bytes 589832 | tf_op jit(solution)/shard_map/ppermute | solution.py:71
  60.5 7.3 %collective-permute-start.19 = (bf16[256,384]{1,0:T(8,128)(2,1)S(1)}, bf16[256,384]{1,0:T(8,128)(2,1)S(1)}, u32[]{:S(2)}, u32[]{:S(2)}) collective-permute-start(bf16[256,384]{1,0:T(8,128)(2,1)S(1)} %get-tuple-element.72), channel_id=1, source_target_pairs={{0,16},{1,17},{2,66},{3,67},{4,20},{5,21},{6,70},{7,71},{8,24},{9,... | collective-permute-start | bytes 589832 | tf_op jit(solution)/shard_map/ppermute | solution.py:71
  68.6 8.9 %collective-permute-start.22 = (bf16[256,384]{1,0:T(8,128)(2,1)}, bf16[256,384]{1,0:T(8,128)(2,1)}, u32[]{:S(2)}, u32[]{:S(2)}) collective-permute-start(bf16[256,384]{1,0:T(8,128)(2,1)} %get-tuple-element.74), channel_id=1, source_target_pairs={{0,64},{1,65},{2,18},{3,19},{4,68},{5,69},{6,22},{7,23},{8,72},{9,... | collective-permute-start | bytes 589832 | tf_op jit(solution)/shard_map/ppermute | solution.py:71
  73.4 8.8 %collective-permute-start.21 = (bf16[256,384]{1,0:T(8,128)(2,1)}, bf16[256,384]{1,0:T(8,128)(2,1)}, u32[]{:S(2)}, u32[]{:S(2)}) collective-permute-start(bf16[256,384]{1,0:T(8,128)(2,1)} %get-tuple-element.74), channel_id=1, source_target_pairs={{0,96},{1,97},{2,26},{3,27},{4,100},{5,101},{6,30},{7,31},{8,104},... | collective-permute-start | bytes 589832 | tf_op jit(solution)/shard_map/ppermute | solution.py:71
  73.5 8.7 %collective-permute-start.20 = (bf16[256,384]{1,0:T(8,128)(2,1)}, bf16[256,384]{1,0:T(8,128)(2,1)}, u32[]{:S(2)}, u32[]{:S(2)}) collective-permute-start(bf16[256,384]{1,0:T(8,128)(2,1)} %get-tuple-element.74), channel_id=1, source_target_pairs={{0,32},{1,33},{2,10},{3,11},{4,36},{5,37},{6,14},{7,15},{8,40},{9,... | collective-permute-start | bytes 589832 | tf_op jit(solution)/shard_map/ppermute | solution.py:71
  73.5 19.7 %collective-permute-start.15 = (bf16[1024,384]{1,0:T(8,128)(2,1)}, bf16[1024,384]{1,0:T(8,128)(2,1)}, u32[]{:S(2)}, u32[]{:S(2)}) collective-permute-start(bf16[1024,384]{1,0:T(8,128)(2,1)} %get-tuple-element.68), channel_id=1, source_target_pairs={{0,32},{1,33},{2,10},{3,11},{4,36},{5,37},{6,14},{7,15},{8,40},{9,... | collective-permute-start | bytes 2359304 | tf_op jit(solution)/shard_map/ppermute | solution.py:71
  75.5 14.1 %collective-permute-start.13 = (bf16[512,384]{1,0:T(8,128)(2,1)}, bf16[512,384]{1,0:T(8,128)(2,1)}, u32[]{:S(2)}, u32[]{:S(2)}) collective-permute-start(bf16[512,384]{1,0:T(8,128)(2,1)} %get-tuple-element.62), channel_id=1, source_target_pairs={{0,24},{1,25},{2,98},{3,99},{4,28},{5,29},{6,102},{7,103},{8,16},{... | collective-permute-start | bytes 1179656 | tf_op jit(solution)/shard_map/ppermute | solution.py:71
  83.5 1.0 copy-start.15
  85.4 12.0 %collective-permute-start.23 = (bf16[192,384]{1,0:T(8,128)(2,1)S(1)}, bf16[192,384]{1,0:T(8,128)(2,1)S(1)}, u32[]{:S(2)}, u32[]{:S(2)}) collective-permute-start(bf16[192,384]{1,0:T(8,128)(2,1)S(1)} %get-tuple-element.77), channel_id=1, source_target_pairs={{0,8},{1,9},{2,34},{3,35},{4,12},{5,13},{6,38},{7,39},{8,0},{9,1},... | collective-permute-start | bytes 442376 | tf_op jit(solution)/shard_map/ppermute | solution.py:71
  87.4 10.1 %collective-permute-start.24 = (bf16[192,384]{1,0:T(8,128)(2,1)S(1)}, bf16[192,384]{1,0:T(8,128)(2,1)S(1)}, u32[]{:S(2)}, u32[]{:S(2)}) collective-permute-start(bf16[192,384]{1,0:T(8,128)(2,1)S(1)} %get-tuple-element.78), channel_id=1, source_target_pairs={{0,24},{1,25},{2,98},{3,99},{4,28},{5,29},{6,102},{7,103},{8,16},{... | collective-permute-start | bytes 442376 | tf_op jit(solution)/shard_map/ppermute | solution.py:71
  88.0 9.5 %collective-permute-start.25 = (bf16[192,384]{1,0:T(8,128)(2,1)S(1)}, bf16[192,384]{1,0:T(8,128)(2,1)S(1)}, u32[]{:S(2)}, u32[]{:S(2)}) collective-permute-start(bf16[192,384]{1,0:T(8,128)(2,1)S(1)} %get-tuple-element.79), channel_id=1, source_target_pairs={{0,16},{1,17},{2,66},{3,67},{4,20},{5,21},{6,70},{7,71},{8,24},{9,... | collective-permute-start | bytes 442376 | tf_op jit(solution)/shard_map/ppermute | solution.py:71
  90.6 10.3 %collective-permute-start.14 = (bf16[256,384]{1,0:T(8,128)(2,1)S(1)}, bf16[256,384]{1,0:T(8,128)(2,1)S(1)}, u32[]{:S(2)}, u32[]{:S(2)}) collective-permute-start(bf16[256,384]{1,0:T(8,128)(2,1)S(1)} %add_convert_fusion.5), channel_id=1, source_target_pairs={{0,8},{1,9},{2,34},{3,35},{4,12},{5,13},{6,38},{7,39},{8,0},{9,1},... | collective-permute-start | bytes 589832 | tf_op jit(solution)/shard_map/ppermute | solution.py:71
  94.3 10.0 %collective-permute-start.16 = (bf16[512,384]{1,0:T(8,128)(2,1)S(1)}, bf16[512,384]{1,0:T(8,128)(2,1)S(1)}, u32[]{:S(2)}, u32[]{:S(2)}) collective-permute-start(bf16[512,384]{1,0:T(8,128)(2,1)S(1)} %add_convert_fusion.refs_4_), channel_id=1, source_target_pairs={{0,96},{1,97},{2,26},{3,27},{4,100},{5,101},{6,30},{7,31},{8,104},... | collective-permute-start | bytes 1179656 | tf_op jit(solution)/shard_map/ppermute | solution.py:71
  97.6 5.9 %collective-permute-start.26 = (bf16[96,384]{1,0:T(8,128)(2,1)S(1)}, bf16[96,384]{1,0:T(8,128)(2,1)S(1)}, u32[]{:S(2)}, u32[]{:S(2)}) collective-permute-start(bf16[96,384]{1,0:T(8,128)(2,1)S(1)} %get-tuple-element.81), channel_id=1, source_target_pairs={{0,1},{1,0},{2,3},{3,2},{4,5},{5,4},{6,7},{7,6},{8,9},{9,8},{10,11... | collective-permute-start | bytes 221192 | tf_op jit(solution)/shard_map/ppermute | solution.py:679

commit v5 on v4

--- a/solution.py
+++ b/solution.py
@@ -25,7 +25,7 @@
 MIB = 1 << 20
 CHUNK = 192
 PADDED = 256
-PAIRS = 2
+PAIRS = 4
 
 
 def roles(ctx, core):

time: 107 us -> 106 us (level)
  Pallas kernels: 25.7 us -> 24.6 us
  waiting for transfers between devices: 16.1 us -> 17.2 us
    pallas_call x13, Pallas kernels: 25.7 us -> 24.6 us  [call(): pl.pallas_call(kernel, name=name, grid=grid, out_shape=[jax.ShapeDtypeStr...]
    ppermute x26, waiting for transfers between devices: 15.1 us -> 16.2 us  [send(): return lax.ppermute(array, ('ctx', 'head', 'dp'), pairs)]
  transfers between devices with their start and end apart: 27 -> 27, of which waited for: 10 -> 11; matrix products, arithmetic and copies ran while one was open for 6% -> 6% of each run, Pallas kernels for 13% -> 13%
where the time goes in v5:
time: 106 us; the launch traced here: 105 us
  starting transfers between devices  47.2 us (45%)
  Pallas kernels  24.6 us (23%)
  waiting for transfers between devices  17.2 us (16%)
  other arithmetic  7.65 us (7%)
  local copies, waits for them, and re-layouts  6.34 us (6%)
  matrix products  1.44 us (1%)
    ppermute x26, starting transfers between devices, send(): return lax.ppermute(array, ('ctx', 'head', 'dp'), pairs)  43.9 us
    pallas_call x13, Pallas kernels, call(): pl.pallas_call(kernel, name=name, grid=grid, out_shape=[jax.ShapeDtypeStr...  24.6 us
    ppermute x26, waiting for transfers between devices, send(): return lax.ppermute(array, ('ctx', 'head', 'dp'), pairs)  16.2 us
    unnamed x32, local copies, waits for them, and re-layouts  5.64 us
    ppermute x1, starting transfers between devices, body(): lax.ppermute(other, 'dp', [(0, 1), (1, 0)]).astype(F32)  3.28 us
  transfers between devices with their start and end apart: 27, of which 11 were waited for; matrix products, arithmetic and copies ran while one was open for 6% of the time, Pallas kernels for 13%

profile of v5, /device:TPU:0, one launch (start us, length us, event | category | flops | bytes accessed | tf_op | source)
XLA Modules:
  0.0 105.4 jit_solution(16107951252320422659)
XLA Ops:
  0.6 0.0 copy-start
  0.7 1.6 %copy-done = bf16[3072,384]{1,0:T(8,128)(2,1)S(1)} copy-done((bf16[3072,384]{1,0:T(8,128)(2,1)S(1)}, bf16[3072,384]{1,0:T(8,128)(2,1)}, u32[]{:S(2)}) %copy-start) | copy-done | bytes 2359320
  2.3 1.4 %convolution_convert_fusion.cond = bf16[64,384]{1,0:T(8,128)(2,1)S(1)} fusion(bf16[3072,384]{1,0:T(8,128)(2,1)S(1)} %copy-done, bf16[1,64,3072]{2,1,0:T(8,128)(2,1)} %param.15), kind=kOutput, calls=%fused_computation | convolution fusion | flops 151019520 | bytes 2801664 | tf_op jit(solution)/shard_map/dot_general | solution.py:654
  3.8 0.1 pack.1
  3.9 2.9 %collective-permute-start.3 = (bf16[592,384]{1,0:T(8,128)(2,1)S(1)}, bf16[592,384]{1,0:T(8,128)(2,1)S(1)}, u32[]{:S(2)}, u32[]{:S(2)}) collective-permute-start(bf16[592,384]{1,0:T(8,128)(2,1)S(1)} %get-tuple-element.43.refs_0_), channel_id=1, source_target_pairs={{0,24},{1,25},{2,98},{3,99},{4,28},{5,29},{6,102},{7,103},{8,16},{... | collective-permute-start | bytes 1363976 | tf_op jit(solution)/shard_map/ppermute | solution.py:71
  6.8 0.2 collective-permute-start
  7.1 2.0 %collective-permute-start.4 = (bf16[512,384]{1,0:T(8,128)(2,1)S(1)}, bf16[512,384]{1,0:T(8,128)(2,1)S(1)}, u32[]{:S(2)}, u32[]{:S(2)}) collective-permute-start(bf16[512,384]{1,0:T(8,128)(2,1)S(1)} %stack.1.refs_4_.refs_0_), channel_id=1, source_target_pairs={{0,32},{1,33},{2,10},{3,11},{4,36},{5,37},{6,14},{7,15},{8,40},{9,... | collective-permute-start | bytes 1179656 | tf_op jit(solution)/shard_map/ppermute | solution.py:71
  9.1 2.5 %collective-permute-start.1 = (bf16[512,384]{1,0:T(8,128)(2,1)S(1)}, bf16[512,384]{1,0:T(8,128)(2,1)}, u32[]{:S(2)}, u32[]{:S(2)}) collective-permute-start(bf16[512,384]{1,0:T(8,128)(2,1)S(1)} %stack.1.refs_4_.refs_0_), channel_id=1, source_target_pairs={{0,96},{1,97},{2,26},{3,27},{4,100},{5,101},{6,30},{7,31},{8,104},... | collective-permute-start | bytes 1179656 | tf_op jit(solution)/shard_map/ppermute | solution.py:71
  11.6 0.7 copy-done.6
  12.3 1.7 %collective-permute-start.2 = (bf16[80,384]{1,0:T(8,128)(2,1)S(1)}, bf16[80,384]{1,0:T(8,128)(2,1)S(1)}, u32[]{:S(2)}, u32[]{:S(2)}) collective-permute-start(bf16[80,384]{1,0:T(8,128)(2,1)S(1)} %get-tuple-element.44), channel_id=1, source_target_pairs={{0,16},{1,17},{2,66},{3,67},{4,20},{5,21},{6,70},{7,71},{8,24},{9,... | collective-permute-start | bytes 184328 | tf_op jit(solution)/shard_map/ppermute | solution.py:71
  14.1 4.8 %collective-permute-done.2.refs_2_.refs_3_ = bf16[80,384]{1,0:T(8,128)(2,1)S(1)} collective-permute-done((bf16[80,384]{1,0:T(8,128)(2,1)S(1)}, bf16[80,384]{1,0:T(8,128)(2,1)S(1)}, u32[]{:S(2)}, u32[]{:S(2)}) %collective-permute-start.2) | collective-permute-done | bytes 61472 | tf_op jit(solution)/shard_map/ppermute | solution.py:71
  18.8 0.2 collective-permute-done.4.refs_4_.refs_5_.refs_1_
  19.1 0.4 collective-permute-done.refs_0_
  19.5 0.4 copy-done.1
  19.8 3.7 %collective-permute-start.5 = (bf16[592,384]{1,0:T(8,128)(2,1)S(1)}, bf16[592,384]{1,0:T(8,128)(2,1)}, u32[]{:S(2)}, u32[]{:S(2)}) collective-permute-start(bf16[592,384]{1,0:T(8,128)(2,1)S(1)} %get-tuple-element.45.refs_1_), channel_id=1, source_target_pairs={{0,24},{1,25},{2,98},{3,99},{4,28},{5,29},{6,102},{7,103},{8,16},{... | collective-permute-start | bytes 1363976 | tf_op jit(solution)/shard_map/ppermute | solution.py:71
  23.5 1.7 %collective-permute-start.6 = (bf16[512,384]{1,0:T(8,128)(2,1)}, bf16[512,384]{1,0:T(8,128)(2,1)}, u32[]{:S(2)}, u32[]{:S(2)}) collective-permute-start(bf16[512,384]{1,0:T(8,128)(2,1)} %get-tuple-element.51.refs_6_.refs_2_), channel_id=1, source_target_pairs={{0,32},{1,33},{2,10},{3,11},{4,36},{5,37},{6,14},{7,15},{8,40},{9,... | collective-permute-start | bytes 1179656 | tf_op jit(solution)/shard_map/ppermute | solution.py:71
  25.3 0.7 dynamic-slice_bitcast_fusion.info
  26.0 1.0 copy-done.3
  27.0 0.8 tokens.1
  27.8 0.2 copy-done.5
  28.0 0.1 join.1
  28.1 0.4 collective-permute-start.7
  28.5 1.9 %collective-permute-start.8 = (bf16[384,384]{1,0:T(8,128)(2,1)S(1)}, bf16[384,384]{1,0:T(8,128)(2,1)S(1)}, u32[]{:S(2)}, u32[]{:S(2)}) collective-permute-start(bf16[384,384]{1,0:T(8,128)(2,1)S(1)} %get-tuple-element.54), channel_id=1, source_target_pairs={{0,96},{1,97},{2,26},{3,27},{4,100},{5,101},{6,30},{7,31},{8,104},... | collective-permute-start | bytes 884744 | tf_op jit(solution)/shard_map/ppermute | solution.py:71
  30.4 1.9 %collective-permute-start.9 = (bf16[384,384]{1,0:T(8,128)(2,1)S(1)}, bf16[384,384]{1,0:T(8,128)(2,1)S(1)}, u32[]{:S(2)}, u32[]{:S(2)}) collective-permute-start(bf16[384,384]{1,0:T(8,128)(2,1)S(1)} %get-tuple-element.55), channel_id=1, source_target_pairs={{0,64},{1,65},{2,18},{3,19},{4,68},{5,69},{6,22},{7,23},{8,72},{9,... | collective-permute-start | bytes 884744 | tf_op jit(solution)/shard_map/ppermute | solution.py:71
  32.3 3.4 %slopes.1 = (f32[8,3,512,128]{3,2,1,0:T(8,128)S(1)}, bf16[1024,384]{1,0:T(8,128)(2,1)S(1)}) custom-call(s32[64]{0:T(128)S(1)} %dynamic-slice_bitcast_fusion.info, s32[32,128]{1,0:T(8,128)S(1)} %get-tuple-element.50.lists, bf16[592,384]{1,0:T(8,128)(2,1)S(1)} %copy-done.5, bf16[592,384]{1,0:T(8,128)(2,1)S(1)} %get-tuple-element.45.refs_1_, ...), custom_call_target="tpu_custom_call" | custom-call | flops 4600000000 | tf_op jit(solution)/shard_map/slopes/pallas_call | solution.py:432
  35.7 3.9 %collective-permute-done.8.refs_10_ = bf16[384,384]{1,0:T(8,128)(2,1)S(1)} collective-permute-done((bf16[384,384]{1,0:T(8,128)(2,1)S(1)}, bf16[384,384]{1,0:T(8,128)(2,1)S(1)}, u32[]{:S(2)}, u32[]{:S(2)}) %collective-permute-start.8) | collective-permute-done | bytes 294944 | tf_op jit(solution)/shard_map/ppermute | solution.py:71
  39.5 4.9 %scores.1 = (bf16[1024,384]{1,0:T(8,128)(2,1)S(1)}, f32[16,1024]{1,0:T(8,128)S(1)}, bf16[8,3,512,128]{3,2,1,0:T(8,128)(2,1)S(1)}, bf16[2,256,384]{2,1,0:T(8,128)(2,1)S(1)}) custom-call(s32[64]{0:T(128)S(1)} %dynamic-slice_bitcast_fusion.info, s32[32,128]{1,0:T(8,128)S(1)} %get-tuple-element.50.lists, bf16[592,384]{1,0:T(8,128)(2,1)S(1)} %copy-done.5, ...), custom_call_target="tpu_custom_call" | custom-call | flops 5750000128 | tf_op jit(solution)/shard_map/scores/pallas_call | solution.py:432
  44.5 0.7 copy-done.14
  45.2 0.7 collective-permute-start.12
  45.9 1.2 %collective-permute-start.11 = (f32[16,1024]{1,0:T(8,128)S(1)}, f32[16,1024]{1,0:T(8,128)S(1)}, u32[]{:S(2)}, u32[]{:S(2)}) collective-permute-start(f32[16,1024]{1,0:T(8,128)S(1)} %get-tuple-element.57.refs_4_.refs_0_), channel_id=1, source_target_pairs={{0,24},{1,25},{2,98},{3,99},{4,28},{5,29},{6,102},{7,103},{8,16},{... | collective-permute-start | bytes 196616 | tf_op jit(solution)/shard_map/ppermute | solution.py:71
  47.2 1.5 %collective-permute-start.10 = (f32[16,1024]{1,0:T(8,128)S(1)}, f32[16,1024]{1,0:T(8,128)S(1)}, u32[]{:S(2)}, u32[]{:S(2)}) collective-permute-start(f32[16,1024]{1,0:T(8,128)S(1)} %get-tuple-element.57.refs_4_.refs_0_), channel_id=1, source_target_pairs={{0,8},{1,9},{2,34},{3,35},{4,12},{5,13},{6,38},{7,39},{8,0},{9,1},... | collective-permute-start | bytes 196616 | tf_op jit(solution)/shard_map/ppermute | solution.py:71
  48.7 2.2 %turn.1 = (bf16[16,384,128]{2,1,0:T(8,128)(2,1)S(1)}, bf16[16,384,128]{2,1,0:T(8,128)(2,1)S(1)}) custom-call(bf16[512,384]{1,0:T(8,128)(2,1)S(1)} %copy-done.7, bf16[512,384]{1,0:T(8,128)(2,1)S(1)} %copy-done.2, bf16[512,384]{1,0:T(8,128)(2,1)} %get-tuple-element.51.refs_6_.refs_2_, bf16[512,384]{1,0:T(8,128)(2,1)} %collective-permute-done.6.refs_7_.refs_3_, ...), custom_call_target="tpu_custom_call" | custom-call | flops 1380000000 | tf_op jit(solution)/shard_map/turn/pallas_call | solution.py:432
  50.9 0.1 collective-permute-done.12.refs_3_
  51.0 0.7 collective-permute-done.11.refs_2_
  51.7 5.5 %query_grads.1 = (bf16[256,384]{1,0:T(8,128)(2,1)S(1)}, bf16[256,384]{1,0:T(8,128)(2,1)S(1)}, bf16[256,384]{1,0:T(8,128)(2,1)S(1)}, bf16[256,384]{1,0:T(8,128)(2...) custom-call(s32[64]{0:T(128)S(1)} %dynamic-slice_bitcast_fusion.info, ...), custom_call_target="tpu_custom_call" | custom-call | flops 5175000064 | tf_op jit(solution)/shard_map/query_grads/pallas_call | solution.py:432
  57.1 1.3 %collective-permute-start.17 = (bf16[256,384]{1,0:T(8,128)(2,1)S(1)}, bf16[256,384]{1,0:T(8,128)(2,1)S(1)}, u32[]{:S(2)}, u32[]{:S(2)}) collective-permute-start(bf16[256,384]{1,0:T(8,128)(2,1)S(1)} %get-tuple-element.70), channel_id=1, source_target_pairs={{0,8},{1,9},{2,34},{3,35},{4,12},{5,13},{6,38},{7,39},{8,0},{9,1},... | collective-permute-start | bytes 589832 | tf_op jit(solution)/shard_map/ppermute | solution.py:71
  58.4 1.7 %collective-permute-start.18 = (bf16[256,384]{1,0:T(8,128)(2,1)S(1)}, bf16[256,384]{1,0:T(8,128)(2,1)S(1)}, u32[]{:S(2)}, u32[]{:S(2)}) collective-permute-start(bf16[256,384]{1,0:T(8,128)(2,1)S(1)} %get-tuple-element.71), channel_id=1, source_target_pairs={{0,24},{1,25},{2,98},{3,99},{4,28},{5,29},{6,102},{7,103},{8,16},{... | collective-permute-start | bytes 589832 | tf_op jit(solution)/shard_map/ppermute | solution.py:71
  60.1 1.1 %collective-permute-start.19 = (bf16[256,384]{1,0:T(8,128)(2,1)S(1)}, bf16[256,384]{1,0:T(8,128)(2,1)S(1)}, u32[]{:S(2)}, u32[]{:S(2)}) collective-permute-start(bf16[256,384]{1,0:T(8,128)(2,1)S(1)} %get-tuple-element.72), channel_id=1, source_target_pairs={{0,16},{1,17},{2,66},{3,67},{4,20},{5,21},{6,70},{7,71},{8,24},{9,... | collective-permute-start | bytes 589832 | tf_op jit(solution)/shard_map/ppermute | solution.py:71
  61.2 5.8 %key_grads.1 = (bf16[1024,384]{1,0:T(8,128)(2,1)S(1)}, bf16[1024,384]{1,0:T(8,128)(2,1)}, f32[8,128]{1,0:T(8,128)S(1)}) custom-call(s32[64]{0:T(128)S(1)} %dynamic-slice_bitcast_fusion.info, s32[32,128]{1,0:T(8,128)S(1)} %get-tuple-element.50.lists, bf16[8,3,512,128]{3,2,1,0:T(8,128)(2,1)S(1)} %get-tuple-element.63.probs_in, ...), custom_call_target="tpu_custom_call" | custom-call | flops 5750000128 | tf_op jit(solution)/shard_map/key_grads/pallas_call | solution.py:432
  67.1 0.3 collective-permute-done.18.refs_2_
  67.4 0.8 sum.1
  68.2 4.4 %collective-permute-start.22 = (bf16[256,384]{1,0:T(8,128)(2,1)}, bf16[256,384]{1,0:T(8,128)(2,1)}, u32[]{:S(2)}, u32[]{:S(2)}) collective-permute-start(bf16[256,384]{1,0:T(8,128)(2,1)} %get-tuple-element.74), channel_id=1, source_target_pairs={{0,64},{1,65},{2,18},{3,19},{4,68},{5,69},{6,22},{7,23},{8,72},{9,... | collective-permute-start | bytes 589832 | tf_op jit(solution)/shard_map/ppermute | solution.py:71
  72.6 0.1 collective-permute-start.21
  72.7 2.0 %collective-permute-start.15 = (bf16[1024,384]{1,0:T(8,128)(2,1)}, bf16[1024,384]{1,0:T(8,128)(2,1)}, u32[]{:S(2)}, u32[]{:S(2)}) collective-permute-start(bf16[1024,384]{1,0:T(8,128)(2,1)} %get-tuple-element.68), channel_id=1, source_target_pairs={{0,32},{1,33},{2,10},{3,11},{4,36},{5,37},{6,14},{7,15},{8,40},{9,... | collective-permute-start | bytes 2359304 | tf_op jit(solution)/shard_map/ppermute | solution.py:71
  74.8 1.8 %collective-permute-start.13 = (bf16[512,384]{1,0:T(8,128)(2,1)}, bf16[512,384]{1,0:T(8,128)(2,1)}, u32[]{:S(2)}, u32[]{:S(2)}) collective-permute-start(bf16[512,384]{1,0:T(8,128)(2,1)} %get-tuple-element.62), channel_id=1, source_target_pairs={{0,24},{1,25},{2,98},{3,99},{4,28},{5,29},{6,102},{7,103},{8,16},{... | collective-permute-start | bytes 1179656 | tf_op jit(solution)/shard_map/ppermute | solution.py:71
  76.6 0.1 collective-permute-done.22
  76.7 4.8 %collective-permute-done.21 = bf16[256,384]{1,0:T(8,128)(2,1)} collective-permute-done((bf16[256,384]{1,0:T(8,128)(2,1)}, bf16[256,384]{1,0:T(8,128)(2,1)}, u32[]{:S(2)}, u32[]{:S(2)}) %collective-permute-start.21) | collective-permute-done | bytes 196640 | tf_op jit(solution)/shard_map/ppermute | solution.py:71
  81.4 1.3 %add_convert_fusion.1.refs_0_ = bf16[256,384]{1,0:T(8,128)(2,1)S(1)} fusion(bf16[256,384]{1,0:T(8,128)(2,1)} %collective-permute-done.22, bf16[256,384]{1,0:T(8,128)(2,1)} %collective-permute-done.21, bf16[256,384]{1,0:T(8,128)(2,1)} %collective-permute-done.20, bf16[256,384]{1,0:T(8,128)(2,1)} %get-tuple-element.74), kind=kLoop, calls=%fused_computation.2 | loop fusion | flops 786432 | bytes 983040 | tf_op jit(solution)/shard_map/convert_element_type | solution.py:674
  82.8 1.0 copy-done.15
  83.8 0.9 weights.1
  84.7 1.6 %collective-permute-start.23 = (bf16[192,384]{1,0:T(8,128)(2,1)S(1)}, bf16[192,384]{1,0:T(8,128)(2,1)S(1)}, u32[]{:S(2)}, u32[]{:S(2)}) collective-permute-start(bf16[192,384]{1,0:T(8,128)(2,1)S(1)} %get-tuple-element.77), channel_id=1, source_target_pairs={{0,8},{1,9},{2,34},{3,35},{4,12},{5,13},{6,38},{7,39},{8,0},{9,1},... | collective-permute-start | bytes 442376 | tf_op jit(solution)/shard_map/ppermute | solution.py:71
  86.3 0.6 collective-permute-start.24
  86.9 2.0 %collective-permute-start.25 = (bf16[192,384]{1,0:T(8,128)(2,1)S(1)}, bf16[192,384]{1,0:T(8,128)(2,1)S(1)}, u32[]{:S(2)}, u32[]{:S(2)}) collective-permute-start(bf16[192,384]{1,0:T(8,128)(2,1)S(1)} %get-tuple-element.79), channel_id=1, source_target_pairs={{0,16},{1,17},{2,66},{3,67},{4,20},{5,21},{6,70},{7,71},{8,24},{9,... | collective-permute-start | bytes 442376 | tf_op jit(solution)/shard_map/ppermute | solution.py:71
  88.9 1.0 add_convert_fusion.5
  89.9 1.6 %collective-permute-start.14 = (bf16[256,384]{1,0:T(8,128)(2,1)S(1)}, bf16[256,384]{1,0:T(8,128)(2,1)S(1)}, u32[]{:S(2)}, u32[]{:S(2)}) collective-permute-start(bf16[256,384]{1,0:T(8,128)(2,1)S(1)} %add_convert_fusion.5), channel_id=1, source_target_pairs={{0,8},{1,9},{2,34},{3,35},{4,12},{5,13},{6,38},{7,39},{8,0},{9,1},... | collective-permute-start | bytes 589832 | tf_op jit(solution)/shard_map/ppermute | solution.py:71
  91.4 1.0 collective-permute-done.15
  92.4 1.1 %add_convert_fusion.refs_4_ = bf16[512,384]{1,0:T(8,128)(2,1)S(1)} fusion(bf16[1024,384]{1,0:T(8,128)(2,1)} %collective-permute-done.15, bf16[1024,384]{1,0:T(8,128)(2,1)S(1)} %get-tuple-element.67), kind=kLoop, calls=%fused_computation.1 | loop fusion | flops 786432 | bytes 1179648 | tf_op jit(solution)/shard_map/convert_element_type | solution.py:86
  93.5 3.2 %collective-permute-start.16 = (bf16[512,384]{1,0:T(8,128)(2,1)S(1)}, bf16[512,384]{1,0:T(8,128)(2,1)S(1)}, u32[]{:S(2)}, u32[]{:S(2)}) collective-permute-start(bf16[512,384]{1,0:T(8,128)(2,1)S(1)} %add_convert_fusion.refs_4_), channel_id=1, source_target_pairs={{0,96},{1,97},{2,26},{3,27},{4,100},{5,101},{6,30},{7,31},{8,104},... | collective-permute-start | bytes 1179656 | tf_op jit(solution)/shard_map/ppermute | solution.py:71
  96.7 0.1 split.1
  96.9 3.3 %collective-permute-start.26 = (bf16[96,384]{1,0:T(8,128)(2,1)S(1)}, bf16[96,384]{1,0:T(8,128)(2,1)S(1)}, u32[]{:S(2)}, u32[]{:S(2)}) collective-permute-start(bf16[96,384]{1,0:T(8,128)(2,1)S(1)} %get-tuple-element.81), channel_id=1, source_target_pairs={{0,1},{1,0},{2,3},{3,2},{4,5},{5,4},{6,7},{7,6},{8,9},{9,8},{10,11... | collective-permute-start | bytes 221192 | tf_op jit(solution)/shard_map/ppermute | solution.py:679
  100.1 1.7 %fusion = bf16[1,256,384]{2,1,0:T(8,128)(2,1)} fusion(bf16[256,384]{1,0:T(8,128)(2,1)S(1)} %collective-permute-done.14, bf16[512,384]{1,0:T(8,128)(2,1)} %collective-permute-done.13, bf16[512,384]{1,0:T(8,128)(2,1)S(1)} %get-tuple-element.61), kind=kLoop, calls=%fused_computation.7 | loop fusion | flops 589824 | bytes 786432 | tf_op jit(solution)/shard_map/broadcast_in_dim | solution.py:680
  101.8 1.0 collective-permute-done.26
  102.8 0.7 convert_add_fusion
  103.5 1.9 %fusion.2 = (bf16[1,256,384]{2,1,0:T(8,128)(2,1)}, bf16[1,256,384]{2,1,0:T(8,128)(2,1)}) fusion(bf16[512,384]{1,0:T(8,128)(2,1)S(1)} %collective-permute-done.16, bf16[1024,384]{1,0:T(8,128)(2,1)} %collective-permute-done.15, bf16[1024,384]{1,0:T(8,128)(2,1)S(1)} %get-tuple-element.67), kind=kLoop, calls=%fused_computation.9 | loop fusion | flops 1179648 | bytes 1572864 | tf_op jit(solution)/shard_map/broadcast_in_dim | solution.py:682
  (43 shorter events, 0.1 us)
Async XLA Ops:
  0.6 1.7 %copy-start = (bf16[3072,384]{1,0:T(8,128)(2,1)S(1)}, bf16[3072,384]{1,0:T(8,128)(2,1)}, u32[]{:S(2)}) copy-start(bf16[3072,384]{1,0:T(8,128)(2,1)} %param.16) | copy-start | bytes 7077892
  0.6 3.1 %copy-start.13 = (s32[4,2]{0,1:T(2,128)S(1)}, s32[4,2]{0,1:T(2,128)}, u32[]{:S(2)}) copy-start(s32[4,2]{0,1:T(2,128)} %param.14) | copy-start | bytes 100
  0.7 3.1 %copy-start.12 = (s32[4,32]{1,0:T(4,128)S(1)}, s32[4,32]{1,0:T(4,128)}, u32[]{:S(2)}) copy-start(s32[4,32]{1,0:T(4,128)} %kv_list.1) | copy-start | bytes 1540
  0.7 3.1 %copy-start.9 = (bf16[1,256,384]{2,1,0:T(8,128)(2,1)S(1)}, bf16[1,256,384]{2,1,0:T(8,128)(2,1)}, u32[]{:S(2)}) copy-start(bf16[1,256,384]{2,1,0:T(8,128)(2,1)} %param.12) | copy-start | bytes 589828
  0.7 3.1 %copy-start.8 = (bf16[1,256,384]{2,1,0:T(8,128)(2,1)S(1)}, bf16[1,256,384]{2,1,0:T(8,128)(2,1)}, u32[]{:S(2)}) copy-start(bf16[1,256,384]{2,1,0:T(8,128)(2,1)} %param.9) | copy-start | bytes 589828
  3.8 3.3 %copy-start.10 = (bf16[1,256,384]{2,1,0:T(8,128)(2,1)S(1)}, bf16[1,256,384]{2,1,0:T(8,128)(2,1)}, u32[]{:S(2)}) copy-start(bf16[1,256,384]{2,1,0:T(8,128)(2,1)} %param.10) | copy-start | bytes 589828
  3.8 3.3 %copy-start.11 = (bf16[1,256,384]{2,1,0:T(8,128)(2,1)S(1)}, bf16[1,256,384]{2,1,0:T(8,128)(2,1)}, u32[]{:S(2)}) copy-start(bf16[1,256,384]{2,1,0:T(8,128)(2,1)} %param.11) | copy-start | bytes 589828
  3.9 15.2 %copy-start.4 = (bf16[592,384]{1,0:T(8,128)(2,1)}, bf16[592,384]{1,0:T(8,128)(2,1)S(1)}, u32[]{:S(2)}) copy-start(bf16[592,384]{1,0:T(8,128)(2,1)S(1)} %get-tuple-element.43.refs_0_) | copy-start | bytes 1363972
  3.9 15.2 %collective-permute-start.3 = (bf16[592,384]{1,0:T(8,128)(2,1)S(1)}, bf16[592,384]{1,0:T(8,128)(2,1)S(1)}, u32[]{:S(2)}, u32[]{:S(2)}) collective-permute-start(bf16[592,384]{1,0:T(8,128)(2,1)S(1)} %get-tuple-element.43.refs_0_), channel_id=1, source_target_pairs={{0,24},{1,25},{2,98},{3,99},{4,28},{5,29},{6,102},{7,103},{8,16},{... | collective-permute-start | bytes 1363976 | tf_op jit(solution)/shard_map/ppermute | solution.py:71
  6.8 12.6 %collective-permute-start = (bf16[592,384]{1,0:T(8,128)(2,1)S(1)}, bf16[592,384]{1,0:T(8,128)(2,1)S(1)}, u32[]{:S(2)}, u32[]{:S(2)}) collective-permute-start(bf16[592,384]{1,0:T(8,128)(2,1)S(1)} %get-tuple-element.43.refs_0_), channel_id=1, source_target_pairs={{0,8},{1,9},{2,34},{3,35},{4,12},{5,13},{6,38},{7,39},{8,0},{9,1},... | collective-permute-start | bytes 1363976 | tf_op jit(solution)/shard_map/ppermute | solution.py:71
  7.1 12.0 %collective-permute-start.4 = (bf16[512,384]{1,0:T(8,128)(2,1)S(1)}, bf16[512,384]{1,0:T(8,128)(2,1)S(1)}, u32[]{:S(2)}, u32[]{:S(2)}) collective-permute-start(bf16[512,384]{1,0:T(8,128)(2,1)S(1)} %stack.1.refs_4_.refs_0_), channel_id=1, source_target_pairs={{0,32},{1,33},{2,10},{3,11},{4,36},{5,37},{6,14},{7,15},{8,40},{9,... | collective-permute-start | bytes 1179656 | tf_op jit(solution)/shard_map/ppermute | solution.py:71
  9.1 10.0 %collective-permute-start.1 = (bf16[512,384]{1,0:T(8,128)(2,1)S(1)}, bf16[512,384]{1,0:T(8,128)(2,1)}, u32[]{:S(2)}, u32[]{:S(2)}) collective-permute-start(bf16[512,384]{1,0:T(8,128)(2,1)S(1)} %stack.1.refs_4_.refs_0_), channel_id=1, source_target_pairs={{0,96},{1,97},{2,26},{3,27},{4,100},{5,101},{6,30},{7,31},{8,104},... | collective-permute-start | bytes 1179656 | tf_op jit(solution)/shard_map/ppermute | solution.py:71
  11.6 0.7 copy-start.6
  12.3 6.5 %collective-permute-start.2 = (bf16[80,384]{1,0:T(8,128)(2,1)S(1)}, bf16[80,384]{1,0:T(8,128)(2,1)S(1)}, u32[]{:S(2)}, u32[]{:S(2)}) collective-permute-start(bf16[80,384]{1,0:T(8,128)(2,1)S(1)} %get-tuple-element.44), channel_id=1, source_target_pairs={{0,16},{1,17},{2,66},{3,67},{4,20},{5,21},{6,70},{7,71},{8,24},{9,... | collective-permute-start | bytes 184328 | tf_op jit(solution)/shard_map/ppermute | solution.py:71
  19.1 0.7 copy-start.1
  19.8 12.5 %collective-permute-start.5 = (bf16[592,384]{1,0:T(8,128)(2,1)S(1)}, bf16[592,384]{1,0:T(8,128)(2,1)}, u32[]{:S(2)}, u32[]{:S(2)}) collective-permute-start(bf16[592,384]{1,0:T(8,128)(2,1)S(1)} %get-tuple-element.45.refs_1_), channel_id=1, source_target_pairs={{0,24},{1,25},{2,98},{3,99},{4,28},{5,29},{6,102},{7,103},{8,16},{... | collective-permute-start | bytes 1363976 | tf_op jit(solution)/shard_map/ppermute | solution.py:71
  23.5 8.7 %collective-permute-start.6 = (bf16[512,384]{1,0:T(8,128)(2,1)}, bf16[512,384]{1,0:T(8,128)(2,1)}, u32[]{:S(2)}, u32[]{:S(2)}) collective-permute-start(bf16[512,384]{1,0:T(8,128)(2,1)} %get-tuple-element.51.refs_6_.refs_2_), channel_id=1, source_target_pairs={{0,32},{1,33},{2,10},{3,11},{4,36},{5,37},{6,14},{7,15},{8,40},{9,... | collective-permute-start | bytes 1179656 | tf_op jit(solution)/shard_map/ppermute | solution.py:71
  26.0 1.0 copy-start.3
  27.0 1.0 copy-start.5
  27.8 4.5 %copy-start.2 = (bf16[512,384]{1,0:T(8,128)(2,1)S(1)}, bf16[512,384]{1,0:T(8,128)(2,1)}, u32[]{:S(2)}) copy-start(bf16[512,384]{1,0:T(8,128)(2,1)} %copy-done.1) | copy-start | bytes 1179652
  27.8 4.5 %copy-start.7 = (bf16[512,384]{1,0:T(8,128)(2,1)S(1)}, bf16[512,384]{1,0:T(8,128)(2,1)}, u32[]{:S(2)}) copy-start(bf16[512,384]{1,0:T(8,128)(2,1)} %copy-done.6) | copy-start | bytes 1179652
  28.1 7.6 %collective-permute-start.7 = (bf16[384,384]{1,0:T(8,128)(2,1)S(1)}, bf16[384,384]{1,0:T(8,128)(2,1)S(1)}, u32[]{:S(2)}, u32[]{:S(2)}) collective-permute-start(bf16[384,384]{1,0:T(8,128)(2,1)S(1)} %get-tuple-element.53), channel_id=1, source_target_pairs={{0,32},{1,33},{2,10},{3,11},{4,36},{5,37},{6,14},{7,15},{8,40},{9,... | collective-permute-start | bytes 884744 | tf_op jit(solution)/shard_map/ppermute | solution.py:71
  28.5 11.1 %collective-permute-start.8 = (bf16[384,384]{1,0:T(8,128)(2,1)S(1)}, bf16[384,384]{1,0:T(8,128)(2,1)S(1)}, u32[]{:S(2)}, u32[]{:S(2)}) collective-permute-start(bf16[384,384]{1,0:T(8,128)(2,1)S(1)} %get-tuple-element.54), channel_id=1, source_target_pairs={{0,96},{1,97},{2,26},{3,27},{4,100},{5,101},{6,30},{7,31},{8,104},... | collective-permute-start | bytes 884744 | tf_op jit(solution)/shard_map/ppermute | solution.py:71
  30.4 9.2 %collective-permute-start.9 = (bf16[384,384]{1,0:T(8,128)(2,1)S(1)}, bf16[384,384]{1,0:T(8,128)(2,1)S(1)}, u32[]{:S(2)}, u32[]{:S(2)}) collective-permute-start(bf16[384,384]{1,0:T(8,128)(2,1)S(1)} %get-tuple-element.55), channel_id=1, source_target_pairs={{0,64},{1,65},{2,18},{3,19},{4,68},{5,69},{6,22},{7,23},{8,72},{9,... | collective-permute-start | bytes 884744 | tf_op jit(solution)/shard_map/ppermute | solution.py:71
  44.5 0.7 copy-start.14
  45.2 5.8 %collective-permute-start.12 = (f32[16,1024]{1,0:T(8,128)S(1)}, f32[16,1024]{1,0:T(8,128)S(1)}, u32[]{:S(2)}, u32[]{:S(2)}) collective-permute-start(f32[16,1024]{1,0:T(8,128)S(1)} %get-tuple-element.57.refs_4_.refs_0_), channel_id=1, source_target_pairs={{0,16},{1,17},{2,66},{3,67},{4,20},{5,21},{6,70},{7,71},{8,24},{9,... | collective-permute-start | bytes 196616 | tf_op jit(solution)/shard_map/ppermute | solution.py:71
  45.9 5.7 %collective-permute-start.11 = (f32[16,1024]{1,0:T(8,128)S(1)}, f32[16,1024]{1,0:T(8,128)S(1)}, u32[]{:S(2)}, u32[]{:S(2)}) collective-permute-start(f32[16,1024]{1,0:T(8,128)S(1)} %get-tuple-element.57.refs_4_.refs_0_), channel_id=1, source_target_pairs={{0,24},{1,25},{2,98},{3,99},{4,28},{5,29},{6,102},{7,103},{8,16},{... | collective-permute-start | bytes 196616 | tf_op jit(solution)/shard_map/ppermute | solution.py:71
  47.2 4.5 %collective-permute-start.10 = (f32[16,1024]{1,0:T(8,128)S(1)}, f32[16,1024]{1,0:T(8,128)S(1)}, u32[]{:S(2)}, u32[]{:S(2)}) collective-permute-start(f32[16,1024]{1,0:T(8,128)S(1)} %get-tuple-element.57.refs_4_.refs_0_), channel_id=1, source_target_pairs={{0,8},{1,9},{2,34},{3,35},{4,12},{5,13},{6,38},{7,39},{8,0},{9,1},... | collective-permute-start | bytes 196616 | tf_op jit(solution)/shard_map/ppermute | solution.py:71
  57.1 9.9 %collective-permute-start.17 = (bf16[256,384]{1,0:T(8,128)(2,1)S(1)}, bf16[256,384]{1,0:T(8,128)(2,1)S(1)}, u32[]{:S(2)}, u32[]{:S(2)}) collective-permute-start(bf16[256,384]{1,0:T(8,128)(2,1)S(1)} %get-tuple-element.70), channel_id=1, source_target_pairs={{0,8},{1,9},{2,34},{3,35},{4,12},{5,13},{6,38},{7,39},{8,0},{9,1},... | collective-permute-start | bytes 589832 | tf_op jit(solution)/shard_map/ppermute | solution.py:71
  58.4 9.0 %collective-permute-start.18 = (bf16[256,384]{1,0:T(8,128)(2,1)S(1)}, bf16[256,384]{1,0:T(8,128)(2,1)S(1)}, u32[]{:S(2)}, u32[]{:S(2)}) collective-permute-start(bf16[256,384]{1,0:T(8,128)(2,1)S(1)} %get-tuple-element.71), channel_id=1, source_target_pairs={{0,24},{1,25},{2,98},{3,99},{4,28},{5,29},{6,102},{7,103},{8,16},{... | collective-permute-start | bytes 589832 | tf_op jit(solution)/shard_map/ppermute | solution.py:71
  60.1 7.3 %collective-permute-start.19 = (bf16[256,384]{1,0:T(8,128)(2,1)S(1)}, bf16[256,384]{1,0:T(8,128)(2,1)S(1)}, u32[]{:S(2)}, u32[]{:S(2)}) collective-permute-start(bf16[256,384]{1,0:T(8,128)(2,1)S(1)} %get-tuple-element.72), channel_id=1, source_target_pairs={{0,16},{1,17},{2,66},{3,67},{4,20},{5,21},{6,70},{7,71},{8,24},{9,... | collective-permute-start | bytes 589832 | tf_op jit(solution)/shard_map/ppermute | solution.py:71
  68.2 8.5 %collective-permute-start.22 = (bf16[256,384]{1,0:T(8,128)(2,1)}, bf16[256,384]{1,0:T(8,128)(2,1)}, u32[]{:S(2)}, u32[]{:S(2)}) collective-permute-start(bf16[256,384]{1,0:T(8,128)(2,1)} %get-tuple-element.74), channel_id=1, source_target_pairs={{0,64},{1,65},{2,18},{3,19},{4,68},{5,69},{6,22},{7,23},{8,72},{9,... | collective-permute-start | bytes 589832 | tf_op jit(solution)/shard_map/ppermute | solution.py:71
  72.6 8.8 %collective-permute-start.21 = (bf16[256,384]{1,0:T(8,128)(2,1)}, bf16[256,384]{1,0:T(8,128)(2,1)}, u32[]{:S(2)}, u32[]{:S(2)}) collective-permute-start(bf16[256,384]{1,0:T(8,128)(2,1)} %get-tuple-element.74), channel_id=1, source_target_pairs={{0,96},{1,97},{2,26},{3,27},{4,100},{5,101},{6,30},{7,31},{8,104},... | collective-permute-start | bytes 589832 | tf_op jit(solution)/shard_map/ppermute | solution.py:71
  72.7 8.7 %collective-permute-start.20 = (bf16[256,384]{1,0:T(8,128)(2,1)}, bf16[256,384]{1,0:T(8,128)(2,1)}, u32[]{:S(2)}, u32[]{:S(2)}) collective-permute-start(bf16[256,384]{1,0:T(8,128)(2,1)} %get-tuple-element.74), channel_id=1, source_target_pairs={{0,32},{1,33},{2,10},{3,11},{4,36},{5,37},{6,14},{7,15},{8,40},{9,... | collective-permute-start | bytes 589832 | tf_op jit(solution)/shard_map/ppermute | solution.py:71
  72.7 19.7 %collective-permute-start.15 = (bf16[1024,384]{1,0:T(8,128)(2,1)}, bf16[1024,384]{1,0:T(8,128)(2,1)}, u32[]{:S(2)}, u32[]{:S(2)}) collective-permute-start(bf16[1024,384]{1,0:T(8,128)(2,1)} %get-tuple-element.68), channel_id=1, source_target_pairs={{0,32},{1,33},{2,10},{3,11},{4,36},{5,37},{6,14},{7,15},{8,40},{9,... | collective-permute-start | bytes 2359304 | tf_op jit(solution)/shard_map/ppermute | solution.py:71
  74.8 14.1 %collective-permute-start.13 = (bf16[512,384]{1,0:T(8,128)(2,1)}, bf16[512,384]{1,0:T(8,128)(2,1)}, u32[]{:S(2)}, u32[]{:S(2)}) collective-permute-start(bf16[512,384]{1,0:T(8,128)(2,1)} %get-tuple-element.62), channel_id=1, source_target_pairs={{0,24},{1,25},{2,98},{3,99},{4,28},{5,29},{6,102},{7,103},{8,16},{... | collective-permute-start | bytes 1179656 | tf_op jit(solution)/shard_map/ppermute | solution.py:71
  82.8 1.0 copy-start.15
  84.7 12.0 %collective-permute-start.23 = (bf16[192,384]{1,0:T(8,128)(2,1)S(1)}, bf16[192,384]{1,0:T(8,128)(2,1)S(1)}, u32[]{:S(2)}, u32[]{:S(2)}) collective-permute-start(bf16[192,384]{1,0:T(8,128)(2,1)S(1)} %get-tuple-element.77), channel_id=1, source_target_pairs={{0,8},{1,9},{2,34},{3,35},{4,12},{5,13},{6,38},{7,39},{8,0},{9,1},... | collective-permute-start | bytes 442376 | tf_op jit(solution)/shard_map/ppermute | solution.py:71
  86.3 10.4 %collective-permute-start.24 = (bf16[192,384]{1,0:T(8,128)(2,1)S(1)}, bf16[192,384]{1,0:T(8,128)(2,1)S(1)}, u32[]{:S(2)}, u32[]{:S(2)}) collective-permute-start(bf16[192,384]{1,0:T(8,128)(2,1)S(1)} %get-tuple-element.78), channel_id=1, source_target_pairs={{0,24},{1,25},{2,98},{3,99},{4,28},{5,29},{6,102},{7,103},{8,16},{... | collective-permute-start | bytes 442376 | tf_op jit(solution)/shard_map/ppermute | solution.py:71
  86.9 9.8 %collective-permute-start.25 = (bf16[192,384]{1,0:T(8,128)(2,1)S(1)}, bf16[192,384]{1,0:T(8,128)(2,1)S(1)}, u32[]{:S(2)}, u32[]{:S(2)}) collective-permute-start(bf16[192,384]{1,0:T(8,128)(2,1)S(1)} %get-tuple-element.79), channel_id=1, source_target_pairs={{0,16},{1,17},{2,66},{3,67},{4,20},{5,21},{6,70},{7,71},{8,24},{9,... | collective-permute-start | bytes 442376 | tf_op jit(solution)/shard_map/ppermute | solution.py:71
  89.9 10.3 %collective-permute-start.14 = (bf16[256,384]{1,0:T(8,128)(2,1)S(1)}, bf16[256,384]{1,0:T(8,128)(2,1)S(1)}, u32[]{:S(2)}, u32[]{:S(2)}) collective-permute-start(bf16[256,384]{1,0:T(8,128)(2,1)S(1)} %add_convert_fusion.5), channel_id=1, source_target_pairs={{0,8},{1,9},{2,34},{3,35},{4,12},{5,13},{6,38},{7,39},{8,0},{9,1},... | collective-permute-start | bytes 589832 | tf_op jit(solution)/shard_map/ppermute | solution.py:71
  93.5 10.0 %collective-permute-start.16 = (bf16[512,384]{1,0:T(8,128)(2,1)S(1)}, bf16[512,384]{1,0:T(8,128)(2,1)S(1)}, u32[]{:S(2)}, u32[]{:S(2)}) collective-permute-start(bf16[512,384]{1,0:T(8,128)(2,1)S(1)} %add_convert_fusion.refs_4_), channel_id=1, source_target_pairs={{0,96},{1,97},{2,26},{3,27},{4,100},{5,101},{6,30},{7,31},{8,104},... | collective-permute-start | bytes 1179656 | tf_op jit(solution)/shard_map/ppermute | solution.py:71
  96.9 5.9 %collective-permute-start.26 = (bf16[96,384]{1,0:T(8,128)(2,1)S(1)}, bf16[96,384]{1,0:T(8,128)(2,1)S(1)}, u32[]{:S(2)}, u32[]{:S(2)}) collective-permute-start(bf16[96,384]{1,0:T(8,128)(2,1)S(1)} %get-tuple-element.81), channel_id=1, source_target_pairs={{0,1},{1,0},{2,3},{3,2},{4,5},{5,4},{6,7},{7,6},{8,9},{9,8},{10,11... | collective-permute-start | bytes 221192 | tf_op jit(solution)/shard_map/ppermute | solution.py:679

commit v6 on v5

--- a/solution.py
+++ b/solution.py
@@ -25,7 +25,7 @@
 MIB = 1 << 20
 CHUNK = 192
 PADDED = 256
-PAIRS = 4
+PAIRS = 8
 
 
 def roles(ctx, core):

time: 106 us -> 105 us (level)
  transfers between devices with their start and end apart: 27 -> 27, of which waited for: 11 -> 11; matrix products, arithmetic and copies ran while one was open for 6% -> 6% of each run, Pallas kernels for 13% -> 12%
where the time goes in v6:
time: 105 us
  starting transfers between devices  46.6 us (44%)
  Pallas kernels  23.8 us (23%)
  waiting for transfers between devices  18.1 us (17%)
  other arithmetic  7.65 us (7%)
  local copies, waits for them, and re-layouts  6.34 us (6%)
  matrix products  1.44 us (1%)
    ppermute x26, starting transfers between devices, send(): return lax.ppermute(array, ('ctx', 'head', 'dp'), pairs)  43.3 us
    pallas_call x13, Pallas kernels, call(): pl.pallas_call(kernel, name=name, grid=grid, out_shape=[jax.ShapeDtypeStr...  23.8 us
    ppermute x26, waiting for transfers between devices, send(): return lax.ppermute(array, ('ctx', 'head', 'dp'), pairs)  17.1 us
    unnamed x32, local copies, waits for them, and re-layouts  5.65 us
    ppermute x1, starting transfers between devices, body(): lax.ppermute(other, 'dp', [(0, 1), (1, 0)]).astype(F32)  3.29 us
  transfers between devices with their start and end apart: 27, of which 11 were waited for; matrix products, arithmetic and copies ran while one was open for 6% of the time, Pallas kernels for 12%

profile of v6, /device:TPU:0, one launch (start us, length us, event | category | flops | bytes accessed | tf_op | source)
XLA Modules:
  0.0 104.8 jit_solution(13207022117991237471)
XLA Ops:
  0.6 0.0 copy-start
  0.7 1.6 %copy-done = bf16[3072,384]{1,0:T(8,128)(2,1)S(1)} copy-done((bf16[3072,384]{1,0:T(8,128)(2,1)S(1)}, bf16[3072,384]{1,0:T(8,128)(2,1)}, u32[]{:S(2)}) %copy-start) | copy-done | bytes 2359320
  2.3 1.4 %convolution_convert_fusion.cond = bf16[64,384]{1,0:T(8,128)(2,1)S(1)} fusion(bf16[3072,384]{1,0:T(8,128)(2,1)S(1)} %copy-done, bf16[1,64,3072]{2,1,0:T(8,128)(2,1)} %param.15), kind=kOutput, calls=%fused_computation | convolution fusion | flops 151019520 | bytes 2801664 | tf_op jit(solution)/shard_map/dot_general | solution.py:654
  3.8 0.1 pack.1
  3.9 2.9 %collective-permute-start.3 = (bf16[592,384]{1,0:T(8,128)(2,1)S(1)}, bf16[592,384]{1,0:T(8,128)(2,1)S(1)}, u32[]{:S(2)}, u32[]{:S(2)}) collective-permute-start(bf16[592,384]{1,0:T(8,128)(2,1)S(1)} %get-tuple-element.43.refs_0_), channel_id=1, source_target_pairs={{0,24},{1,25},{2,98},{3,99},{4,28},{5,29},{6,102},{7,103},{8,16},{... | collective-permute-start | bytes 1363976 | tf_op jit(solution)/shard_map/ppermute | solution.py:71
  6.8 0.2 collective-permute-start
  7.1 2.0 %collective-permute-start.4 = (bf16[512,384]{1,0:T(8,128)(2,1)S(1)}, bf16[512,384]{1,0:T(8,128)(2,1)S(1)}, u32[]{:S(2)}, u32[]{:S(2)}) collective-permute-start(bf16[512,384]{1,0:T(8,128)(2,1)S(1)} %stack.1.refs_4_.refs_0_), channel_id=1, source_target_pairs={{0,32},{1,33},{2,10},{3,11},{4,36},{5,37},{6,14},{7,15},{8,40},{9,... | collective-permute-start | bytes 1179656 | tf_op jit(solution)/shard_map/ppermute | solution.py:71
  9.1 2.5 %collective-permute-start.1 = (bf16[512,384]{1,0:T(8,128)(2,1)S(1)}, bf16[512,384]{1,0:T(8,128)(2,1)}, u32[]{:S(2)}, u32[]{:S(2)}) collective-permute-start(bf16[512,384]{1,0:T(8,128)(2,1)S(1)} %stack.1.refs_4_.refs_0_), channel_id=1, source_target_pairs={{0,96},{1,97},{2,26},{3,27},{4,100},{5,101},{6,30},{7,31},{8,104},... | collective-permute-start | bytes 1179656 | tf_op jit(solution)/shard_map/ppermute | solution.py:71
  11.6 0.7 copy-done.6
  12.3 1.7 %collective-permute-start.2 = (bf16[80,384]{1,0:T(8,128)(2,1)S(1)}, bf16[80,384]{1,0:T(8,128)(2,1)S(1)}, u32[]{:S(2)}, u32[]{:S(2)}) collective-permute-start(bf16[80,384]{1,0:T(8,128)(2,1)S(1)} %get-tuple-element.44), channel_id=1, source_target_pairs={{0,16},{1,17},{2,66},{3,67},{4,20},{5,21},{6,70},{7,71},{8,24},{9,... | collective-permute-start | bytes 184328 | tf_op jit(solution)/shard_map/ppermute | solution.py:71
  14.1 4.8 %collective-permute-done.2.refs_2_.refs_3_ = bf16[80,384]{1,0:T(8,128)(2,1)S(1)} collective-permute-done((bf16[80,384]{1,0:T(8,128)(2,1)S(1)}, bf16[80,384]{1,0:T(8,128)(2,1)S(1)}, u32[]{:S(2)}, u32[]{:S(2)}) %collective-permute-start.2) | collective-permute-done | bytes 61472 | tf_op jit(solution)/shard_map/ppermute | solution.py:71
  18.8 0.2 collective-permute-done.4.refs_4_.refs_5_.refs_1_
  19.1 0.4 collective-permute-done.refs_0_
  19.5 0.4 copy-done.1
  19.8 3.7 %collective-permute-start.5 = (bf16[592,384]{1,0:T(8,128)(2,1)S(1)}, bf16[592,384]{1,0:T(8,128)(2,1)}, u32[]{:S(2)}, u32[]{:S(2)}) collective-permute-start(bf16[592,384]{1,0:T(8,128)(2,1)S(1)} %get-tuple-element.45.refs_1_), channel_id=1, source_target_pairs={{0,24},{1,25},{2,98},{3,99},{4,28},{5,29},{6,102},{7,103},{8,16},{... | collective-permute-start | bytes 1363976 | tf_op jit(solution)/shard_map/ppermute | solution.py:71
  23.5 1.7 %collective-permute-start.6 = (bf16[512,384]{1,0:T(8,128)(2,1)}, bf16[512,384]{1,0:T(8,128)(2,1)}, u32[]{:S(2)}, u32[]{:S(2)}) collective-permute-start(bf16[512,384]{1,0:T(8,128)(2,1)} %get-tuple-element.51.refs_6_.refs_2_), channel_id=1, source_target_pairs={{0,32},{1,33},{2,10},{3,11},{4,36},{5,37},{6,14},{7,15},{8,40},{9,... | collective-permute-start | bytes 1179656 | tf_op jit(solution)/shard_map/ppermute | solution.py:71
  25.3 0.7 dynamic-slice_bitcast_fusion.info
  26.0 1.0 copy-done.3
  27.0 0.8 tokens.1
  27.8 0.2 copy-done.5
  28.0 0.1 join.1
  28.1 0.4 collective-permute-start.7
  28.5 1.9 %collective-permute-start.8 = (bf16[384,384]{1,0:T(8,128)(2,1)S(1)}, bf16[384,384]{1,0:T(8,128)(2,1)S(1)}, u32[]{:S(2)}, u32[]{:S(2)}) collective-permute-start(bf16[384,384]{1,0:T(8,128)(2,1)S(1)} %get-tuple-element.54), channel_id=1, source_target_pairs={{0,96},{1,97},{2,26},{3,27},{4,100},{5,101},{6,30},{7,31},{8,104},... | collective-permute-start | bytes 884744 | tf_op jit(solution)/shard_map/ppermute | solution.py:71
  30.4 1.9 %collective-permute-start.9 = (bf16[384,384]{1,0:T(8,128)(2,1)S(1)}, bf16[384,384]{1,0:T(8,128)(2,1)S(1)}, u32[]{:S(2)}, u32[]{:S(2)}) collective-permute-start(bf16[384,384]{1,0:T(8,128)(2,1)S(1)} %get-tuple-element.55), channel_id=1, source_target_pairs={{0,64},{1,65},{2,18},{3,19},{4,68},{5,69},{6,22},{7,23},{8,72},{9,... | collective-permute-start | bytes 884744 | tf_op jit(solution)/shard_map/ppermute | solution.py:71
  32.3 3.1 %slopes.1 = (f32[8,3,512,128]{3,2,1,0:T(8,128)S(1)}, bf16[1024,384]{1,0:T(8,128)(2,1)S(1)}) custom-call(s32[64]{0:T(128)S(1)} %dynamic-slice_bitcast_fusion.info, s32[32,128]{1,0:T(8,128)S(1)} %get-tuple-element.50.lists, bf16[592,384]{1,0:T(8,128)(2,1)S(1)} %copy-done.5, bf16[592,384]{1,0:T(8,128)(2,1)S(1)} %get-tuple-element.45.refs_1_, ...), custom_call_target="tpu_custom_call" | custom-call | flops 4600000000 | tf_op jit(solution)/shard_map/slopes/pallas_call | solution.py:432
  35.4 4.1 %collective-permute-done.8.refs_10_ = bf16[384,384]{1,0:T(8,128)(2,1)S(1)} collective-permute-done((bf16[384,384]{1,0:T(8,128)(2,1)S(1)}, bf16[384,384]{1,0:T(8,128)(2,1)S(1)}, u32[]{:S(2)}, u32[]{:S(2)}) %collective-permute-start.8) | collective-permute-done | bytes 294944 | tf_op jit(solution)/shard_map/ppermute | solution.py:71
  39.5 4.7 %scores.1 = (bf16[1024,384]{1,0:T(8,128)(2,1)S(1)}, f32[16,1024]{1,0:T(8,128)S(1)}, bf16[8,3,512,128]{3,2,1,0:T(8,128)(2,1)S(1)}, bf16[2,256,384]{2,1,0:T(8,128)(2,1)S(1)}) custom-call(s32[64]{0:T(128)S(1)} %dynamic-slice_bitcast_fusion.info, s32[32,128]{1,0:T(8,128)S(1)} %get-tuple-element.50.lists, bf16[592,384]{1,0:T(8,128)(2,1)S(1)} %copy-done.5, ...), custom_call_target="tpu_custom_call" | custom-call | flops 5750000128 | tf_op jit(solution)/shard_map/scores/pallas_call | solution.py:432
  44.3 0.7 copy-done.14
  45.0 0.7 collective-permute-start.12
  45.7 1.2 %collective-permute-start.11 = (f32[16,1024]{1,0:T(8,128)S(1)}, f32[16,1024]{1,0:T(8,128)S(1)}, u32[]{:S(2)}, u32[]{:S(2)}) collective-permute-start(f32[16,1024]{1,0:T(8,128)S(1)} %get-tuple-element.57.refs_4_.refs_0_), channel_id=1, source_target_pairs={{0,24},{1,25},{2,98},{3,99},{4,28},{5,29},{6,102},{7,103},{8,16},{... | collective-permute-start | bytes 196616 | tf_op jit(solution)/shard_map/ppermute | solution.py:71
  47.0 1.5 %collective-permute-start.10 = (f32[16,1024]{1,0:T(8,128)S(1)}, f32[16,1024]{1,0:T(8,128)S(1)}, u32[]{:S(2)}, u32[]{:S(2)}) collective-permute-start(f32[16,1024]{1,0:T(8,128)S(1)} %get-tuple-element.57.refs_4_.refs_0_), channel_id=1, source_target_pairs={{0,8},{1,9},{2,34},{3,35},{4,12},{5,13},{6,38},{7,39},{8,0},{9,1},... | collective-permute-start | bytes 196616 | tf_op jit(solution)/shard_map/ppermute | solution.py:71
  48.5 2.2 %turn.1 = (bf16[16,384,128]{2,1,0:T(8,128)(2,1)S(1)}, bf16[16,384,128]{2,1,0:T(8,128)(2,1)S(1)}) custom-call(bf16[512,384]{1,0:T(8,128)(2,1)S(1)} %copy-done.7, bf16[512,384]{1,0:T(8,128)(2,1)S(1)} %copy-done.2, bf16[512,384]{1,0:T(8,128)(2,1)} %get-tuple-element.51.refs_6_.refs_2_, bf16[512,384]{1,0:T(8,128)(2,1)} %collective-permute-done.6.refs_7_.refs_3_, ...), custom_call_target="tpu_custom_call" | custom-call | flops 1380000000 | tf_op jit(solution)/shard_map/turn/pallas_call | solution.py:432
  50.7 0.1 collective-permute-done.12.refs_3_
  50.8 0.7 collective-permute-done.11.refs_2_
  51.5 5.4 %query_grads.1 = (bf16[256,384]{1,0:T(8,128)(2,1)S(1)}, bf16[256,384]{1,0:T(8,128)(2,1)S(1)}, bf16[256,384]{1,0:T(8,128)(2,1)S(1)}, bf16[256,384]{1,0:T(8,128)(2...) custom-call(s32[64]{0:T(128)S(1)} %dynamic-slice_bitcast_fusion.info, ...), custom_call_target="tpu_custom_call" | custom-call | flops 5175000064 | tf_op jit(solution)/shard_map/query_grads/pallas_call | solution.py:432
  56.9 1.3 %collective-permute-start.17 = (bf16[256,384]{1,0:T(8,128)(2,1)S(1)}, bf16[256,384]{1,0:T(8,128)(2,1)S(1)}, u32[]{:S(2)}, u32[]{:S(2)}) collective-permute-start(bf16[256,384]{1,0:T(8,128)(2,1)S(1)} %get-tuple-element.70), channel_id=1, source_target_pairs={{0,8},{1,9},{2,34},{3,35},{4,12},{5,13},{6,38},{7,39},{8,0},{9,1},... | collective-permute-start | bytes 589832 | tf_op jit(solution)/shard_map/ppermute | solution.py:71
  58.2 1.7 %collective-permute-start.18 = (bf16[256,384]{1,0:T(8,128)(2,1)S(1)}, bf16[256,384]{1,0:T(8,128)(2,1)S(1)}, u32[]{:S(2)}, u32[]{:S(2)}) collective-permute-start(bf16[256,384]{1,0:T(8,128)(2,1)S(1)} %get-tuple-element.71), channel_id=1, source_target_pairs={{0,24},{1,25},{2,98},{3,99},{4,28},{5,29},{6,102},{7,103},{8,16},{... | collective-permute-start | bytes 589832 | tf_op jit(solution)/shard_map/ppermute | solution.py:71
  59.9 1.1 %collective-permute-start.19 = (bf16[256,384]{1,0:T(8,128)(2,1)S(1)}, bf16[256,384]{1,0:T(8,128)(2,1)S(1)}, u32[]{:S(2)}, u32[]{:S(2)}) collective-permute-start(bf16[256,384]{1,0:T(8,128)(2,1)S(1)} %get-tuple-element.72), channel_id=1, source_target_pairs={{0,16},{1,17},{2,66},{3,67},{4,20},{5,21},{6,70},{7,71},{8,24},{9,... | collective-permute-start | bytes 589832 | tf_op jit(solution)/shard_map/ppermute | solution.py:71
  61.0 5.5 %key_grads.1 = (bf16[1024,384]{1,0:T(8,128)(2,1)S(1)}, bf16[1024,384]{1,0:T(8,128)(2,1)}, f32[8,128]{1,0:T(8,128)S(1)}) custom-call(s32[64]{0:T(128)S(1)} %dynamic-slice_bitcast_fusion.info, s32[32,128]{1,0:T(8,128)S(1)} %get-tuple-element.50.lists, bf16[8,3,512,128]{3,2,1,0:T(8,128)(2,1)S(1)} %get-tuple-element.63.probs_in, ...), custom_call_target="tpu_custom_call" | custom-call | flops 5750000128 | tf_op jit(solution)/shard_map/key_grads/pallas_call | solution.py:432
  66.5 0.7 collective-permute-done.18.refs_2_
  67.1 0.8 sum.1
  67.9 4.2 %collective-permute-start.22 = (bf16[256,384]{1,0:T(8,128)(2,1)}, bf16[256,384]{1,0:T(8,128)(2,1)}, u32[]{:S(2)}, u32[]{:S(2)}) collective-permute-start(bf16[256,384]{1,0:T(8,128)(2,1)} %get-tuple-element.74), channel_id=1, source_target_pairs={{0,64},{1,65},{2,18},{3,19},{4,68},{5,69},{6,22},{7,23},{8,72},{9,... | collective-permute-start | bytes 589832 | tf_op jit(solution)/shard_map/ppermute | solution.py:71
  72.1 0.1 collective-permute-start.21
  72.2 2.0 %collective-permute-start.15 = (bf16[1024,384]{1,0:T(8,128)(2,1)}, bf16[1024,384]{1,0:T(8,128)(2,1)}, u32[]{:S(2)}, u32[]{:S(2)}) collective-permute-start(bf16[1024,384]{1,0:T(8,128)(2,1)} %get-tuple-element.68), channel_id=1, source_target_pairs={{0,32},{1,33},{2,10},{3,11},{4,36},{5,37},{6,14},{7,15},{8,40},{9,... | collective-permute-start | bytes 2359304 | tf_op jit(solution)/shard_map/ppermute | solution.py:71
  74.2 1.8 %collective-permute-start.13 = (bf16[512,384]{1,0:T(8,128)(2,1)}, bf16[512,384]{1,0:T(8,128)(2,1)}, u32[]{:S(2)}, u32[]{:S(2)}) collective-permute-start(bf16[512,384]{1,0:T(8,128)(2,1)} %get-tuple-element.62), channel_id=1, source_target_pairs={{0,24},{1,25},{2,98},{3,99},{4,28},{5,29},{6,102},{7,103},{8,16},{... | collective-permute-start | bytes 1179656 | tf_op jit(solution)/shard_map/ppermute | solution.py:71
  76.0 0.1 collective-permute-done.22
  76.2 4.7 %collective-permute-done.21 = bf16[256,384]{1,0:T(8,128)(2,1)} collective-permute-done((bf16[256,384]{1,0:T(8,128)(2,1)}, bf16[256,384]{1,0:T(8,128)(2,1)}, u32[]{:S(2)}, u32[]{:S(2)}) %collective-permute-start.21) | collective-permute-done | bytes 196640 | tf_op jit(solution)/shard_map/ppermute | solution.py:71
  80.9 1.3 %add_convert_fusion.1.refs_0_ = bf16[256,384]{1,0:T(8,128)(2,1)S(1)} fusion(bf16[256,384]{1,0:T(8,128)(2,1)} %collective-permute-done.22, bf16[256,384]{1,0:T(8,128)(2,1)} %collective-permute-done.21, bf16[256,384]{1,0:T(8,128)(2,1)} %collective-permute-done.20, bf16[256,384]{1,0:T(8,128)(2,1)} %get-tuple-element.74), kind=kLoop, calls=%fused_computation.2 | loop fusion | flops 786432 | bytes 983040 | tf_op jit(solution)/shard_map/convert_element_type | solution.py:674
  82.2 1.0 copy-done.15
  83.2 0.9 weights.1
  84.1 1.3 %collective-permute-start.23 = (bf16[192,384]{1,0:T(8,128)(2,1)S(1)}, bf16[192,384]{1,0:T(8,128)(2,1)S(1)}, u32[]{:S(2)}, u32[]{:S(2)}) collective-permute-start(bf16[192,384]{1,0:T(8,128)(2,1)S(1)} %get-tuple-element.77), channel_id=1, source_target_pairs={{0,8},{1,9},{2,34},{3,35},{4,12},{5,13},{6,38},{7,39},{8,0},{9,1},... | collective-permute-start | bytes 442376 | tf_op jit(solution)/shard_map/ppermute | solution.py:71
  85.4 0.8 collective-permute-start.24
  86.2 2.1 %collective-permute-start.25 = (bf16[192,384]{1,0:T(8,128)(2,1)S(1)}, bf16[192,384]{1,0:T(8,128)(2,1)S(1)}, u32[]{:S(2)}, u32[]{:S(2)}) collective-permute-start(bf16[192,384]{1,0:T(8,128)(2,1)S(1)} %get-tuple-element.79), channel_id=1, source_target_pairs={{0,16},{1,17},{2,66},{3,67},{4,20},{5,21},{6,70},{7,71},{8,24},{9,... | collective-permute-start | bytes 442376 | tf_op jit(solution)/shard_map/ppermute | solution.py:71
  88.3 1.0 add_convert_fusion.5
  89.3 1.3 %collective-permute-start.14 = (bf16[256,384]{1,0:T(8,128)(2,1)S(1)}, bf16[256,384]{1,0:T(8,128)(2,1)S(1)}, u32[]{:S(2)}, u32[]{:S(2)}) collective-permute-start(bf16[256,384]{1,0:T(8,128)(2,1)S(1)} %add_convert_fusion.5), channel_id=1, source_target_pairs={{0,8},{1,9},{2,34},{3,35},{4,12},{5,13},{6,38},{7,39},{8,0},{9,1},... | collective-permute-start | bytes 589832 | tf_op jit(solution)/shard_map/ppermute | solution.py:71
  90.5 1.3 %collective-permute-done.15 = bf16[1024,384]{1,0:T(8,128)(2,1)} collective-permute-done((bf16[1024,384]{1,0:T(8,128)(2,1)}, bf16[1024,384]{1,0:T(8,128)(2,1)}, u32[]{:S(2)}, u32[]{:S(2)}) %collective-permute-start.15) | collective-permute-done | bytes 786464 | tf_op jit(solution)/shard_map/ppermute | solution.py:71
  91.9 1.1 %add_convert_fusion.refs_4_ = bf16[512,384]{1,0:T(8,128)(2,1)S(1)} fusion(bf16[1024,384]{1,0:T(8,128)(2,1)} %collective-permute-done.15, bf16[1024,384]{1,0:T(8,128)(2,1)S(1)} %get-tuple-element.67), kind=kLoop, calls=%fused_computation.1 | loop fusion | flops 786432 | bytes 1179648 | tf_op jit(solution)/shard_map/convert_element_type | solution.py:86
  93.0 3.2 %collective-permute-start.16 = (bf16[512,384]{1,0:T(8,128)(2,1)S(1)}, bf16[512,384]{1,0:T(8,128)(2,1)S(1)}, u32[]{:S(2)}, u32[]{:S(2)}) collective-permute-start(bf16[512,384]{1,0:T(8,128)(2,1)S(1)} %add_convert_fusion.refs_4_), channel_id=1, source_target_pairs={{0,96},{1,97},{2,26},{3,27},{4,100},{5,101},{6,30},{7,31},{8,104},... | collective-permute-start | bytes 1179656 | tf_op jit(solution)/shard_map/ppermute | solution.py:71
  96.2 0.1 split.1
  96.3 3.3 %collective-permute-start.26 = (bf16[96,384]{1,0:T(8,128)(2,1)S(1)}, bf16[96,384]{1,0:T(8,128)(2,1)S(1)}, u32[]{:S(2)}, u32[]{:S(2)}) collective-permute-start(bf16[96,384]{1,0:T(8,128)(2,1)S(1)} %get-tuple-element.81), channel_id=1, source_target_pairs={{0,1},{1,0},{2,3},{3,2},{4,5},{5,4},{6,7},{7,6},{8,9},{9,8},{10,11... | collective-permute-start | bytes 221192 | tf_op jit(solution)/shard_map/ppermute | solution.py:679
  99.6 1.7 %fusion = bf16[1,256,384]{2,1,0:T(8,128)(2,1)} fusion(bf16[256,384]{1,0:T(8,128)(2,1)S(1)} %collective-permute-done.14, bf16[512,384]{1,0:T(8,128)(2,1)} %collective-permute-done.13, bf16[512,384]{1,0:T(8,128)(2,1)S(1)} %get-tuple-element.61), kind=kLoop, calls=%fused_computation.7 | loop fusion | flops 589824 | bytes 786432 | tf_op jit(solution)/shard_map/broadcast_in_dim | solution.py:680
  101.3 1.0 collective-permute-done.26
  102.3 0.7 convert_add_fusion
  102.9 1.9 %fusion.2 = (bf16[1,256,384]{2,1,0:T(8,128)(2,1)}, bf16[1,256,384]{2,1,0:T(8,128)(2,1)}) fusion(bf16[512,384]{1,0:T(8,128)(2,1)S(1)} %collective-permute-done.16, bf16[1024,384]{1,0:T(8,128)(2,1)} %collective-permute-done.15, bf16[1024,384]{1,0:T(8,128)(2,1)S(1)} %get-tuple-element.67), kind=kLoop, calls=%fused_computation.9 | loop fusion | flops 1179648 | bytes 1572864 | tf_op jit(solution)/shard_map/broadcast_in_dim | solution.py:682
  (43 shorter events, 0.1 us)
Async XLA Ops:
  0.6 1.7 %copy-start = (bf16[3072,384]{1,0:T(8,128)(2,1)S(1)}, bf16[3072,384]{1,0:T(8,128)(2,1)}, u32[]{:S(2)}) copy-start(bf16[3072,384]{1,0:T(8,128)(2,1)} %param.16) | copy-start | bytes 7077892
  0.6 3.1 %copy-start.13 = (s32[4,2]{0,1:T(2,128)S(1)}, s32[4,2]{0,1:T(2,128)}, u32[]{:S(2)}) copy-start(s32[4,2]{0,1:T(2,128)} %param.14) | copy-start | bytes 100
  0.7 3.1 %copy-start.12 = (s32[4,32]{1,0:T(4,128)S(1)}, s32[4,32]{1,0:T(4,128)}, u32[]{:S(2)}) copy-start(s32[4,32]{1,0:T(4,128)} %kv_list.1) | copy-start | bytes 1540
  0.7 3.1 %copy-start.9 = (bf16[1,256,384]{2,1,0:T(8,128)(2,1)S(1)}, bf16[1,256,384]{2,1,0:T(8,128)(2,1)}, u32[]{:S(2)}) copy-start(bf16[1,256,384]{2,1,0:T(8,128)(2,1)} %param.12) | copy-start | bytes 589828
  0.7 3.1 %copy-start.8 = (bf16[1,256,384]{2,1,0:T(8,128)(2,1)S(1)}, bf16[1,256,384]{2,1,0:T(8,128)(2,1)}, u32[]{:S(2)}) copy-start(bf16[1,256,384]{2,1,0:T(8,128)(2,1)} %param.9) | copy-start | bytes 589828
  3.8 3.3 %copy-start.10 = (bf16[1,256,384]{2,1,0:T(8,128)(2,1)S(1)}, bf16[1,256,384]{2,1,0:T(8,128)(2,1)}, u32[]{:S(2)}) copy-start(bf16[1,256,384]{2,1,0:T(8,128)(2,1)} %param.10) | copy-start | bytes 589828
  3.8 3.3 %copy-start.11 = (bf16[1,256,384]{2,1,0:T(8,128)(2,1)S(1)}, bf16[1,256,384]{2,1,0:T(8,128)(2,1)}, u32[]{:S(2)}) copy-start(bf16[1,256,384]{2,1,0:T(8,128)(2,1)} %param.11) | copy-start | bytes 589828
  3.9 15.2 %copy-start.4 = (bf16[592,384]{1,0:T(8,128)(2,1)}, bf16[592,384]{1,0:T(8,128)(2,1)S(1)}, u32[]{:S(2)}) copy-start(bf16[592,384]{1,0:T(8,128)(2,1)S(1)} %get-tuple-element.43.refs_0_) | copy-start | bytes 1363972
  3.9 15.2 %collective-permute-start.3 = (bf16[592,384]{1,0:T(8,128)(2,1)S(1)}, bf16[592,384]{1,0:T(8,128)(2,1)S(1)}, u32[]{:S(2)}, u32[]{:S(2)}) collective-permute-start(bf16[592,384]{1,0:T(8,128)(2,1)S(1)} %get-tuple-element.43.refs_0_), channel_id=1, source_target_pairs={{0,24},{1,25},{2,98},{3,99},{4,28},{5,29},{6,102},{7,103},{8,16},{... | collective-permute-start | bytes 1363976 | tf_op jit(solution)/shard_map/ppermute | solution.py:71
  6.8 12.6 %collective-permute-start = (bf16[592,384]{1,0:T(8,128)(2,1)S(1)}, bf16[592,384]{1,0:T(8,128)(2,1)S(1)}, u32[]{:S(2)}, u32[]{:S(2)}) collective-permute-start(bf16[592,384]{1,0:T(8,128)(2,1)S(1)} %get-tuple-element.43.refs_0_), channel_id=1, source_target_pairs={{0,8},{1,9},{2,34},{3,35},{4,12},{5,13},{6,38},{7,39},{8,0},{9,1},... | collective-permute-start | bytes 1363976 | tf_op jit(solution)/shard_map/ppermute | solution.py:71
  7.1 12.0 %collective-permute-start.4 = (bf16[512,384]{1,0:T(8,128)(2,1)S(1)}, bf16[512,384]{1,0:T(8,128)(2,1)S(1)}, u32[]{:S(2)}, u32[]{:S(2)}) collective-permute-start(bf16[512,384]{1,0:T(8,128)(2,1)S(1)} %stack.1.refs_4_.refs_0_), channel_id=1, source_target_pairs={{0,32},{1,33},{2,10},{3,11},{4,36},{5,37},{6,14},{7,15},{8,40},{9,... | collective-permute-start | bytes 1179656 | tf_op jit(solution)/shard_map/ppermute | solution.py:71
  9.1 10.0 %collective-permute-start.1 = (bf16[512,384]{1,0:T(8,128)(2,1)S(1)}, bf16[512,384]{1,0:T(8,128)(2,1)}, u32[]{:S(2)}, u32[]{:S(2)}) collective-permute-start(bf16[512,384]{1,0:T(8,128)(2,1)S(1)} %stack.1.refs_4_.refs_0_), channel_id=1, source_target_pairs={{0,96},{1,97},{2,26},{3,27},{4,100},{5,101},{6,30},{7,31},{8,104},... | collective-permute-start | bytes 1179656 | tf_op jit(solution)/shard_map/ppermute | solution.py:71
  11.6 0.7 copy-start.6
  12.3 6.5 %collective-permute-start.2 = (bf16[80,384]{1,0:T(8,128)(2,1)S(1)}, bf16[80,384]{1,0:T(8,128)(2,1)S(1)}, u32[]{:S(2)}, u32[]{:S(2)}) collective-permute-start(bf16[80,384]{1,0:T(8,128)(2,1)S(1)} %get-tuple-element.44), channel_id=1, source_target_pairs={{0,16},{1,17},{2,66},{3,67},{4,20},{5,21},{6,70},{7,71},{8,24},{9,... | collective-permute-start | bytes 184328 | tf_op jit(solution)/shard_map/ppermute | solution.py:71
  19.1 0.7 copy-start.1
  19.8 12.5 %collective-permute-start.5 = (bf16[592,384]{1,0:T(8,128)(2,1)S(1)}, bf16[592,384]{1,0:T(8,128)(2,1)}, u32[]{:S(2)}, u32[]{:S(2)}) collective-permute-start(bf16[592,384]{1,0:T(8,128)(2,1)S(1)} %get-tuple-element.45.refs_1_), channel_id=1, source_target_pairs={{0,24},{1,25},{2,98},{3,99},{4,28},{5,29},{6,102},{7,103},{8,16},{... | collective-permute-start | bytes 1363976 | tf_op jit(solution)/shard_map/ppermute | solution.py:71
  23.5 8.7 %collective-permute-start.6 = (bf16[512,384]{1,0:T(8,128)(2,1)}, bf16[512,384]{1,0:T(8,128)(2,1)}, u32[]{:S(2)}, u32[]{:S(2)}) collective-permute-start(bf16[512,384]{1,0:T(8,128)(2,1)} %get-tuple-element.51.refs_6_.refs_2_), channel_id=1, source_target_pairs={{0,32},{1,33},{2,10},{3,11},{4,36},{5,37},{6,14},{7,15},{8,40},{9,... | collective-permute-start | bytes 1179656 | tf_op jit(solution)/shard_map/ppermute | solution.py:71
  26.0 1.0 copy-start.3
  27.0 1.0 copy-start.5
  27.8 4.5 %copy-start.2 = (bf16[512,384]{1,0:T(8,128)(2,1)S(1)}, bf16[512,384]{1,0:T(8,128)(2,1)}, u32[]{:S(2)}) copy-start(bf16[512,384]{1,0:T(8,128)(2,1)} %copy-done.1) | copy-start | bytes 1179652
  27.8 4.5 %copy-start.7 = (bf16[512,384]{1,0:T(8,128)(2,1)S(1)}, bf16[512,384]{1,0:T(8,128)(2,1)}, u32[]{:S(2)}) copy-start(bf16[512,384]{1,0:T(8,128)(2,1)} %copy-done.6) | copy-start | bytes 1179652
  28.1 7.3 %collective-permute-start.7 = (bf16[384,384]{1,0:T(8,128)(2,1)S(1)}, bf16[384,384]{1,0:T(8,128)(2,1)S(1)}, u32[]{:S(2)}, u32[]{:S(2)}) collective-permute-start(bf16[384,384]{1,0:T(8,128)(2,1)S(1)} %get-tuple-element.53), channel_id=1, source_target_pairs={{0,32},{1,33},{2,10},{3,11},{4,36},{5,37},{6,14},{7,15},{8,40},{9,... | collective-permute-start | bytes 884744 | tf_op jit(solution)/shard_map/ppermute | solution.py:71
  28.5 11.1 %collective-permute-start.8 = (bf16[384,384]{1,0:T(8,128)(2,1)S(1)}, bf16[384,384]{1,0:T(8,128)(2,1)S(1)}, u32[]{:S(2)}, u32[]{:S(2)}) collective-permute-start(bf16[384,384]{1,0:T(8,128)(2,1)S(1)} %get-tuple-element.54), channel_id=1, source_target_pairs={{0,96},{1,97},{2,26},{3,27},{4,100},{5,101},{6,30},{7,31},{8,104},... | collective-permute-start | bytes 884744 | tf_op jit(solution)/shard_map/ppermute | solution.py:71
  30.4 9.2 %collective-permute-start.9 = (bf16[384,384]{1,0:T(8,128)(2,1)S(1)}, bf16[384,384]{1,0:T(8,128)(2,1)S(1)}, u32[]{:S(2)}, u32[]{:S(2)}) collective-permute-start(bf16[384,384]{1,0:T(8,128)(2,1)S(1)} %get-tuple-element.55), channel_id=1, source_target_pairs={{0,64},{1,65},{2,18},{3,19},{4,68},{5,69},{6,22},{7,23},{8,72},{9,... | collective-permute-start | bytes 884744 | tf_op jit(solution)/shard_map/ppermute | solution.py:71
  44.2 0.7 copy-start.14
  45.0 5.8 %collective-permute-start.12 = (f32[16,1024]{1,0:T(8,128)S(1)}, f32[16,1024]{1,0:T(8,128)S(1)}, u32[]{:S(2)}, u32[]{:S(2)}) collective-permute-start(f32[16,1024]{1,0:T(8,128)S(1)} %get-tuple-element.57.refs_4_.refs_0_), channel_id=1, source_target_pairs={{0,16},{1,17},{2,66},{3,67},{4,20},{5,21},{6,70},{7,71},{8,24},{9,... | collective-permute-start | bytes 196616 | tf_op jit(solution)/shard_map/ppermute | solution.py:71
  45.7 5.8 %collective-permute-start.11 = (f32[16,1024]{1,0:T(8,128)S(1)}, f32[16,1024]{1,0:T(8,128)S(1)}, u32[]{:S(2)}, u32[]{:S(2)}) collective-permute-start(f32[16,1024]{1,0:T(8,128)S(1)} %get-tuple-element.57.refs_4_.refs_0_), channel_id=1, source_target_pairs={{0,24},{1,25},{2,98},{3,99},{4,28},{5,29},{6,102},{7,103},{8,16},{... | collective-permute-start | bytes 196616 | tf_op jit(solution)/shard_map/ppermute | solution.py:71
  47.0 4.5 %collective-permute-start.10 = (f32[16,1024]{1,0:T(8,128)S(1)}, f32[16,1024]{1,0:T(8,128)S(1)}, u32[]{:S(2)}, u32[]{:S(2)}) collective-permute-start(f32[16,1024]{1,0:T(8,128)S(1)} %get-tuple-element.57.refs_4_.refs_0_), channel_id=1, source_target_pairs={{0,8},{1,9},{2,34},{3,35},{4,12},{5,13},{6,38},{7,39},{8,0},{9,1},... | collective-permute-start | bytes 196616 | tf_op jit(solution)/shard_map/ppermute | solution.py:71
  56.9 9.6 %collective-permute-start.17 = (bf16[256,384]{1,0:T(8,128)(2,1)S(1)}, bf16[256,384]{1,0:T(8,128)(2,1)S(1)}, u32[]{:S(2)}, u32[]{:S(2)}) collective-permute-start(bf16[256,384]{1,0:T(8,128)(2,1)S(1)} %get-tuple-element.70), channel_id=1, source_target_pairs={{0,8},{1,9},{2,34},{3,35},{4,12},{5,13},{6,38},{7,39},{8,0},{9,1},... | collective-permute-start | bytes 589832 | tf_op jit(solution)/shard_map/ppermute | solution.py:71
  58.2 9.0 %collective-permute-start.18 = (bf16[256,384]{1,0:T(8,128)(2,1)S(1)}, bf16[256,384]{1,0:T(8,128)(2,1)S(1)}, u32[]{:S(2)}, u32[]{:S(2)}) collective-permute-start(bf16[256,384]{1,0:T(8,128)(2,1)S(1)} %get-tuple-element.71), channel_id=1, source_target_pairs={{0,24},{1,25},{2,98},{3,99},{4,28},{5,29},{6,102},{7,103},{8,16},{... | collective-permute-start | bytes 589832 | tf_op jit(solution)/shard_map/ppermute | solution.py:71
  59.9 7.3 %collective-permute-start.19 = (bf16[256,384]{1,0:T(8,128)(2,1)S(1)}, bf16[256,384]{1,0:T(8,128)(2,1)S(1)}, u32[]{:S(2)}, u32[]{:S(2)}) collective-permute-start(bf16[256,384]{1,0:T(8,128)(2,1)S(1)} %get-tuple-element.72), channel_id=1, source_target_pairs={{0,16},{1,17},{2,66},{3,67},{4,20},{5,21},{6,70},{7,71},{8,24},{9,... | collective-permute-start | bytes 589832 | tf_op jit(solution)/shard_map/ppermute | solution.py:71
  67.9 8.2 %collective-permute-start.22 = (bf16[256,384]{1,0:T(8,128)(2,1)}, bf16[256,384]{1,0:T(8,128)(2,1)}, u32[]{:S(2)}, u32[]{:S(2)}) collective-permute-start(bf16[256,384]{1,0:T(8,128)(2,1)} %get-tuple-element.74), channel_id=1, source_target_pairs={{0,64},{1,65},{2,18},{3,19},{4,68},{5,69},{6,22},{7,23},{8,72},{9,... | collective-permute-start | bytes 589832 | tf_op jit(solution)/shard_map/ppermute | solution.py:71
  72.1 8.8 %collective-permute-start.21 = (bf16[256,384]{1,0:T(8,128)(2,1)}, bf16[256,384]{1,0:T(8,128)(2,1)}, u32[]{:S(2)}, u32[]{:S(2)}) collective-permute-start(bf16[256,384]{1,0:T(8,128)(2,1)} %get-tuple-element.74), channel_id=1, source_target_pairs={{0,96},{1,97},{2,26},{3,27},{4,100},{5,101},{6,30},{7,31},{8,104},... | collective-permute-start | bytes 589832 | tf_op jit(solution)/shard_map/ppermute | solution.py:71
  72.2 8.7 %collective-permute-start.20 = (bf16[256,384]{1,0:T(8,128)(2,1)}, bf16[256,384]{1,0:T(8,128)(2,1)}, u32[]{:S(2)}, u32[]{:S(2)}) collective-permute-start(bf16[256,384]{1,0:T(8,128)(2,1)} %get-tuple-element.74), channel_id=1, source_target_pairs={{0,32},{1,33},{2,10},{3,11},{4,36},{5,37},{6,14},{7,15},{8,40},{9,... | collective-permute-start | bytes 589832 | tf_op jit(solution)/shard_map/ppermute | solution.py:71
  72.2 19.7 %collective-permute-start.15 = (bf16[1024,384]{1,0:T(8,128)(2,1)}, bf16[1024,384]{1,0:T(8,128)(2,1)}, u32[]{:S(2)}, u32[]{:S(2)}) collective-permute-start(bf16[1024,384]{1,0:T(8,128)(2,1)} %get-tuple-element.68), channel_id=1, source_target_pairs={{0,32},{1,33},{2,10},{3,11},{4,36},{5,37},{6,14},{7,15},{8,40},{9,... | collective-permute-start | bytes 2359304 | tf_op jit(solution)/shard_map/ppermute | solution.py:71
  74.2 14.1 %collective-permute-start.13 = (bf16[512,384]{1,0:T(8,128)(2,1)}, bf16[512,384]{1,0:T(8,128)(2,1)}, u32[]{:S(2)}, u32[]{:S(2)}) collective-permute-start(bf16[512,384]{1,0:T(8,128)(2,1)} %get-tuple-element.62), channel_id=1, source_target_pairs={{0,24},{1,25},{2,98},{3,99},{4,28},{5,29},{6,102},{7,103},{8,16},{... | collective-permute-start | bytes 1179656 | tf_op jit(solution)/shard_map/ppermute | solution.py:71
  82.2 1.0 copy-start.15
  84.1 12.1 %collective-permute-start.23 = (bf16[192,384]{1,0:T(8,128)(2,1)S(1)}, bf16[192,384]{1,0:T(8,128)(2,1)S(1)}, u32[]{:S(2)}, u32[]{:S(2)}) collective-permute-start(bf16[192,384]{1,0:T(8,128)(2,1)S(1)} %get-tuple-element.77), channel_id=1, source_target_pairs={{0,8},{1,9},{2,34},{3,35},{4,12},{5,13},{6,38},{7,39},{8,0},{9,1},... | collective-permute-start | bytes 442376 | tf_op jit(solution)/shard_map/ppermute | solution.py:71
  85.4 10.8 %collective-permute-start.24 = (bf16[192,384]{1,0:T(8,128)(2,1)S(1)}, bf16[192,384]{1,0:T(8,128)(2,1)S(1)}, u32[]{:S(2)}, u32[]{:S(2)}) collective-permute-start(bf16[192,384]{1,0:T(8,128)(2,1)S(1)} %get-tuple-element.78), channel_id=1, source_target_pairs={{0,24},{1,25},{2,98},{3,99},{4,28},{5,29},{6,102},{7,103},{8,16},{... | collective-permute-start | bytes 442376 | tf_op jit(solution)/shard_map/ppermute | solution.py:71
  86.2 10.0 %collective-permute-start.25 = (bf16[192,384]{1,0:T(8,128)(2,1)S(1)}, bf16[192,384]{1,0:T(8,128)(2,1)S(1)}, u32[]{:S(2)}, u32[]{:S(2)}) collective-permute-start(bf16[192,384]{1,0:T(8,128)(2,1)S(1)} %get-tuple-element.79), channel_id=1, source_target_pairs={{0,16},{1,17},{2,66},{3,67},{4,20},{5,21},{6,70},{7,71},{8,24},{9,... | collective-permute-start | bytes 442376 | tf_op jit(solution)/shard_map/ppermute | solution.py:71
  89.3 10.3 %collective-permute-start.14 = (bf16[256,384]{1,0:T(8,128)(2,1)S(1)}, bf16[256,384]{1,0:T(8,128)(2,1)S(1)}, u32[]{:S(2)}, u32[]{:S(2)}) collective-permute-start(bf16[256,384]{1,0:T(8,128)(2,1)S(1)} %add_convert_fusion.5), channel_id=1, source_target_pairs={{0,8},{1,9},{2,34},{3,35},{4,12},{5,13},{6,38},{7,39},{8,0},{9,1},... | collective-permute-start | bytes 589832 | tf_op jit(solution)/shard_map/ppermute | solution.py:71
  93.0 10.0 %collective-permute-start.16 = (bf16[512,384]{1,0:T(8,128)(2,1)S(1)}, bf16[512,384]{1,0:T(8,128)(2,1)S(1)}, u32[]{:S(2)}, u32[]{:S(2)}) collective-permute-start(bf16[512,384]{1,0:T(8,128)(2,1)S(1)} %add_convert_fusion.refs_4_), channel_id=1, source_target_pairs={{0,96},{1,97},{2,26},{3,27},{4,100},{5,101},{6,30},{7,31},{8,104},... | collective-permute-start | bytes 1179656 | tf_op jit(solution)/shard_map/ppermute | solution.py:71
  96.3 5.9 %collective-permute-start.26 = (bf16[96,384]{1,0:T(8,128)(2,1)S(1)}, bf16[96,384]{1,0:T(8,128)(2,1)S(1)}, u32[]{:S(2)}, u32[]{:S(2)}) collective-permute-start(bf16[96,384]{1,0:T(8,128)(2,1)S(1)} %get-tuple-element.81), channel_id=1, source_target_pairs={{0,1},{1,0},{2,3},{3,2},{4,5},{5,4},{6,7},{7,6},{8,9},{9,8},{10,11... | collective-permute-start | bytes 221192 | tf_op jit(solution)/shard_map/ppermute | solution.py:679
